TPU v7x, 32 devices: a whole 2x2x4 slice. The times are simulated.
32 devices in a mesh: dp: 4 (over x, core), expert: 8 (over z, y).
Axes of the slice: x: 2, y: 2, z: 4, core: 2. Of those that a mesh axis runs over, the one named last changes fastest.
Arguments:
- hidden_states: bfloat16 [4096, 2048], P(('dp', 'expert')), may hold values from -18 to 18
- out_grad: bfloat16 [4096, 2048], P(('dp', 'expert')), may hold values from -6 to 6
- seq_lengths: int32 [4, 3], P('dp'), may hold values from 1 to 512, 1024 in all within a row
- seq_order: int32 [4, 3], P('dp'), may hold values from 0 to 2, each once within a row
- expert_routes: int32 [4096, 8], P(('dp', 'expert')), may hold values from 0 to 15, all different within a row; in each aligned block of 128 rows (0 to 127, 128 to 255, ...) at most 96 rows name the same one
- attn_gain: float32 [2048], replicated, may hold values from 0.5 to 1.5
- qkv_weight: bfloat16 [2048, 3, 2048], P('dp', None, 'expert'), may hold values from -0.125 to 0.125
- out_weight: bfloat16 [2048, 2048], P('dp', 'expert'), may hold values from -2.5 to 2.5
- query_gain: float32 [128], replicated, may hold values from 0.5 to 1.5
- key_gain: float32 [128], replicated, may hold values from 0.5 to 1.5
- ffn_gain: float32 [2048], replicated, may hold values from 0.5 to 1.5
- router_weight: bfloat16 [2048, 16], replicated, may hold values from -0.0625 to 0.0625
- expert_gate_up: bfloat16 [1024, 16, 2, 2048], P('dp', 'expert'), may hold values from -0.125 to 0.125
- expert_down: bfloat16 [1024, 16, 2048], P('dp', 'expert'), may hold values from -4 to 4
Outputs:
- output_states: bfloat16 [4096, 2048], P(('dp', 'expert'))
- input_grad: bfloat16 [4096, 2048], P(('dp', 'expert'))
- attn_gain_grad: float32 [2048], replicated
- qkv_weight_grad: float32 [2048, 3, 2048], P('dp', None, 'expert')
- out_weight_grad: float32 [2048, 2048], P('dp', 'expert')
- query_gain_grad: float32 [128], replicated
- key_gain_grad: float32 [128], replicated
- ffn_gain_grad: float32 [2048], replicated
- router_grad: float32 [2048, 16], replicated
- gate_up_grad: float32 [1024, 16, 2, 2048], P('dp', 'expert')
- down_grad: float32 [1024, 16, 2048], P('dp', 'expert')
- stream_rms: float32 [3], replicated
Inputs may be any that keep to these rules, and one draw needn't show every extreme that they name: `seq_lengths`: each row holds the lengths of the 3 sequences of one data group; they sum to 1024, and the longest of each row is exactly 512. `seq_order`: each row is a permutation of 0 to 2. `expert_routes`: each row names 8 different experts; within the rows of one device no expert is named more than 96 times, and this bound is reached.
All inputs are finite; a program needn't handle non-finite values.
Results may differ from a plain program's by a relative error of at most 0.022.
Values may be sent and summed in bfloat16 or wider, within the bound.
No kernel may reach another device: no remote copies, remote signals or barrier semaphores. Data moves between devices by JAX's collectives and lax.ppermute only.
A program may use at most 320 MiB of HBM per device.

v0:
```python
import jax
import jax.numpy as jnp
from jax import lax
from jax.sharding import PartitionSpec as P

eps_norm = 1e-06
rope_base = 10000.0
big_negative = -1e30


def norm_rows(values, norm_gain):
    row_scale = lax.rsqrt(jnp.mean(values * values, axis=-1, keepdims=True) + eps_norm)
    normed = values * row_scale
    return (normed * norm_gain, normed, row_scale)


def norm_back(grad_out, norm_gain, normed, row_scale):
    scaled = grad_out * norm_gain
    inner_mean = jnp.mean(normed * scaled, axis=-1, keepdims=True)
    return row_scale * (scaled - normed * inner_mean)


def seq_layout(lengths, seq_order, row_count):
    seq_count = lengths.shape[0]
    picked_seq = seq_order[:, None] == jnp.arange(seq_count, dtype=jnp.int32)[None, :]
    ordered = jnp.sum(jnp.where(picked_seq, lengths[None, :], 0), axis=1)
    seq_ends = jnp.cumsum(ordered)
    starts = seq_ends - ordered
    places = jnp.arange(row_count, dtype=jnp.int32)
    segment = jnp.sum((places[:, None] >= seq_ends[None, :]).astype(jnp.int32), axis=1)
    member = segment[:, None] == jnp.arange(seq_count, dtype=jnp.int32)[None, :]
    position = places - jnp.sum(jnp.where(member, starts[None, :], 0), axis=1)
    return (segment, position)


def rope_tables(position, head_dim):
    half_dim = head_dim // 2
    inv_freq = rope_base ** (-(jnp.arange(half_dim, dtype=jnp.float32) * 2.0 / head_dim))
    angles = position.astype(jnp.float32)[:, None] * inv_freq[None, :]
    return (jnp.cos(angles), jnp.sin(angles))


def rotate(values, cos_rows, sin_rows):
    half_dim = values.shape[-1] // 2
    lead_half = values[..., :half_dim]
    tail_half = values[..., half_dim:]
    cos_part = cos_rows[:, None, :]
    sin_part = sin_rows[:, None, :]
    return jnp.concatenate(
        [lead_half * cos_part - tail_half * sin_part, tail_half * cos_part + lead_half * sin_part],
        axis=-1,
    )


def rotate_back(grad_out, cos_rows, sin_rows):
    half_dim = grad_out.shape[-1] // 2
    lead_half = grad_out[..., :half_dim]
    tail_half = grad_out[..., half_dim:]
    cos_part = cos_rows[:, None, :]
    sin_part = sin_rows[:, None, :]
    return jnp.concatenate(
        [lead_half * cos_part + tail_half * sin_part, tail_half * cos_part - lead_half * sin_part],
        axis=-1,
    )


def masked_scores(query_blk, key_low, seg_blk, segment, scaling):
    scores = (
        jnp.einsum("qhd,khd->hqk", query_blk, key_low, preferred_element_type=jnp.float32) * scaling
    )
    allowed = seg_blk[:, None] == segment[None, :]
    return jnp.where(allowed[None, :, :], scores, big_negative)


def attention_forward(query_low, key_low, value_low, segment, block_rows, scaling):
    row_count = query_low.shape[0]

    def one_block(block_id):
        row_start = block_id * block_rows
        query_blk = lax.dynamic_slice_in_dim(query_low, row_start, block_rows, 0)
        seg_blk = lax.dynamic_slice_in_dim(segment, row_start, block_rows, 0)
        scores = masked_scores(query_blk, key_low, seg_blk, segment, scaling)
        row_max = jnp.max(scores, axis=-1, keepdims=True)
        exp_scores = jnp.exp(scores - row_max)
        row_sum = jnp.sum(exp_scores, axis=-1, keepdims=True)
        weights = (exp_scores / row_sum).astype(jnp.bfloat16)
        attended = jnp.einsum(
            "hqk,khd->qhd", weights, value_low, preferred_element_type=jnp.float32
        )
        return (attended, (row_max + jnp.log(row_sum))[..., 0])

    attended, log_sums = lax.map(one_block, jnp.arange(row_count // block_rows, dtype=jnp.int32))
    return (attended.reshape(query_low.shape), log_sums)


def attention_backward(
    query_low, key_low, value_low, grad_low, segment, log_sums, block_rows, scaling
):
    row_count = query_low.shape[0]
    zero_grad = jnp.zeros(key_low.shape, jnp.float32)

    def one_block(carry_grads, inputs):
        grad_key, grad_value = carry_grads
        block_id, lse_blk = inputs
        row_start = block_id * block_rows
        query_blk = lax.dynamic_slice_in_dim(query_low, row_start, block_rows, 0)
        seg_blk = lax.dynamic_slice_in_dim(segment, row_start, block_rows, 0)
        grad_blk = lax.dynamic_slice_in_dim(grad_low, row_start, block_rows, 0)
        scores = masked_scores(query_blk, key_low, seg_blk, segment, scaling)
        soft_probs = jnp.exp(scores - lse_blk[..., None])
        grad_probs = jnp.einsum(
            "qhd,khd->hqk", grad_blk, value_low, preferred_element_type=jnp.float32
        )
        inner_sum = jnp.sum(soft_probs * grad_probs, axis=-1, keepdims=True)
        grad_scores = (soft_probs * (grad_probs - inner_sum)).astype(jnp.bfloat16)
        grad_query = (
            jnp.einsum("hqk,khd->qhd", grad_scores, key_low, preferred_element_type=jnp.float32)
            * scaling
        )
        grad_key = (
            grad_key
            + jnp.einsum("hqk,qhd->khd", grad_scores, query_blk, preferred_element_type=jnp.float32)
            * scaling
        )
        grad_value = grad_value + jnp.einsum(
            "hqk,qhd->khd",
            soft_probs.astype(jnp.bfloat16),
            grad_blk,
            preferred_element_type=jnp.float32,
        )
        return ((grad_key, grad_value), grad_query)

    block_ids = jnp.arange(row_count // block_rows, dtype=jnp.int32)
    (grad_key, grad_value), grad_query = lax.scan(
        one_block, (zero_grad, zero_grad), (block_ids, log_sums)
    )
    return (grad_query.reshape(query_low.shape), grad_key, grad_value)


def on_device(
    hidden_states,
    out_grad,
    seq_lengths,
    seq_order,
    expert_routes,
    attn_gain,
    qkv_weight,
    out_weight,
    query_gain,
    key_gain,
    ffn_gain,
    router_weight,
    expert_gate_up,
    expert_down,
):
    tok_rows, width = hidden_states.shape
    head_dim = query_gain.shape[0]
    top_count = expert_routes.shape[1]
    experts_dev = expert_gate_up.shape[1]
    expert_devs = lax.axis_size("expert")
    all_devices = lax.axis_size("dp") * expert_devs
    num_experts = experts_dev * expert_devs
    capacity = tok_rows * top_count * 3 // (2 * num_experts)
    scaling = head_dim ** (-0.5)
    states = hidden_states.astype(jnp.float32)
    attn_in, attn_normed, attn_scale = norm_rows(states, attn_gain)
    attn_low = attn_in.astype(jnp.bfloat16)
    features = lax.all_gather(attn_low, "expert", axis=0, tiled=True)
    qkv_local, out_local, gate_up_full, down_full = (
        lax.all_gather(qkv_weight, "dp", axis=0, tiled=True),
        lax.all_gather(out_weight, "dp", axis=0, tiled=True),
        lax.all_gather(expert_gate_up, "dp", axis=0, tiled=True),
        lax.all_gather(expert_down, "dp", axis=0, tiled=True),
    )
    group_rows = features.shape[0]
    local_width = qkv_local.shape[2]
    local_heads = local_width // head_dim
    projected = jnp.einsum("gd,dcf->gcf", features, qkv_local, preferred_element_type=jnp.float32)
    head_proj = projected.reshape(group_rows, 3, local_heads, head_dim)
    segment, position = seq_layout(seq_lengths[0], seq_order[0], group_rows)
    cos_rows, sin_rows = rope_tables(position, head_dim)
    query_in, query_normed, query_scale = norm_rows(head_proj[:, 0], query_gain)
    key_in, key_normed, key_scale = norm_rows(head_proj[:, 1], key_gain)
    query_low = rotate(query_in, cos_rows, sin_rows).astype(jnp.bfloat16)
    key_low = rotate(key_in, cos_rows, sin_rows).astype(jnp.bfloat16)
    value_low = head_proj[:, 2].astype(jnp.bfloat16)
    block_rows = min(512, group_rows)
    attended, log_sums = attention_forward(
        query_low, key_low, value_low, segment, block_rows, scaling
    )
    attended_low = attended.reshape(group_rows, local_width).astype(jnp.bfloat16)
    branch = lax.psum_scatter(
        jnp.einsum("gf,df->gd", attended_low, out_local, preferred_element_type=jnp.float32),
        "expert",
        scatter_dimension=0,
        tiled=True,
    )
    mixed_rows = states + branch
    ffn_in, ffn_normed, ffn_scale = norm_rows(mixed_rows, ffn_gain)
    ffn_low = ffn_in.astype(jnp.bfloat16)
    logits = jnp.dot(ffn_low, router_weight, preferred_element_type=jnp.float32)
    router = jax.nn.softmax(logits, axis=-1)
    chosen = expert_routes[:, :, None] == jnp.arange(num_experts, dtype=jnp.int32)[None, None, :]
    chosen_mask = chosen.astype(jnp.float32)
    gate_vals = jnp.sum(router[:, None, :] * chosen_mask, axis=-1)
    route_hits = chosen.reshape(tok_rows * top_count, num_experts).astype(jnp.int32)
    route_rank = jnp.cumsum(route_hits, axis=0) - 1
    slot_of = jnp.sum(route_rank * route_hits, axis=1)
    targets = expert_routes.reshape(-1) * capacity + slot_of
    copies = jnp.repeat(ffn_low, top_count, axis=0)
    send_rows = jnp.zeros((num_experts * capacity, width), jnp.bfloat16).at[targets].set(copies)
    send_rows = send_rows.reshape(expert_devs, experts_dev, capacity, width)
    expert_received = lax.all_to_all(send_rows, "expert", split_axis=0, concat_axis=0, tiled=True)
    pre_act = jnp.einsum(
        "secd,fekd->seckf", expert_received, gate_up_full, preferred_element_type=jnp.float32
    )
    gate_pre = pre_act[:, :, :, 0]
    up_pre = pre_act[:, :, :, 1]
    expert_activated = (jax.nn.silu(gate_pre) * up_pre).astype(jnp.bfloat16)
    expert_out = jnp.einsum(
        "secf,fed->secd", expert_activated, down_full, preferred_element_type=jnp.float32
    ).astype(jnp.bfloat16)
    returned = lax.all_to_all(expert_out, "expert", split_axis=0, concat_axis=0, tiled=True)
    returned, received, gate_pre, up_pre, activated = (
        returned,
        expert_received,
        gate_pre,
        up_pre,
        expert_activated,
    )
    picked = returned.reshape(num_experts * capacity, width)[targets].reshape(
        tok_rows, top_count, width
    )
    moe_out = jnp.sum(gate_vals[:, :, None] * picked.astype(jnp.float32), axis=1)
    output = mixed_rows + moe_out
    grad_top = out_grad.astype(jnp.float32)
    grad_gates = jnp.sum(picked.astype(jnp.float32) * grad_top[:, None, :], axis=-1)
    grad_picked = (gate_vals[:, :, None] * grad_top[:, None, :]).astype(jnp.bfloat16)
    grad_send = (
        jnp.zeros((num_experts * capacity, width), jnp.bfloat16)
        .at[targets]
        .set(grad_picked.reshape(-1, width))
    )
    grad_send = grad_send.reshape(expert_devs, experts_dev, capacity, width)
    grad_recv = lax.all_to_all(grad_send, "expert", split_axis=0, concat_axis=0, tiled=True)
    grad_act = jnp.einsum(
        "secd,fed->secf", grad_recv, down_full, preferred_element_type=jnp.float32
    )
    sigmoid_gate = jax.nn.sigmoid(gate_pre)
    silu_gate = gate_pre * sigmoid_gate
    grad_gate = grad_act * up_pre * sigmoid_gate * (1.0 + gate_pre * (1.0 - sigmoid_gate))
    grad_up = grad_act * silu_gate
    grad_pair = jnp.stack([grad_gate, grad_up], axis=3).astype(jnp.bfloat16)
    grad_in = jnp.einsum(
        "seckf,fekd->secd", grad_pair, gate_up_full, preferred_element_type=jnp.float32
    ).astype(jnp.bfloat16)
    grad_back = lax.all_to_all(grad_in, "expert", split_axis=0, concat_axis=0, tiled=True)
    grad_copies = grad_back.reshape(num_experts * capacity, width)[targets].reshape(
        tok_rows, top_count, width
    )
    grad_ffn = jnp.sum(grad_copies.astype(jnp.float32), axis=1)
    gate_up_term = jnp.einsum(
        "secd,seckf->fekd", received, grad_pair, preferred_element_type=jnp.float32
    )
    down_term = jnp.einsum(
        "secf,secd->fed", activated, grad_recv, preferred_element_type=jnp.float32
    )
    expert_sums = lax.psum_scatter(
        jnp.concatenate([gate_up_term, down_term[:, :, None, :]], axis=2).astype(jnp.bfloat16),
        "dp",
        scatter_dimension=0,
        tiled=True,
    ).astype(jnp.float32)
    grad_router_probs = jnp.sum(grad_gates[:, :, None] * chosen_mask, axis=1)
    grad_logits = router * (
        grad_router_probs - jnp.sum(router * grad_router_probs, axis=-1, keepdims=True)
    )
    logit_low = grad_logits.astype(jnp.bfloat16)
    grad_ffn = grad_ffn + jnp.dot(logit_low, router_weight.T, preferred_element_type=jnp.float32)
    grad_router = jnp.dot(ffn_low.T, logit_low, preferred_element_type=jnp.float32)
    grad_ffn_gain = jnp.sum(ffn_normed * grad_ffn, axis=0)
    grad_mixed = grad_top + norm_back(grad_ffn, ffn_gain, ffn_normed, ffn_scale)
    mixed_low = grad_mixed.astype(jnp.bfloat16)
    grad_rows_all = lax.all_gather(mixed_low, "expert", axis=0, tiled=True)
    grad_attended = jnp.dot(grad_rows_all, out_local, preferred_element_type=jnp.float32)
    grad_attended = grad_attended.reshape(group_rows, local_heads, head_dim).astype(jnp.bfloat16)
    grad_query, grad_key, grad_value = attention_backward(
        query_low, key_low, value_low, grad_attended, segment, log_sums, block_rows, scaling
    )
    grad_query = rotate_back(grad_query, cos_rows, sin_rows)
    grad_key = rotate_back(grad_key, cos_rows, sin_rows)
    grad_query_gain = jnp.sum(query_normed * grad_query, axis=(0, 1))
    grad_key_gain = jnp.sum(key_normed * grad_key, axis=(0, 1))
    grad_query = norm_back(grad_query, query_gain, query_normed, query_scale)
    grad_key = norm_back(grad_key, key_gain, key_normed, key_scale)
    grad_proj = (
        jnp.stack([grad_query, grad_key, grad_value], axis=1)
        .reshape(group_rows, 3, local_width)
        .astype(jnp.bfloat16)
    )
    qkv_term = jnp.einsum("gd,gcf->dcf", features, grad_proj, preferred_element_type=jnp.float32)
    out_term = jnp.einsum(
        "gd,gf->df", grad_rows_all, attended_low, preferred_element_type=jnp.float32
    )
    attn_sums = lax.psum_scatter(
        jnp.concatenate([qkv_term, out_term[:, None, :]], axis=1).astype(jnp.bfloat16),
        "dp",
        scatter_dimension=0,
        tiled=True,
    ).astype(jnp.float32)
    grad_features = lax.psum_scatter(
        jnp.einsum("gcf,dcf->gd", grad_proj, qkv_local, preferred_element_type=jnp.float32).astype(
            jnp.bfloat16
        ),
        "expert",
        scatter_dimension=0,
        tiled=True,
    ).astype(jnp.float32)
    grad_attn_gain = jnp.sum(attn_normed * grad_features, axis=0)
    input_grad = (grad_mixed + norm_back(grad_features, attn_gain, attn_normed, attn_scale)).astype(
        jnp.bfloat16
    )
    squares = jnp.stack(
        [jnp.sum(output * output), jnp.sum(branch * branch), jnp.sum(moe_out * moe_out)]
    )
    totals = lax.psum(
        (grad_attn_gain, grad_query_gain, grad_key_gain, grad_ffn_gain, grad_router, squares),
        ("dp", "expert"),
    )
    stream_rms = jnp.sqrt(totals[5] / (tok_rows * width * all_devices))
    return (
        output.astype(jnp.bfloat16),
        input_grad,
        totals[0],
        attn_sums[:, :3],
        attn_sums[:, 3],
        totals[1],
        totals[2],
        totals[3],
        totals[4],
        expert_sums[:, :, :2],
        expert_sums[:, :, 2],
        stream_rms,
    )


def solution(mesh):
    in_specs = (
        P(("dp", "expert"), None),
        P(("dp", "expert"), None),
        P("dp", None),
        P("dp", None),
        P(("dp", "expert"), None),
        P(),
        P("dp", None, "expert"),
        P("dp", "expert"),
        P(),
        P(),
        P(),
        P(),
        P("dp", "expert", None, None),
        P("dp", "expert", None),
    )
    out_specs = (
        P(("dp", "expert"), None),
        P(("dp", "expert"), None),
        P(),
        P("dp", None, "expert"),
        P("dp", "expert"),
        P(),
        P(),
        P(),
        P(),
        P("dp", "expert", None, None),
        P("dp", "expert", None),
        P(),
    )
    return jax.shard_map(
        on_device, mesh=mesh, in_specs=in_specs, out_specs=out_specs, check_vma=False
    )
```

profile of v0, /device:TPU:0, one launch (start us, length us, event | category | flops | bytes accessed | tf_op | source)
XLA Modules:
  0.0 1522.8 jit_solution(4851156312184918491)
XLA Ops:
  16.8 24.6 %all-gather.9.cloned.1.call-done = bf16[2048,3,256]{0,2,1:T(8,128)(2,1)} async-done(((bf16[512,3,256]{0,2,1:T(8,128)(2,1)}), bf16[2048,3,256]{0,2,1:T(8,128)(2,1)}) %all-gather.9.cloned.1.call-update) | async-done | bytes 3145744 | tf_op jit(solution)/shard_map/all_gather | solution.py:170
  41.4 76.1 %all-gather.7.cloned.1.call-done = bf16[1024,2048]{1,0:T(8,128)(2,1)} async-done(((bf16[128,2048]{1,0:T(8,128)(2,1)}), bf16[1024,2048]{1,0:T(8,128)(2,1)}) %all-gather.7.cloned.1.call-update) | async-done | bytes 4194320 | tf_op jit(solution)/shard_map/all_gather | solution.py:168
  133.6 17.2 %while.27 = (s32[]{:T(128)}, bf16[2,512,2,128]{3,1,2,0:T(8,128)(2,1)}, f32[2,2,512]{2,1,0:T(2,128)S(1)}, s32[2]{0:T(128)S(1)}, s32[1024]{0:T(1024)S(1)}, /*index...) while((s32[]{:T(128)}, ...), condition=%wide.region_10.11_spmd, body=%wide.region_7.10_spmd.sunk | while | flops 549977088 | bytes 20752640 | solution.py:92
  171.8 134.5 %reduce-scatter.5.cloned.1.call-done = f32[128,2048]{1,0:T(8,128)} async-done(((f32[1024,2048]{1,0:T(8,128)}), f32[128,2048]{1,0:T(8,128)}) %reduce-scatter.5.cloned.1.call-update) | async-done | bytes 1048592 | tf_op jit(solution)/shard_map/reduce_scatter | solution.py:192
  308.6 11.0 scatter_custom_fusion
  340.4 122.6 %all-to-all-done = bf16[8,2,96,2048]{3,2,1,0:T(8,128)(2,1)} async-done(((bf16[8,2,96,2048]{3,2,1,0:T(8,128)(2,1)}), bf16[8,2,96,2048]{3,2,1,0:T(8,128)(2,1)}, u32[]{:S(2)}, u32[]{:S(2)}) %all-to-all-start) | async-done | bytes 6291488 | tf_op jit(solution)/shard_map/all_to_all | solution.py:213
  468.0 20.3 %fusion.64 = f32[8,2,96,2,1024]{4,2,3,0,1:T(8,128)} fusion(bf16[1024,2,2,2048]{3,0,2,1:T(8,128)(2,1)} %all-gather.13.cloned.1.call-done, bf16[8,2,96,2048]{3,2,1,0:T(8,128)(2,1)} %all-to-all-done), kind=kOutput, calls=%fused_computation.90 | convolution fusion | flops 12884901888 | bytes 35651584 | tf_op jit(solution)/shard_map/secd,fekd->seckf/dot_general | solution.py:214
  488.3 117.2 %all-to-all-done.2 = bf16[8,2,96,2048]{3,2,1,0:T(8,128)(2,1)} async-done(((bf16[8,2,96,2048]{3,2,1,0:T(8,128)(2,1)}), bf16[8,2,96,2048]{3,2,1,0:T(8,128)(2,1)}, u32[]{:S(2)}, u32[]{:S(2)}) %all-to-all-start.2) | async-done | bytes 6291488 | tf_op jit(solution)/shard_map/all_to_all | solution.py:245
  605.5 17.3 %fusion.86 = (bf16[8,2,96,1,1024]{4,2,0,1,3:T(8,128)(2,1)}, bf16[8,2,96,1,1024]{4,2,0,1,3:T(8,128)(2,1)}, bf16[8,2,96,1024]{3,2,0,1:T(8,128)(2,1)}) fusion(f32[8,2,96,2,1024]{4,2,3,0,1:T(8,128)} %fusion.64, bf16[1024,2,2048]{2,0,1:T(8,128)(2,1)} %all-gather.15.cloned.1.call-done, bf16[8,2,96,2048]{3,2,1,0:T(8,128)(2,1)} %all-to-all-done.2), kind=kOutput, calls=%fused_computation.107 | convolution fusion | flops 6466043904 | bytes 36700160 | tf_op jit(solution)/shard_map/secd,fed->secf/dot_general | solution.py:246
  641.8 20.3 %fusion.42 = bf16[2,8,96,2048,1]{3,2,1,0,4:T(8,128)(2,1)} fusion(bf16[8,2,96,1,1024]{4,2,0,1,3:T(8,128)(2,1)} %get-tuple-element.342, bf16[8,2,96,1,1024]{4,2,0,1,3:T(8,128)(2,1)} %get-tuple-element.341, bf16[1024,2,2,2048]{3,0,2,1:T(8,128)(2,1)} %all-gather.13.cloned.1.call-done), kind=kOutput, calls=%fused_computation.56 | convolution fusion | flops 12888047616 | bytes 29360128 | tf_op jit(solution)/shard_map/seckf,fekd->secd/dot_general | solution.py:254
  668.7 110.4 %all-to-all-done.1 = bf16[8,2,96,2048]{3,2,1,0:T(8,128)(2,1)} async-done(((bf16[8,2,96,2048]{3,2,1,0:T(8,128)(2,1)}), bf16[8,2,96,2048]{3,2,1,0:T(8,128)(2,1)}, u32[]{:S(2)}, u32[]{:S(2)}) %all-to-all-start.1) | async-done | bytes 6291488 | tf_op jit(solution)/shard_map/all_to_all | solution.py:223
  783.9 12.8 gather_fusion
  802.5 118.5 %all-to-all-done.3 = bf16[8,2,96,2048]{3,2,1,0:T(8,128)(2,1)} async-done(((bf16[8,2,96,2048]{3,2,1,0:T(8,128)(2,1)}), bf16[8,2,96,2048]{3,2,1,0:T(8,128)(2,1)}, u32[]{:S(2)}, u32[]{:S(2)}) %all-to-all-start.3) | async-done | bytes 6291488 | tf_op jit(solution)/shard_map/all_to_all | solution.py:257
  921.1 12.4 gather_fusion.1
  945.3 72.1 %all-gather.17.cloned.1.call-done = bf16[1024,2048]{1,0:T(8,128)(2,1)} async-done(((bf16[128,2048]{1,0:T(8,128)(2,1)}), bf16[1024,2048]{1,0:T(8,128)(2,1)}) %all-gather.17.cloned.1.call-update) | async-done | bytes 4194320 | tf_op jit(solution)/shard_map/all_gather | solution.py:284
  1022.0 33.2 %while.28 = (s32[]{:T(128)}, f32[1024,2,128]{0,2,1:T(8,128)}, f32[1024,2,128]{0,2,1:T(8,128)}, f32[2,512,2,128]{3,1,0,2:T(8,128)}, s32[2]{0:T(128)S(1)}, /*index...) while((s32[]{:T(128)}, f32[1024,2,128]{0,2,1:T(8,128)}, ...), condition=%wide.region_29.30_spmd.clone, body=%wide.region_27.29_spmd.clone.sunk | while | flops 1359870976 | bytes 82876776 | solution.py:134
  1082.2 11.9 fusion.46
  1094.0 20.7 %fusion.39 = bf16[1024,2,2,2048]{3,0,2,1:T(8,128)(2,1)} fusion(bf16[8,2,96,1,1024]{4,2,0,1,3:T(8,128)(2,1)} %get-tuple-element.342, bf16[8,2,96,1,1024]{4,2,0,1,3:T(8,128)(2,1)} %get-tuple-element.341, bf16[8,2,96,2048]{3,2,1,0:T(8,128)(2,1)} %all-to-all-done), kind=kOutput, calls=%fused_computation.52 | convolution fusion | flops 12896436224 | bytes 29360128 | tf_op jit(solution)/shard_map/secd,seckf->fekd/dot_general | solution.py:262
  1114.8 20.8 %pad_maximum_fusion = bf16[1024,2,3,2048]{3,0,2,1:T(8,128)(2,1)} fusion(bf16[1024,2,1,2048]{3,0,2,1:T(8,128)(2,1)} %fusion.46, bf16[1024,2,2,2048]{3,0,2,1:T(8,128)(2,1)} %fusion.39), kind=kLoop, calls=%fused_computation.51 | loop fusion | flops 12582912 | bytes 50331648 | tf_op jit(solution)/shard_map/concatenate | solution.py:269
  1139.5 16.3 %reduce-scatter.7.cloned.1.call-done = bf16[128,2048]{1,0:T(8,128)(2,1)} async-done(((bf16[1024,2048]{1,0:T(8,128)(2,1)}), bf16[128,2048]{1,0:T(8,128)(2,1)}) %reduce-scatter.7.cloned.1.call-update) | async-done | bytes 524304 | tf_op jit(solution)/shard_map/reduce_scatter | solution.py:311
  1157.3 45.4 %reduce-scatter.9.cloned.1.call-done = bf16[512,4,256]{2,0,1:T(8,128)(2,1)} async-done(((bf16[2048,4,256]{2,0,1:T(8,128)(2,1)}), bf16[512,4,256]{2,0,1:T(8,128)(2,1)}) %reduce-scatter.9.cloned.1.call-update) | async-done | bytes 1048592 | tf_op jit(solution)/shard_map/reduce_scatter | solution.py:305
  1204.9 40.0 %all-reduce = (f32[2048]{0:T(1024)}, f32[128]{0:T(128)}, f32[128]{0:T(128)}, f32[2048]{0:T(1024)}, f32[3]{0:T(128)S(1)}) all-reduce(f32[2048]{0:T(1024)S(1)} %get-tuple-element.286, f32[128]{0:T(128)S(1)} %get-tuple-element.282, f32[128]{0:T(128)S(1)} %get-tuple-element.280, ...), channel_id=1, replica_groups=mesh['dp'=4,'expert'=8] {'dp','expert'}, use_global_device_ids=true, to_apply=%region_35.36 | all-reduce | flops 4355 | bytes 34840 | tf_op jit(solution)/shard_map/psum | solution.py:326
  1250.4 135.3 %reduce-scatter.11.cloned.1.call-done = bf16[256,2,3,2048]{3,0,2,1:T(8,128)(2,1)} async-done(((bf16[1024,2,3,2048]{3,0,2,1:T(8,128)(2,1)}), bf16[256,2,3,2048]{3,0,2,1:T(8,128)(2,1)}) %reduce-scatter.11.cloned.1.call-update) | async-done | bytes 6291472 | tf_op jit(solution)/shard_map/reduce_scatter | solution.py:268
  1409.0 105.3 %all-reduce.3.cloned.1.call-done = f32[2048,16]{0,1:T(8,128)} async-done(((f32[2048,16]{0,1:T(8,128)}), f32[2048,16]{0,1:T(8,128)}) %all-reduce.3.cloned.1.call-update) | async-done | bytes 131088 | tf_op jit(solution)/shard_map/psum | solution.py:326
  (310 shorter events, 238.7 us)
Async XLA Ops:
  7.2 322.1 %copy-start = (bf16[2048,16]{0,1:T(8,128)(2,1)S(1)}, bf16[2048,16]{0,1:T(8,128)(2,1)}, u32[]{:S(2)}) copy-start(bf16[2048,16]{0,1:T(8,128)(2,1)} %param.29) | copy-start | bytes 196612
  7.2 34.2 %all-gather.9.cloned.1.call-start = ((), (), s32[]{:S(2)}) async-start(), calls=%async_computation.9 | async-start | bytes 3932160 | tf_op jit(solution)/shard_map/all_gather | solution.py:170
  9.6 108.0 %all-gather.7.cloned.1.call-start = ((), (), s32[]{:S(2)}) async-start(), calls=%async_computation.8 | async-start | bytes 4718592 | tf_op jit(solution)/shard_map/all_gather | solution.py:168
  13.5 139.1 %all-gather.11.cloned.1.call-start = ((), (), s32[]{:S(2)}) async-start(), calls=%async_computation.10 | async-start | bytes 1310720 | tf_op jit(solution)/shard_map/all_gather | solution.py:171
  14.2 292.0 %reduce-scatter.5.cloned.1.call-start = ((), (), s32[]{:S(2)}) async-start(), calls=%async_computation.11 | async-start | bytes 9437184 | tf_op jit(solution)/shard_map/reduce_scatter | solution.py:192
  16.8 114.7 %copy-start.19 = (f32[1024,64]{1,0:T(8,128)}, f32[1024,64]{1,0:T(8,128)S(1)}, u32[]{:S(2)}) copy-start(f32[1024,64]{1,0:T(8,128)S(1)} %get-tuple-element.360) | copy-start | bytes 786436
  16.8 114.7 %copy-start.21 = (f32[1024,64]{1,0:T(8,128)}, f32[1024,64]{1,0:T(8,128)S(1)}, u32[]{:S(2)}) copy-start(f32[1024,64]{1,0:T(8,128)S(1)} %get-tuple-element.361) | copy-start | bytes 786436
  158.7 309.2 %all-gather.13.cloned.1.call-start = ((), (), s32[]{:S(2)}) async-start(), calls=%async_computation.12 | async-start | bytes 20971520 | tf_op jit(solution)/shard_map/all_gather | solution.py:172
  165.6 140.6 %copy-start.13 = (bf16[128,2048]{1,0:T(8,128)(2,1)S(1)}, bf16[128,2048]{1,0:T(8,128)(2,1)}, u32[]{:S(2)}) copy-start(bf16[128,2048]{1,0:T(8,128)(2,1)} %param.18) | copy-start | bytes 1572868
  165.6 142.8 %copy-start.36 = (f32[2048]{0:T(1024)S(1)}, f32[2048]{0:T(1024)}, u32[]{:S(2)}) copy-start(f32[2048]{0:T(1024)} %param.28) | copy-start | bytes 24580
  308.4 634.6 %copy-start.11 = (f32[128,2048]{1,0:T(8,128)}, f32[128,2048]{1,0:T(8,128)S(1)}, u32[]{:S(2)}) copy-start(f32[128,2048]{1,0:T(8,128)S(1)} %get-tuple-element.336) | copy-start | bytes 3145732
  308.4 634.6 %copy-start.49 = (f32[128]{0:T(128)}, f32[128]{0:T(128)S(1)}, u32[]{:S(2)}) copy-start(f32[128]{0:T(128)S(1)} %add_rsqrt_fusion.2) | copy-start | bytes 1540
  319.6 143.5 %all-to-all-start = ((bf16[8,2,96,2048]{3,2,1,0:T(8,128)(2,1)}), bf16[8,2,96,2048]{3,2,1,0:T(8,128)(2,1)}, u32[]{:S(2)}, u32[]{:S(2)}) async-start(bf16[8,2,96,2048]{3,2,1,0:T(8,128)(2,1)} %bitcast.286), calls=%async_computation.1 | async-start | bytes 12582912 | tf_op jit(solution)/shard_map/all_to_all | solution.py:213
  324.6 163.7 %all-gather.15.cloned.1.call-start = ((), (), s32[]{:S(2)}) async-start(), calls=%async_computation.13 | async-start | bytes 10485760 | tf_op jit(solution)/shard_map/all_gather | solution.py:173
  463.0 142.5 %all-to-all-start.2 = ((bf16[8,2,96,2048]{3,2,1,0:T(8,128)(2,1)}), bf16[8,2,96,2048]{3,2,1,0:T(8,128)(2,1)}, u32[]{:S(2)}, u32[]{:S(2)}) async-start(bf16[8,2,96,2048]{3,2,1,0:T(8,128)(2,1)} %bitcast.288), calls=%async_computation.3 | async-start | bytes 12582912 | tf_op jit(solution)/shard_map/all_to_all | solution.py:245
  637.0 142.0 %all-to-all-start.1 = ((bf16[8,2,96,2048]{3,2,1,0:T(8,128)(2,1)}), bf16[8,2,96,2048]{3,2,1,0:T(8,128)(2,1)}, u32[]{:S(2)}, u32[]{:S(2)}) async-start(bf16[8,2,96,2048]{3,2,1,0:T(8,128)(2,1)} %copy.179), calls=%async_computation.2 | async-start | bytes 12582912 | tf_op jit(solution)/shard_map/all_to_all | solution.py:223
  779.1 142.0 %all-to-all-start.3 = ((bf16[8,2,96,2048]{3,2,1,0:T(8,128)(2,1)}), bf16[8,2,96,2048]{3,2,1,0:T(8,128)(2,1)}, u32[]{:S(2)}, u32[]{:S(2)}) async-start(bf16[8,2,96,2048]{3,2,1,0:T(8,128)(2,1)} %bitcast.287), calls=%async_computation.4 | async-start | bytes 12582912 | tf_op jit(solution)/shard_map/all_to_all | solution.py:257
  783.8 233.6 %all-gather.17.cloned.1.call-start = ((), (), s32[]{:S(2)}) async-start(), calls=%async_computation.14 | async-start | bytes 4718592 | tf_op jit(solution)/shard_map/all_gather | solution.py:284
  945.2 210.6 %reduce-scatter.7.cloned.1.call-start = ((), (), s32[]{:S(2)}) async-start(), calls=%async_computation.15 | async-start | bytes 4718592 | tf_op jit(solution)/shard_map/reduce_scatter | solution.py:311
  1069.5 133.2 %reduce-scatter.9.cloned.1.call-start = ((), (), s32[]{:S(2)}) async-start(), calls=%async_computation.16 | async-start | bytes 5242880 | tf_op jit(solution)/shard_map/reduce_scatter | solution.py:305
  1080.3 305.4 %reduce-scatter.11.cloned.1.call-start = ((), (), s32[]{:S(2)}) async-start(), calls=%async_computation.18 | async-start | bytes 31457280 | tf_op jit(solution)/shard_map/reduce_scatter | solution.py:268
  1135.6 378.7 %all-reduce.3.cloned.1.call-start = ((), (), s32[]{:S(2)}) async-start(), calls=%async_computation.17 | async-start | bytes 262144 | tf_op jit(solution)/shard_map/psum | solution.py:326
  1139.5 108.3 %copy-start.50 = (f32[128]{0:T(128)S(1)}, f32[128]{0:T(128)}, u32[]{:S(2)}) copy-start(f32[128]{0:T(128)} %copy-done.49) | copy-start | bytes 1540
  1393.8 122.0 %copy-start.1 = (bf16[2048,16]{0,1:T(8,128)(2,1)S(1)}, bf16[2048,16]{0,1:T(8,128)(2,1)}, u32[]{:S(2)}) copy-start(bf16[2048,16]{0,1:T(8,128)(2,1)} %param.29) | copy-start | bytes 196612
  (61 other events, 1160.5 us)
Sparse Core Ops, SparseCore 0:
  10.2 31.2 all-gather.8
  44.1 73.3 all-gather.6
  119.2 14.9 all-gather.10
  158.9 147.3 reduce-scatter.4
  308.3 104.9 all-gather.12
  414.8 58.2 all-gather.14
  945.3 72.0 all-gather.16
  1069.6 86.1 reduce-scatter.6
  1158.3 44.2 reduce-scatter.8
  1205.2 180.4 reduce-scatter.10
  1391.8 122.4 all-reduce.2
where the time goes:
time: 1530 us; the launch traced here: 1520 us
  waiting for transfers between devices  1080 us (71%)
  matrix products  170 us (11%)
  local copies, waits for them, and re-layouts  106 us (7%)
  other arithmetic  88.2 us (6%)
  blocking collectives  40 us (3%)
  starting transfers between devices  20.8 us (1%)
  between operations  15.3 us (1%)
    reduce_scatter x1, waiting for transfers between devices, on_device(): lax.psum_scatter(jnp.concatenate([gate_up_term, down_term[:, :, None, :]]...  135 us
    reduce_scatter x1, waiting for transfers between devices, on_device(): lax.psum_scatter(jnp.einsum('gf,df->gd', attended_low, out_local, preferr...  134 us
    all_to_all x1, waiting for transfers between devices, on_device(): lax.all_to_all(send_rows, 'expert', split_axis=0, concat_axis=0, tiled=True)  123 us
    all_to_all x1, waiting for transfers between devices, on_device(): lax.all_to_all(grad_in, 'expert', split_axis=0, concat_axis=0, tiled=True)  119 us
    all_to_all x1, waiting for transfers between devices, on_device(): lax.all_to_all(grad_send, 'expert', split_axis=0, concat_axis=0, tiled=True)  117 us
    all_to_all x1, waiting for transfers between devices, on_device(): lax.all_to_all(expert_out, 'expert', split_axis=0, concat_axis=0, tiled=T...  110 us
    psum x1, waiting for transfers between devices, on_device(): lax.psum((grad_attn_gain, grad_query_gain, grad_key_gain, grad_ffn_gain,...  105 us
    all_gather x1, waiting for transfers between devices, on_device(): features = lax.all_gather(attn_low, 'expert', axis=0, tiled=True)  76.1 us
  transfers between devices with their start and end apart: 15, of which 12 were waited for; matrix products, arithmetic and copies ran while one was open for 16% of the time, Pallas kernels for 0%

commit v1 on v0

v1 whole, which is shorter than its diff:
```python
import functools

import jax
import jax.numpy as jnp
from jax import lax
from jax.experimental import pallas as pl
from jax.experimental.pallas import tpu as pltpu
from jax.sharding import PartitionSpec as P

eps_norm = 1e-06
rope_base = 10000.0
big_negative = -1e30
bf16 = jnp.bfloat16
f32 = jnp.float32


def expert_ring(count):
    nz = 4
    ny = count // nz
    walk = [(z, 0) for z in range(nz)]
    for z in range(nz - 1, -1, -1):
        ys = range(1, ny) if (nz - 1 - z) % 2 == 0 else range(ny - 1, 0, -1)
        walk += [(z, y) for y in ys]
    return [z * ny + y for z, y in walk]


def dot(a, b, dims):
    return lax.dot_general(a, b, (dims, ((), ())), preferred_element_type=f32)


class Ring:
    def __init__(self, count):
        self.count = count
        self.order = expert_ring(count)
        n = count
        self.down = [(self.order[(i + 1) % n], self.order[i]) for i in range(n)]
        self.up = [(self.order[i], self.order[(i + 1) % n]) for i in range(n)]
        place = [0] * n
        for i, m in enumerate(self.order):
            place[m] = i
        me = lax.axis_index("expert")
        self.me = me
        self.pos = jnp.array(place, jnp.int32)[me]
        ids = jnp.arange(n, dtype=jnp.int32)
        places = (self.pos + jnp.array(slot_order(n), jnp.int32)) % n
        table = jnp.array(self.order, jnp.int32)
        self.members = jnp.sum(jnp.where(places[:, None] == ids[None, :], table[None, :], 0), axis=1)

    def send(self, x, way):
        return lax.ppermute(x, "expert", way)

    def gather(self, own):
        n = self.count
        half = own.shape[0] // 2
        slots = [None] * n
        slots[0] = own
        ahead = behind = own
        for s in range(1, n // 2):
            ahead = self.send(ahead, self.down)
            behind = self.send(behind, self.up)
            slots[s] = ahead
            slots[n - s] = behind
        slots[n // 2] = jnp.concatenate(
            [self.send(ahead[:half], self.down), self.send(behind[half:], self.up)], axis=0
        )
        return slots

    def reduce(self, parts):
        n = self.count
        far = parts[n // 2]
        half = far.shape[0] // 2
        fwd, back = far[:half].astype(bf16), far[half:].astype(bf16)
        for s in range(n // 2 - 1, -1, -1):
            fwd = self.send(fwd, self.up)
            back = self.send(back, self.down)
            if s == 0:
                break
            a, b = parts[s].astype(f32), parts[n - s].astype(f32)
            if s == n // 2 - 1:
                fwd = jnp.concatenate([a[:half] + fwd.astype(f32), a[half:]], axis=0)
                back = jnp.concatenate([b[:half], b[half:] + back.astype(f32)], axis=0)
            else:
                fwd = a + fwd.astype(f32)
                back = b + back.astype(f32)
            fwd, back = fwd.astype(bf16), back.astype(bf16)
        return parts[0].astype(f32) + fwd.astype(f32) + back.astype(f32)


class Chips:
    def __init__(self, count):
        self.steps = count // 2
        self.swap = [(i, i ^ 1) for i in range(count)]

    def other_core(self, x):
        return lax.ppermute(x, "dp", self.swap)

    def from_ahead(self, x, step):
        n = self.steps
        return lax.ppermute(
            x, "dp", [(((i // 2 + step) % n) * 2 + i % 2, i) for i in range(2 * n)]
        )

    def to_ahead(self, x, step):
        n = self.steps
        return lax.ppermute(
            x, "dp", [(i, ((i // 2 + step) % n) * 2 + i % 2) for i in range(2 * n)]
        )

    def gather(self, own):
        blocks = []
        for step in range(self.steps):
            block = own if step == 0 else self.from_ahead(own, step)
            blocks += [block, self.other_core(block)]
        return blocks

    def reduce(self, term):
        total = None
        for step in range(self.steps - 1, -1, -1):
            theirs = self.other_core(term(2 * step + 1).astype(bf16)).astype(f32)
            mine = term(2 * step) + theirs
            if step:
                mine = self.to_ahead(mine.astype(bf16), step).astype(f32)
            total = mine if total is None else total + mine
        return total


def expert_kernel(
    steps,
    num_experts,
    f_ref,
    h_ref,
    mask_ref,
    sel_ref,
    wr_ref,
    w_ref,
    *refs,
):
    gc_ref, gp_ref, ga_ref, gl_ref, acc, router, gate_sums = refs[-7:]
    step = pl.program_id(0)
    experts_dev = sel_ref.shape[0]
    ff_tile = w_ref.shape[3]
    rows_in = f_ref[...]

    @pl.when(step == 0)
    def _():
        logits = jnp.dot(rows_in, wr_ref[...], preferred_element_type=f32)
        lane = lax.broadcasted_iota(jnp.int32, logits.shape, 1)
        logits = jnp.where(lane < num_experts, logits, big_negative)
        exps = jnp.exp(logits - jnp.max(logits, axis=-1, keepdims=True))
        router[...] = exps / jnp.sum(exps, axis=-1, keepdims=True)
        gate_sums[...] = jnp.zeros_like(gate_sums)
        acc[...] = jnp.zeros_like(acc)

    lanes = sel_ref[pl.ds(step % experts_dev, 1), :] * mask_ref[...].astype(f32)
    gate = jnp.sum(router[...] * lanes, axis=-1, keepdims=True)
    weight_gate, weight_up = w_ref[0, 0, 0], w_ref[0, 0, 1]
    gate_pre = dot(rows_in, weight_gate, ((1,), (1,)))
    up_pre = dot(rows_in, weight_up, ((1,), (1,)))
    back_hidden = h_ref[...]
    sigmoid_gate = 1.0 / (1.0 + jnp.exp(-gate_pre))
    silu_gate = gate_pre * sigmoid_gate
    act = silu_gate * up_pre
    gate_sums[...] += lanes * jnp.sum(act * back_hidden, axis=-1, keepdims=True)
    grad_hidden = back_hidden * gate
    grad_gate = grad_hidden * up_pre * sigmoid_gate * (1.0 + gate_pre * (1.0 - sigmoid_gate))
    grad_gate = grad_gate.astype(bf16)
    grad_up = (grad_hidden * silu_gate).astype(bf16)
    gp_ref[:, :ff_tile] = grad_gate
    gp_ref[:, ff_tile:] = grad_up
    ga_ref[...] = (act * gate).astype(bf16)
    acc[...] += jnp.dot(grad_gate, weight_gate, preferred_element_type=f32) + jnp.dot(
        grad_up, weight_up, preferred_element_type=f32
    )

    @pl.when(step == steps - 1)
    def _():
        sums = gate_sums[...]
        inner = jnp.sum(router[...] * sums, axis=-1, keepdims=True)
        grad_logits = (router[...] * (sums - inner)).astype(bf16)
        gl_ref[...] = grad_logits
        total = acc[...] + dot(grad_logits, wr_ref[...], ((1,), (1,)))
        gc_ref[...] = total.astype(bf16)


def expert_chunk(index, chunks, num_experts, f, hidden, mask, select, router, weights, kept):
    blocks, experts_dev, _, ff_tile, width = weights.shape
    steps = blocks * experts_dev
    rows = f.shape[0]
    whole = pl.BlockSpec(memory_space=pltpu.VMEM)
    in_specs = [
        whole,
        pl.BlockSpec((rows, ff_tile), lambda j: (index, j)),
        pl.BlockSpec((rows, 128), lambda j: (index, 0)),
        whole,
        whole,
        pl.BlockSpec(
            (1, 1, 2, ff_tile, width), lambda j: (j // experts_dev, j % experts_dev, 0, 0, 0)
        ),
    ]
    args = [f, hidden, mask, select, router, weights]
    aliases = {}
    if kept is not None:
        in_specs += [pl.BlockSpec(memory_space=pl.ANY)] * 2
        aliases = {len(args): 1, len(args) + 1: 2}
        args += list(kept)
    total = rows * chunks
    return pl.pallas_call(
        functools.partial(expert_kernel, steps, num_experts),
        grid=(steps,),
        in_specs=in_specs,
        out_specs=[
            pl.BlockSpec((rows, width), lambda j: (0, 0)),
            pl.BlockSpec((rows, 2 * ff_tile), lambda j: (index, j)),
            pl.BlockSpec((rows, ff_tile), lambda j: (index, j)),
            pl.BlockSpec((rows, 128), lambda j: (0, 0)),
        ],
        out_shape=[
            jax.ShapeDtypeStruct((rows, width), bf16),
            jax.ShapeDtypeStruct((total, 2 * ff_tile * steps), bf16),
            jax.ShapeDtypeStruct((total, ff_tile * steps), bf16),
            jax.ShapeDtypeStruct((rows, 128), bf16),
        ],
        scratch_shapes=[
            pltpu.VMEM((rows, width), f32),
            pltpu.VMEM((rows, 128), f32),
            pltpu.VMEM((rows, 128), f32),
        ],
        input_output_aliases=aliases,
        compiler_params=pltpu.CompilerParams(vmem_limit_bytes=48 << 20),
        cost_estimate=pl.CostEstimate(
            flops=8 * rows * ff_tile * steps * width,
            bytes_accessed=4 * ff_tile * steps * width,
            transcendentals=0,
        ),
    )(*args)


def all_sum(x):
    for axis in ("dp", "expert"):
        n = lax.axis_size(axis)
        bit = 1
        while bit < n:
            x = x + lax.ppermute(x, axis, [(i, i ^ bit) for i in range(n)])
            bit *= 2
    return x


def slot_order(n):
    return [k for i in range(n // 2) for k in ((n - i) % n, i + 1)]


def in_order(slots):
    return jnp.concatenate([slots[k] for k in slot_order(len(slots))], axis=0)


def after(x, *others):
    return lax.optimization_barrier((x, *others))[0]


def rms_scale(values):
    return lax.rsqrt(jnp.mean(values * values, axis=-1, keepdims=True) + eps_norm)


def norm_back(grad_out, norm_gain, normed, row_scale):
    scaled = grad_out * norm_gain
    inner_mean = jnp.mean(normed * scaled, axis=-1, keepdims=True)
    return row_scale * (scaled - normed * inner_mean)


def seq_layout(lengths, seq_order, places):
    seq_count = lengths.shape[0]
    ids = jnp.arange(seq_count, dtype=jnp.int32)
    picked_seq = seq_order[:, None] == ids[None, :]
    ordered = jnp.sum(jnp.where(picked_seq, lengths[None, :], 0), axis=1)
    upto = ids[:, None] >= ids[None, :]
    seq_ends = jnp.sum(jnp.where(upto, ordered[None, :], 0), axis=1)
    starts = seq_ends - ordered
    segment = jnp.sum((places[:, None] >= seq_ends[None, :]).astype(jnp.int32), axis=1)
    member = segment[:, None] == ids[None, :]
    position = places - jnp.sum(jnp.where(member, starts[None, :], 0), axis=1)
    return (segment, position)


def rope_tables(position, head_dim):
    half_dim = head_dim // 2
    inv_freq = rope_base ** (-(jnp.arange(half_dim, dtype=f32) * 2.0 / head_dim))
    angles = position.astype(f32)[:, None] * inv_freq[None, :]
    return (jnp.cos(angles), jnp.sin(angles))


def rotate(values, cos_rows, sin_rows):
    half_dim = values.shape[-1] // 2
    a, b = values[..., :half_dim], values[..., half_dim:]
    return jnp.concatenate([a * cos_rows - b * sin_rows, b * cos_rows + a * sin_rows], axis=-1)


def rotate_back(grad_out, cos_rows, sin_rows):
    return rotate(grad_out, cos_rows, -sin_rows)


def attend(query, key, value, segment, scaling):
    scores = jnp.einsum("hqd,hkd->hqk", query, key, preferred_element_type=f32) * scaling
    allowed = segment[:, None] == segment[None, :]
    scores = jnp.where(allowed[None], scores, big_negative)
    row_max = jnp.max(scores, axis=-1, keepdims=True)
    exp_scores = jnp.exp(scores - row_max)
    row_sum = jnp.sum(exp_scores, axis=-1, keepdims=True)
    probs = (exp_scores / row_sum).astype(bf16)
    attended = jnp.einsum("hqk,hkd->hqd", probs, value, preferred_element_type=f32)
    return attended, row_max + jnp.log(row_sum)


def attend_back(query, key, value, grad, segment, log_sums, scaling):
    scores = jnp.einsum("hqd,hkd->hqk", query, key, preferred_element_type=f32) * scaling
    allowed = segment[:, None] == segment[None, :]
    scores = jnp.where(allowed[None], scores, big_negative)
    probs = jnp.exp(scores - log_sums)
    grad_probs = jnp.einsum("hqd,hkd->hqk", grad, value, preferred_element_type=f32)
    inner = jnp.sum(probs * grad_probs, axis=-1, keepdims=True)
    grad_scores = (probs * (grad_probs - inner)).astype(bf16)
    grad_query = jnp.einsum("hqk,hkd->hqd", grad_scores, key, preferred_element_type=f32) * scaling
    grad_key = jnp.einsum("hqk,hqd->hkd", grad_scores, query, preferred_element_type=f32) * scaling
    grad_value = jnp.einsum("hqk,hqd->hkd", probs.astype(bf16), grad, preferred_element_type=f32)
    return grad_query, grad_key, grad_value


def on_device(
    hidden_states,
    out_grad,
    seq_lengths,
    seq_order,
    expert_routes,
    attn_gain,
    qkv_weight,
    out_weight,
    query_gain,
    key_gain,
    ffn_gain,
    router_weight,
    expert_gate_up,
    expert_down,
):
    tok_rows, width = hidden_states.shape
    head_dim = query_gain.shape[0]
    ff_dev, experts_dev = expert_gate_up.shape[:2]
    n_dp = lax.axis_size("dp")
    n_exp = lax.axis_size("expert")
    ff = ff_dev * n_dp
    num_experts = experts_dev * n_exp
    scaling = head_dim ** (-0.5)
    ring = Ring(n_exp)
    rows = tok_rows * n_exp

    chips = Chips(n_dp)
    qkv_full = lax.all_gather(qkv_weight.transpose(1, 0, 2), "dp", axis=1, tiled=True)
    out_full = lax.all_gather(out_weight, "dp", axis=0, tiled=True)
    local_width = out_full.shape[1]
    heads = local_width // head_dim

    states_slots = ring.gather(hidden_states)
    states_all = in_order(states_slots).astype(f32)
    attn_scale = rms_scale(states_all)
    attn_normed = states_all * attn_scale
    features = (attn_normed * attn_gain).astype(bf16)

    gu_blocks = chips.gather(after(expert_gate_up, states_slots[1]).transpose(1, 2, 0, 3))
    gu_all = jnp.stack(gu_blocks)
    down_blocks = chips.gather(after(expert_down, gu_blocks[2]).transpose(1, 0, 2))
    down_all = jnp.stack(down_blocks).reshape(experts_dev * ff, width)

    expert_ids = jnp.arange(num_experts, dtype=jnp.int32)
    chosen = jnp.any(expert_routes[:, :, None] == expert_ids[None, None, :], axis=1)
    chosen = jnp.pad(chosen.astype(bf16), ((0, 0), (0, 128 - num_experts)))
    sent_grad = jnp.concatenate([out_grad, chosen], axis=1)
    grad_slots = ring.gather(after(sent_grad, states_slots[n_exp // 2]))
    grad_top_all = in_order([g[:, :width] for g in grad_slots])
    chosen_all = in_order([g[:, width:] for g in grad_slots])

    place = (ring.members[:, None] * tok_rows + jnp.arange(tok_rows, dtype=jnp.int32)).reshape(-1)
    segment, position = seq_layout(seq_lengths[0], seq_order[0], place)
    cos_rows, sin_rows = rope_tables(position, head_dim)

    projected = jnp.einsum("td,cdf->ctf", features, qkv_full, preferred_element_type=f32)
    head_proj = projected.reshape(3, rows, heads, head_dim).transpose(0, 2, 1, 3)
    query_scale, key_scale = rms_scale(head_proj[0]), rms_scale(head_proj[1])
    query_normed, key_normed = head_proj[0] * query_scale, head_proj[1] * key_scale
    query = rotate(query_normed * query_gain, cos_rows, sin_rows).astype(bf16)
    key = rotate(key_normed * key_gain, cos_rows, sin_rows).astype(bf16)
    value = head_proj[2].astype(bf16)
    attended, log_sums = attend(query, key, value, segment, scaling)
    attended = attended.transpose(1, 0, 2).reshape(rows, local_width).astype(bf16)
    branch_part = dot(attended, out_full, ((1,), (1,)))

    def slots_of(x):
        where = slot_order(n_exp)
        return [x[i * tok_rows : (i + 1) * tok_rows] for i in map(where.index, range(n_exp))]

    branch = ring.reduce(slots_of(branch_part))
    states = hidden_states.astype(f32)
    mixed = states + branch
    ffn_scale = rms_scale(mixed)
    ffn_normed = mixed * ffn_scale
    ffn_in = (ffn_normed * ffn_gain).astype(bf16)
    ffn_slots = ring.gather(ffn_in)
    ffn_all = in_order(ffn_slots)

    back_hidden = dot(grad_top_all, down_all, ((1,), (1,)))
    router_wide = jnp.pad(router_weight, ((0, 0), (0, 128 - num_experts)))
    lanes = jnp.arange(128, dtype=jnp.int32)
    own_ids = ring.me * experts_dev + jnp.arange(experts_dev, dtype=jnp.int32)
    select = (lanes[None, :] == own_ids[:, None]).astype(f32)
    kept = None
    grad_ffn_parts = [None] * n_exp
    logit_chunks = []
    chunks = n_exp // 2
    for i in range(chunks):
        a, b = (n_exp - i) % n_exp, i + 1
        chunk = jnp.concatenate([ffn_slots[a], ffn_slots[b]], axis=0)
        grad_chunk, grad_pre, gated_act, logit_low = expert_chunk(
            i, chunks, num_experts, chunk, back_hidden, chosen_all, select, router_wide, gu_all, kept
        )
        kept = (grad_pre, gated_act)
        grad_ffn_parts[a], grad_ffn_parts[b] = grad_chunk[:tok_rows], grad_chunk[tok_rows:]
        logit_chunks.append(logit_low)
    logit_low = jnp.concatenate(logit_chunks, axis=0)
    router_part = dot(ffn_all, logit_low, ((0,), (0,)))[:, :num_experts]
    grad_ffn = ring.reduce(grad_ffn_parts)
    moe_part = dot(gated_act, down_all, ((1,), (0,)))

    gu_cols, down_cols = experts_dev * 2 * ff_dev, experts_dev * ff_dev
    down_grad = chips.reduce(
        lambda b: dot(gated_act[:, b * down_cols : (b + 1) * down_cols], grad_top_all, ((0,), (0,)))
    ).reshape(experts_dev, ff_dev, width)
    gate_up_grad = chips.reduce(
        lambda b: dot(grad_pre[:, b * gu_cols : (b + 1) * gu_cols], ffn_all, ((0,), (0,)))
    ).reshape(experts_dev, 2, ff_dev, width)

    grad_top = out_grad.astype(f32)
    ffn_gain_part = jnp.sum(ffn_normed * grad_ffn, axis=0)
    grad_mixed = grad_top + norm_back(grad_ffn, ffn_gain, ffn_normed, ffn_scale)
    branch_slots = ring.gather(grad_mixed.astype(bf16))
    grad_rows = in_order(branch_slots)
    moe_part = after(moe_part.astype(bf16), branch_slots[n_exp // 2])
    moe = ring.reduce(slots_of(moe_part))
    output = mixed + moe

    grad_attended = dot(grad_rows, out_full, ((1,), (0,))).astype(bf16)
    grad_attended = grad_attended.reshape(rows, heads, head_dim).transpose(1, 0, 2)
    grad_query, grad_key, grad_value = attend_back(
        query, key, value, grad_attended, segment, log_sums, scaling
    )
    grad_query = rotate_back(grad_query, cos_rows, sin_rows)
    grad_key = rotate_back(grad_key, cos_rows, sin_rows)
    query_gain_part = jnp.sum(query_normed * grad_query, axis=(0, 1))
    key_gain_part = jnp.sum(key_normed * grad_key, axis=(0, 1))
    grad_query = norm_back(grad_query, query_gain, query_normed, query_scale)
    grad_key = norm_back(grad_key, key_gain, key_normed, key_scale)
    grad_proj = (
        jnp.stack([grad_query, grad_key, grad_value], axis=0)
        .astype(bf16)
        .transpose(0, 2, 1, 3)
        .reshape(3, rows, local_width)
    )
    features_part = jnp.einsum("ctf,cdf->td", grad_proj, qkv_full, preferred_element_type=f32)
    grad_features = ring.reduce(slots_of(features_part))
    qkv_term = jnp.einsum("td,ctf->cdf", features, grad_proj, preferred_element_type=f32)
    out_term = dot(grad_rows, attended, ((0,), (0,)))
    attn_sums = lax.psum_scatter(
        jnp.concatenate([qkv_term, out_term[None]], axis=0).astype(bf16),
        "dp",
        scatter_dimension=1,
        tiled=True,
    ).astype(f32)
    attn_gain_part = jnp.sum(attn_normed * features_part, axis=0)
    own_scale = rms_scale(states)
    input_grad = grad_mixed + norm_back(grad_features, attn_gain, states * own_scale, own_scale)

    squares = jnp.stack([jnp.sum(output * output), jnp.sum(branch * branch), jnp.sum(moe * moe)])
    wide = all_sum(jnp.concatenate([router_part.T, ffn_gain_part[None]], axis=0))
    small = all_sum(
        jnp.concatenate(
            [attn_gain_part, query_gain_part, key_gain_part, jnp.pad(squares, (0, 125))]
        ).reshape(-1, 128)
    ).reshape(-1)
    stream_rms = jnp.sqrt(small[width + 2 * head_dim :][:3] / (rows * n_dp * width))
    return (
        output.astype(bf16),
        input_grad.astype(bf16),
        small[:width],
        attn_sums[:3].transpose(1, 0, 2),
        attn_sums[3],
        small[width : width + head_dim],
        small[width + head_dim : width + 2 * head_dim],
        wide[num_experts],
        wide[:num_experts].T,
        gate_up_grad.transpose(2, 0, 1, 3),
        down_grad.transpose(1, 0, 2),
        stream_rms,
    )


def solution(mesh):
    in_specs = (
        P(("dp", "expert"), None),
        P(("dp", "expert"), None),
        P("dp", None),
        P("dp", None),
        P(("dp", "expert"), None),
        P(),
        P("dp", None, "expert"),
        P("dp", "expert"),
        P(),
        P(),
        P(),
        P(),
        P("dp", "expert", None, None),
        P("dp", "expert", None),
    )
    out_specs = (
        P(("dp", "expert"), None),
        P(("dp", "expert"), None),
        P(),
        P("dp", None, "expert"),
        P("dp", "expert"),
        P(),
        P(),
        P(),
        P(),
        P("dp", "expert", None, None),
        P("dp", "expert", None),
        P(),
    )
    return jax.shard_map(
        on_device, mesh=mesh, in_specs=in_specs, out_specs=out_specs, check_vma=False
    )
```

time: 1530 us -> 722 us (0.47)
  waiting for transfers between devices: 1080 us -> 296 us
  starting transfers between devices: 20.8 us -> 92.5 us
  Pallas kernels: 0 us -> 68 us
  matrix products: 170 us -> 122 us
  blocking collectives: 40 us -> 0 us
  local copies, waits for them, and re-layouts: 106 us -> 67.2 us
  other arithmetic: 88.2 us -> 53.7 us
    all_to_all x4 -> x0, waiting for transfers between devices: 469 us -> none  [the longest x1 123 us: on_device(): lax.all_to_all(send_rows, 'expert', split_axis=0, concat_axis=0, tiled=True)]
    reduce_scatter x4 -> x1, waiting for transfers between devices: 331 us -> 0.01 us  [on_device(): lax.psum_scatter(jnp.concatenate([qkv_term, out_term[None]], axis=0).asty...]
    ppermute x0 -> x86, waiting for transfers between devices: none -> 296 us  [the longest x64 193 us: send(): return lax.ppermute(x, 'expert', way)]
    all_gather x6 -> x2, waiting for transfers between devices: 173 us -> 0.04 us  [the longest x1 0.02 us: on_device(): lax.all_gather(qkv_weight.transpose(1, 0, 2), 'dp', axis=1, tiled=True)]
    psum x1 -> x0, waiting for transfers between devices: 105 us -> none  [on_device(): lax.psum((grad_attn_gain, grad_query_gain, grad_key_gain, grad_ffn_gain,...]
    ppermute x0 -> x86, starting transfers between devices: none -> 92.4 us  [the longest x64 71.6 us: send(): return lax.ppermute(x, 'expert', way)]
    pallas_call x0 -> x4, Pallas kernels: none -> 68 us  [expert_chunk(): pl.pallas_call(functools.partial(expert_kernel, steps, num_experts), grid...]
    dot_general x29 -> x23, matrix products: 170 us -> 122 us  [the longest x14 86.8 us: dot(): return lax.dot_general(a, b, (dims, ((), ())), preferred_element_type=f32)]
  transfers between devices with their start and end apart: 15 -> 89, of which waited for: 12 -> 40; matrix products, arithmetic and copies ran while one was open for 16% -> 30% of each run, Pallas kernels for 0% -> 7%
where the time goes in v1:
time: 722 us; the launch traced here: 715 us
  waiting for transfers between devices  296 us (41%)
  matrix products  122 us (17%)
  starting transfers between devices  92.5 us (13%)
  Pallas kernels  68 us (9%)
  local copies, waits for them, and re-layouts  67.2 us (9%)
  other arithmetic  53.7 us (7%)
  between operations  15.7 us (2%)
    ppermute x64, waiting for transfers between devices, send(): return lax.ppermute(x, 'expert', way)  193 us
    dot_general x14, matrix products, dot(): return lax.dot_general(a, b, (dims, ((), ())), preferred_element_type=f32)  86.8 us
    ppermute x2, waiting for transfers between devices, to_ahead(): lax.ppermute(x, 'dp', [(i, (i // 2 + step) % n * 2 + i % 2) for i in rang...  86.2 us
    ppermute x64, starting transfers between devices, send(): return lax.ppermute(x, 'expert', way)  71.6 us
    pallas_call x4, Pallas kernels, expert_chunk(): pl.pallas_call(functools.partial(expert_kernel, steps, num_experts), grid...  68 us
    unnamed x157, local copies, waits for them, and re-layouts  34.6 us
  transfers between devices with their start and end apart: 89, of which 40 were waited for; matrix products, arithmetic and copies ran while one was open for 30% of the time, Pallas kernels for 7%

profile of v1, /device:TPU:0, one launch (start us, length us, event | category | flops | bytes accessed | tf_op | source)
XLA Modules:
  0.0 715.0 jit_solution(14539763303818519630)
XLA Ops:
  51.7 11.5 %collective-permute-done.27 = bf16[128,2176]{1,0:T(8,128)(2,1)} collective-permute-done((bf16[128,2176]{1,0:T(8,128)(2,1)}, bf16[128,2176]{1,0:T(8,128)(2,1)}, u32[]{:S(2)}, u32[]{:S(2)}) %collective-permute-start.27) | collective-permute-done | bytes 557088 | tf_op jit(solution)/shard_map/ppermute | solution.py:50
  78.5 11.8 %collective-permute-done.7 = bf16[64,2048]{1,0:T(8,128)(2,1)S(1)} collective-permute-done((bf16[64,2048]{1,0:T(8,128)(2,1)S(1)}, bf16[64,2048]{1,0:T(8,128)(2,1)S(1)}, u32[]{:S(2)}, u32[]{:S(2)}) %collective-permute-start.7) | collective-permute-done | bytes 262176 | tf_op jit(solution)/shard_map/ppermute | solution.py:50
  134.5 11.3 %collective-permute-done.9 = bf16[128,2048]{1,0:T(8,128)(2,1)S(1)} collective-permute-done((bf16[128,2048]{1,0:T(8,128)(2,1)S(1)}, bf16[128,2048]{1,0:T(8,128)(2,1)S(1)}, u32[]{:S(2)}, u32[]{:S(2)}) %collective-permute-start.9) | collective-permute-done | bytes 524320 | tf_op jit(solution)/shard_map/ppermute | solution.py:50
  148.1 9.9 %collective-permute-done.13 = bf16[128,2048]{1,0:T(8,128)(2,1)S(1)} collective-permute-done((bf16[128,2048]{1,0:T(8,128)(2,1)S(1)}, bf16[128,2048]{1,0:T(8,128)(2,1)S(1)}, u32[]{:S(2)}, u32[]{:S(2)}) %collective-permute-start.13) | collective-permute-done | bytes 524320 | tf_op jit(solution)/shard_map/ppermute | solution.py:50
  161.5 14.3 %collective-permute-done.14 = bf16[128,2048]{1,0:T(8,128)(2,1)S(1)} collective-permute-done((bf16[128,2048]{1,0:T(8,128)(2,1)S(1)}, bf16[128,2048]{1,0:T(8,128)(2,1)S(1)}, u32[]{:S(2)}, u32[]{:S(2)}) %collective-permute-start.14) | collective-permute-done | bytes 524320 | tf_op jit(solution)/shard_map/ppermute | solution.py:50
  190.4 10.1 %collective-permute-done.19 = bf16[128,2048]{1,0:T(8,128)(2,1)S(1)} collective-permute-done((bf16[128,2048]{1,0:T(8,128)(2,1)S(1)}, bf16[128,2048]{1,0:T(8,128)(2,1)S(1)}, u32[]{:S(2)}, u32[]{:S(2)}) %collective-permute-start.19) | collective-permute-done | bytes 524320 | tf_op jit(solution)/shard_map/ppermute | solution.py:50
  205.2 9.8 %collective-permute-done.20 = bf16[128,2048]{1,0:T(8,128)(2,1)S(1)} collective-permute-done((bf16[128,2048]{1,0:T(8,128)(2,1)S(1)}, bf16[128,2048]{1,0:T(8,128)(2,1)S(1)}, u32[]{:S(2)}, u32[]{:S(2)}) %collective-permute-start.20) | collective-permute-done | bytes 524320 | tf_op jit(solution)/shard_map/ppermute | solution.py:50
  231.7 12.3 %pad_maximum_fusion.w_ref = bf16[4,2,2,256,2048]{4,3,2,1,0:T(8,128)(2,1)} fusion(bf16[1,2,2,256,2048]{4,3,2,1,0:T(8,128)(2,1)S(1)} %bitcast.171, bf16[1,2,2,256,2048]{4,3,2,1,0:T(8,128)(2,1)} %bitcast.23, bf16[1,2,2,256,2048]{4,3,2,1,0:T(8,128)(2,1)} %bitcast.22, bf16[1,2,2,256,2048]{4,3,2,1,0:T(8,128)(2,1)} %bitcast.144), kind=kLoop, calls=%fused_computation | loop fusion | flops 25165824 | bytes 33554432 | tf_op jit(solution)/shard_map/stack | solution.py:367
  248.4 11.1 %fusion.89.h_ref = f32[1024,2048]{1,0:T(8,128)} fusion(bf16[1024,2048]{1,0:T(8,128)(2,1)S(1)} %slice_dynamic-update-slice_fusion, bf16[2048,2048]{1,0:T(8,128)(2,1)S(1)} %bitcast.161), kind=kOutput, calls=%fused_computation.282 | convolution fusion | flops 8589934592 | bytes 20971520 | tf_op jit(solution)/shard_map/dot_general | solution.py:28
  259.5 16.9 %shard_map.256 = (bf16[256,2048]{1,0:T(8,128)(2,1)S(1)}, bf16[1024,4096]{1,0:T(8,128)(2,1)}, bf16[1024,2048]{1,0:T(8,128)(2,1)}, bf16[256,128]{1,0:T(8,128)(2,1)S(1)}) custom-call(bf16[256,2048]{1,0:T(8,128)(2,1)S(1)} %pad_maximum_fusion.6.f_ref, f32[1024,2048]{1,0:T(8,128)} %fusion.89.h_ref, ...), custom_call_target="tpu_custom_call" | custom-call | flops 8589934592 | bytes 16777216 | tf_op jit(solution)/shard_map/pallas_call | solution.py:207
  276.5 16.9 %shard_map.257 = (bf16[256,2048]{1,0:T(8,128)(2,1)S(1)}, bf16[1024,4096]{1,0:T(8,128)(2,1)}, bf16[1024,2048]{1,0:T(8,128)(2,1)}, bf16[256,128]{1,0:T(8,128)(2,1)S(1)}) custom-call(bf16[256,2048]{1,0:T(8,128)(2,1)S(1)} %pad_maximum_fusion.5.f_ref, f32[1024,2048]{1,0:T(8,128)} %fusion.89.h_ref, ...), custom_call_target="tpu_custom_call", output_to_operand_aliasing={{1}: (6, {}), {2}: (7, {})} | custom-call | flops 8589934592 | bytes 16777216 | tf_op jit(solution)/shard_map/pallas_call | solution.py:207
  293.4 16.9 %shard_map.258 = (bf16[256,2048]{1,0:T(8,128)(2,1)S(1)}, bf16[1024,4096]{1,0:T(8,128)(2,1)}, bf16[1024,2048]{1,0:T(8,128)(2,1)}, bf16[256,128]{1,0:T(8,128)(2,1)S(1)}) custom-call(bf16[256,2048]{1,0:T(8,128)(2,1)S(1)} %pad_maximum_fusion.4.f_ref, f32[1024,2048]{1,0:T(8,128)} %fusion.89.h_ref, ...), custom_call_target="tpu_custom_call", output_to_operand_aliasing={{1}: (6, {}), {2}: (7, {})} | custom-call | flops 8589934592 | bytes 16777216 | tf_op jit(solution)/shard_map/pallas_call | solution.py:207
  310.5 17.1 %shard_map.259 = (bf16[256,2048]{1,0:T(8,128)(2,1)S(1)}, bf16[1024,4096]{1,0:T(8,128)(2,1)}, bf16[1024,2048]{1,0:T(8,128)(2,1)}, bf16[256,128]{1,0:T(8,128)(2,1)S(1)}) custom-call(bf16[256,2048]{1,0:T(8,128)(2,1)S(1)} %pad_maximum_fusion.3.f_ref, f32[1024,2048]{1,0:T(8,128)} %fusion.89.h_ref, ...), custom_call_target="tpu_custom_call", output_to_operand_aliasing={{1}: (6, {}), {2}: (7, {})} | custom-call | flops 8589934592 | bytes 16777216 | tf_op jit(solution)/shard_map/pallas_call | solution.py:207
  327.6 12.5 %convolution_convert_fusion = bf16[1024,2048]{1,0:T(8,128)(2,1)S(1)} fusion(bf16[1024,2048]{1,0:T(8,128)(2,1)} %get-tuple-element.38, bf16[2048,2048]{1,0:T(8,128)(2,1)} %bitcast.162), kind=kOutput, calls=%fused_computation.29 | convolution fusion | flops 8592031744 | bytes 16777216 | tf_op jit(solution)/shard_map/dot_general | solution.py:28
  358.2 8.9 %collective-permute-done.51 = bf16[128,2048]{1,0:T(8,128)(2,1)S(1)} collective-permute-done((bf16[128,2048]{1,0:T(8,128)(2,1)S(1)}, bf16[128,2048]{1,0:T(8,128)(2,1)S(1)}, u32[]{:S(2)}, u32[]{:S(2)}) %collective-permute-start.51) | collective-permute-done | bytes 524320 | tf_op jit(solution)/shard_map/ppermute | solution.py:50
  390.6 8.8 %convolution_convert_fusion.2 = bf16[1024,2048]{1,0:T(8,128)(2,1)} fusion(bf16[1024,2048]{1,0:T(8,128)(2,1)} %constant_dynamic-update-slice_fusion.28, bf16[1024,4096]{1,0:T(8,128)(2,1)S(1)} %bitcast.149), kind=kOutput, calls=%fused_computation.31 | convolution fusion | flops 4297064448 | bytes 10485760 | tf_op jit(solution)/shard_map/dot_general | solution.py:28
  460.0 10.2 %collective-permute-done.59 = bf16[128,2048]{1,0:T(8,128)(2,1)S(1)} collective-permute-done((bf16[128,2048]{1,0:T(8,128)(2,1)S(1)}, bf16[128,2048]{1,0:T(8,128)(2,1)S(1)}, u32[]{:S(2)}, u32[]{:S(2)}) %collective-permute-start.59) | collective-permute-done | bytes 524320 | tf_op jit(solution)/shard_map/ppermute | solution.py:50
  499.2 11.2 %fusion.3 = (f32[2048]{0:T(1024)S(1)}, bf16[1024,2048]{1,0:T(8,128)(2,1)S(1)}, f32[1024,2048]{1,0:T(8,128)}) fusion(bf16[1024,2048]{1,0:T(8,128)(2,1)} %copy-done.10, f32[1024]{0:T(1024)S(1)} %copy-done.45, bf16[3,1024,256]{1,2,0:T(8,128)(2,1)} %bitcast.181, bf16[3,2048,256]{1,2,0:T(8,128)(2,1)} %all-gather.3.cloned.1.call-done), kind=kOutput, calls=%fused_computation.6 | convolution fusion | flops 3231709184 | bytes 21508096 | tf_op jit(solution)/shard_map/ctf,cdf->td/dot_general | solution.py:464
  529.2 12.5 %add_convert_fusion = bf16[1024,2048]{1,0:T(8,128)(2,1)} fusion(bf16[1024,2048]{1,0:T(8,128)(2,1)} %collective-permute-done.80, bf16[1024,2048]{1,0:T(8,128)(2,1)} %constant_dynamic-update-slice_fusion.28, bf16[1024,4096]{1,0:T(8,128)(2,1)} %get-tuple-element.47), kind=kOutput, calls=%fused_computation.11 | convolution fusion | flops 4301258752 | bytes 14680064 | tf_op jit(solution)/shard_map/dot_general | solution.py:28
  557.4 12.7 %collective-permute-done.64 = bf16[128,2048]{1,0:T(8,128)(2,1)S(1)} collective-permute-done((bf16[128,2048]{1,0:T(8,128)(2,1)S(1)}, bf16[128,2048]{1,0:T(8,128)(2,1)S(1)}, u32[]{:S(2)}, u32[]{:S(2)}) %collective-permute-start.64) | collective-permute-done | bytes 524320 | tf_op jit(solution)/shard_map/ppermute | solution.py:50
  572.6 22.0 %collective-permute-done.84 = bf16[512,2048]{1,0:T(8,128)(2,1)S(1)} collective-permute-done((bf16[512,2048]{1,0:T(8,128)(2,1)}, bf16[512,2048]{1,0:T(8,128)(2,1)S(1)}, u32[]{:S(2)}, u32[]{:S(2)}) %collective-permute-start.84) | collective-permute-done | bytes 2097184 | tf_op jit(solution)/shard_map/ppermute | solution.py:105
  619.0 64.2 %collective-permute-done.81 = bf16[1024,2048]{1,0:T(8,128)(2,1)} collective-permute-done((bf16[1024,2048]{1,0:T(8,128)(2,1)}, bf16[1024,2048]{1,0:T(8,128)(2,1)}, u32[]{:S(2)}, u32[]{:S(2)}) %collective-permute-start.81) | collective-permute-done | bytes 4194336 | tf_op jit(solution)/shard_map/ppermute | solution.py:105
  683.2 10.7 %add_add_fusion = f32[1024,2048]{1,0:T(8,128)S(1)} fusion(bf16[1024,2048]{1,0:T(8,128)(2,1)} %collective-permute-done.82, bf16[1024,2048]{1,0:T(8,128)(2,1)} %collective-permute-done.81, bf16[1024,2048]{1,0:T(8,128)(2,1)} %constant_dynamic-update-slice_fusion.28, bf16[1024,4096]{1,0:T(8,128)(2,1)} %get-tuple-element.47), kind=kOutput, calls=%fused_computation.10 | convolution fusion | flops 4303355904 | bytes 23068672 | tf_op jit(solution)/shard_map/dot_general | solution.py:28
  694.0 9.9 %copy.128 = f32[2,2,256,2048]{3,1,0,2:T(2,128)} copy(f32[2,2,256,2048]{3,2,1,0:T(8,128)S(1)} %bitcast.164) | data formatting | bytes 16777216 | tf_op jit(solution)/shard_map/reshape | solution.py:436
  (468 shorter events, 345.6 us)
Async XLA Ops:
  7.3 86.0 %all-gather.3.cloned.1.call-start = ((), (), s32[]{:S(2)}) async-start(), calls=%async_computation.1 | async-start | bytes 3932160 | tf_op jit(solution)/shard_map/all_gather | solution.py:355
  9.7 109.3 %all-gather.5.cloned.1.call-start = ((), (), s32[]{:S(2)}) async-start(), calls=%async_computation.2 | async-start | bytes 1310720 | tf_op jit(solution)/shard_map/all_gather | solution.py:356
  14.8 24.9 %collective-permute-start.25 = (bf16[128,2176]{1,0:T(8,128)(2,1)S(1)}, bf16[128,2176]{1,0:T(8,128)(2,1)}, u32[]{:S(2)}, u32[]{:S(2)}) collective-permute-start(bf16[128,2176]{1,0:T(8,128)(2,1)S(1)} %pad_maximum_fusion.9), channel_id=1, source_target_pairs={{0,2},{2,4},{4,6},{6,7},{7,5},{5,3},{3,1},{1,0},{8,10},{10,12},{12... | collective-permute-start | bytes 1671176 | tf_op jit(solution)/shard_map/ppermute | solution.py:50
  16.9 23.5 %collective-permute-start.24 = (bf16[128,2176]{1,0:T(8,128)(2,1)S(1)}, bf16[128,2176]{1,0:T(8,128)(2,1)}, u32[]{:S(2)}, u32[]{:S(2)}) collective-permute-start(bf16[128,2176]{1,0:T(8,128)(2,1)S(1)} %pad_maximum_fusion.9), channel_id=1, source_target_pairs={{2,0},{4,2},{6,4},{7,6},{5,7},{3,5},{1,3},{0,1},{10,8},{12,10},{14... | collective-permute-start | bytes 1671176 | tf_op jit(solution)/shard_map/ppermute | solution.py:50
  16.9 686.9 %reduce-scatter.2.cloned.1.call-start = ((), (), s32[]{:S(2)}) async-start(), calls=%async_computation.3 | async-start | bytes 5242880 | tf_op jit(solution)/shard_map/reduce_scatter | solution.py:468
  32.6 145.5 %collective-permute-start.32 = (bf16[2,2,256,2048]{3,2,1,0:T(8,128)(2,1)}, bf16[2,2,256,2048]{3,2,1,0:T(8,128)(2,1)}, u32[]{:S(2)}, u32[]{:S(2)}) collective-permute-start(bf16[2,2,256,2048]{3,2,1,0:T(8,128)(2,1)} %bitcast.65.clone.2), channel_id=1, source_target_pairs={{16,0},{24,8},{0,16},{8,24},{17,1},{25,9},{1,17},{9,25},{18,2},{26... | collective-permute-start | bytes 12582920 | tf_op jit(solution)/shard_map/ppermute | solution.py:99
  63.2 167.9 %collective-permute-start.36 = (bf16[2,2,256,2048]{3,2,1,0:T(8,128)(2,1)}, bf16[2,2,256,2048]{3,2,1,0:T(8,128)(2,1)}, u32[]{:S(2)}, u32[]{:S(2)}) collective-permute-start(bf16[2,2,256,2048]{3,2,1,0:T(8,128)(2,1)} %bitcast.65.clone.2), channel_id=1, source_target_pairs={{0,8},{8,0},{16,24},{24,16},{1,9},{9,1},{17,25},{25,17},{2,10},{10... | collective-permute-start | bytes 12582920 | tf_op jit(solution)/shard_map/ppermute | solution.py:95
  63.2 69.7 %collective-permute-start.29 = (bf16[128,2176]{1,0:T(8,128)(2,1)}, bf16[128,2176]{1,0:T(8,128)(2,1)S(1)}, u32[]{:S(2)}, u32[]{:S(2)}) collective-permute-start(bf16[128,2176]{1,0:T(8,128)(2,1)} %collective-permute-done.27), channel_id=1, source_target_pairs={{0,2},{2,4},{4,6},{6,7},{7,5},{5,3},{3,1},{1,0},{8,10},{10,12},{12... | collective-permute-start | bytes 1671176 | tf_op jit(solution)/shard_map/ppermute | solution.py:50
  133.0 45.2 %collective-permute-start.31 = (bf16[64,2176]{1,0:T(8,128)(2,1)S(1)}, bf16[64,2176]{1,0:T(8,128)(2,1)S(1)}, u32[]{:S(2)}, u32[]{:S(2)}) collective-permute-start(bf16[64,2176]{1,0:T(8,128)(2,1)S(1)} %slice.498), channel_id=1, source_target_pairs={{0,2},{2,4},{4,6},{6,7},{7,5},{5,3},{3,1},{1,0},{8,10},{10,12},{12... | collective-permute-start | bytes 835592 | tf_op jit(solution)/shard_map/ppermute | solution.py:50
  178.1 53.6 %collective-permute-start.37 = (bf16[2,2,256,2048]{3,2,1,0:T(8,128)(2,1)}, bf16[2,2,256,2048]{3,2,1,0:T(8,128)(2,1)S(1)}, u32[]{:S(2)}, u32[]{:S(2)}) collective-permute-start(bf16[2,2,256,2048]{3,2,1,0:T(8,128)(2,1)} %collective-permute-done.32), channel_id=1, source_target_pairs={{0,8},{8,0},{16,24},{24,16},{1,9},{9,1},{17,25},{25,17},{2,10},{10... | collective-permute-start | bytes 12582920 | tf_op jit(solution)/shard_map/ppermute | solution.py:95
  179.1 48.1 %collective-permute-start.34 = (bf16[2,256,2048]{2,1,0:T(8,128)(2,1)S(1)}, bf16[2,256,2048]{2,1,0:T(8,128)(2,1)S(1)}, u32[]{:S(2)}, u32[]{:S(2)}) collective-permute-start(bf16[2,256,2048]{2,1,0:T(8,128)(2,1)S(1)} %bitcast.165), channel_id=1, source_target_pairs={{16,0},{24,8},{0,16},{8,24},{17,1},{25,9},{1,17},{9,25},{18,2},{26... | collective-permute-start | bytes 6291464 | tf_op jit(solution)/shard_map/ppermute | solution.py:99
  227.7 82.6 %collective-permute-start.22 = (bf16[64,2048]{1,0:T(8,128)(2,1)S(1)}, bf16[64,2048]{1,0:T(8,128)(2,1)S(1)}, u32[]{:S(2)}, u32[]{:S(2)}) collective-permute-start(bf16[64,2048]{1,0:T(8,128)(2,1)S(1)} %slice.488), channel_id=1, source_target_pairs={{2,0},{4,2},{6,4},{7,6},{5,7},{3,5},{1,3},{0,1},{10,8},{12,10},{14... | collective-permute-start | bytes 786440 | tf_op jit(solution)/shard_map/ppermute | solution.py:50
  231.1 79.2 %collective-permute-start.23 = (bf16[64,2048]{1,0:T(8,128)(2,1)S(1)}, bf16[64,2048]{1,0:T(8,128)(2,1)S(1)}, u32[]{:S(2)}, u32[]{:S(2)}) collective-permute-start(bf16[64,2048]{1,0:T(8,128)(2,1)S(1)} %slice.489), channel_id=1, source_target_pairs={{0,2},{2,4},{4,6},{6,7},{7,5},{5,3},{3,1},{1,0},{8,10},{10,12},{12... | collective-permute-start | bytes 786440 | tf_op jit(solution)/shard_map/ppermute | solution.py:50
  351.8 33.5 %collective-permute-start.47 = (bf16[128,2048]{1,0:T(8,128)(2,1)S(1)}, bf16[128,2048]{1,0:T(8,128)(2,1)S(1)}, u32[]{:S(2)}, u32[]{:S(2)}) collective-permute-start(bf16[128,2048]{1,0:T(8,128)(2,1)S(1)} %pad_maximum_fusion.16), channel_id=1, source_target_pairs={{0,2},{2,4},{4,6},{6,7},{7,5},{5,3},{3,1},{1,0},{8,10},{10,12},{12... | collective-permute-start | bytes 1572872 | tf_op jit(solution)/shard_map/ppermute | solution.py:50
  357.4 32.0 %collective-permute-start.43 = (bf16[128,2048]{1,0:T(8,128)(2,1)S(1)}, bf16[128,2048]{1,0:T(8,128)(2,1)S(1)}, u32[]{:S(2)}, u32[]{:S(2)}) collective-permute-start(bf16[128,2048]{1,0:T(8,128)(2,1)S(1)} %pad_maximum_fusion.15), channel_id=1, source_target_pairs={{2,0},{4,2},{6,4},{7,6},{5,7},{3,5},{1,3},{0,1},{10,8},{12,10},{14... | collective-permute-start | bytes 1572872 | tf_op jit(solution)/shard_map/ppermute | solution.py:50
  406.5 30.2 %collective-permute-start.83 = (bf16[512,2048]{1,0:T(8,128)(2,1)S(1)}, bf16[512,2048]{1,0:T(8,128)(2,1)S(1)}, u32[]{:S(2)}, u32[]{:S(2)}) collective-permute-start(bf16[512,2048]{1,0:T(8,128)(2,1)S(1)} %convolution_convert_fusion.5), channel_id=1, source_target_pairs={{0,8},{8,0},{16,24},{24,16},{1,9},{9,1},{17,25},{25,17},{2,10},{10... | collective-permute-start | bytes 6291464 | tf_op jit(solution)/shard_map/ppermute | solution.py:95
  435.4 135.4 %collective-permute-start.85 = (bf16[512,2048]{1,0:T(8,128)(2,1)}, bf16[512,2048]{1,0:T(8,128)(2,1)}, u32[]{:S(2)}, u32[]{:S(2)}) collective-permute-start(bf16[512,2048]{1,0:T(8,128)(2,1)} %convolution_convert_fusion.4), channel_id=1, source_target_pairs={{0,8},{8,0},{16,24},{24,16},{1,9},{9,1},{17,25},{25,17},{2,10},{10... | collective-permute-start | bytes 6291464 | tf_op jit(solution)/shard_map/ppermute | solution.py:95
  436.7 91.7 %collective-permute-start.80 = (bf16[1024,2048]{1,0:T(8,128)(2,1)}, bf16[1024,2048]{1,0:T(8,128)(2,1)}, u32[]{:S(2)}, u32[]{:S(2)}) collective-permute-start(bf16[1024,2048]{1,0:T(8,128)(2,1)} %convolution_convert_fusion.2), channel_id=1, source_target_pairs={{0,8},{8,0},{16,24},{24,16},{1,9},{9,1},{17,25},{25,17},{2,10},{10... | collective-permute-start | bytes 12582920 | tf_op jit(solution)/shard_map/ppermute | solution.py:95
  523.3 71.3 %collective-permute-start.84 = (bf16[512,2048]{1,0:T(8,128)(2,1)}, bf16[512,2048]{1,0:T(8,128)(2,1)S(1)}, u32[]{:S(2)}, u32[]{:S(2)}) collective-permute-start(bf16[512,2048]{1,0:T(8,128)(2,1)} %add_convert_fusion.1), channel_id=1, source_target_pairs={{0,16},{8,24},{16,0},{24,8},{1,17},{9,25},{17,1},{25,9},{2,18},{10... | collective-permute-start | bytes 6291464 | tf_op jit(solution)/shard_map/ppermute | solution.py:105
  526.7 29.3 %collective-permute-start.67 = (bf16[128,2048]{1,0:T(8,128)(2,1)S(1)}, bf16[128,2048]{1,0:T(8,128)(2,1)S(1)}, u32[]{:S(2)}, u32[]{:S(2)}) collective-permute-start(bf16[128,2048]{1,0:T(8,128)(2,1)S(1)} %pad_maximum_fusion.19), channel_id=1, source_target_pairs={{2,0},{4,2},{6,4},{7,6},{5,7},{3,5},{1,3},{0,1},{10,8},{12,10},{14... | collective-permute-start | bytes 1572872 | tf_op jit(solution)/shard_map/ppermute | solution.py:50
  552.5 66.4 %collective-permute-start.82 = (bf16[1024,2048]{1,0:T(8,128)(2,1)}, bf16[1024,2048]{1,0:T(8,128)(2,1)}, u32[]{:S(2)}, u32[]{:S(2)}) collective-permute-start(bf16[1024,2048]{1,0:T(8,128)(2,1)} %convolution_convert_fusion.1), channel_id=1, source_target_pairs={{0,8},{8,0},{16,24},{24,16},{1,9},{9,1},{17,25},{25,17},{2,10},{10... | collective-permute-start | bytes 12582920 | tf_op jit(solution)/shard_map/ppermute | solution.py:95
  552.5 130.7 %collective-permute-start.81 = (bf16[1024,2048]{1,0:T(8,128)(2,1)}, bf16[1024,2048]{1,0:T(8,128)(2,1)}, u32[]{:S(2)}, u32[]{:S(2)}) collective-permute-start(bf16[1024,2048]{1,0:T(8,128)(2,1)} %add_convert_fusion), channel_id=1, source_target_pairs={{0,16},{8,24},{16,0},{24,8},{1,17},{9,25},{17,1},{25,9},{2,18},{10... | collective-permute-start | bytes 12582920 | tf_op jit(solution)/shard_map/ppermute | solution.py:105
  570.1 34.5 %collective-permute-start.74 = (f32[19,128]{1,0:T(8,128)S(1)}, f32[19,128]{1,0:T(8,128)S(1)}, u32[]{:S(2)}, u32[]{:S(2)}) collective-permute-start(f32[19,128]{1,0:T(8,128)S(1)} %add.334), channel_id=1, source_target_pairs={{0,4},{1,5},{2,6},{3,7},{4,0},{5,1},{6,2},{7,3},{8,12},{9,13},{10,... | collective-permute-start | bytes 29192 | tf_op jit(solution)/shard_map/ppermute | solution.py:243
  570.8 35.1 %collective-permute-start.68 = (bf16[128,2048]{1,0:T(8,128)(2,1)S(1)}, bf16[128,2048]{1,0:T(8,128)(2,1)S(1)}, u32[]{:S(2)}, u32[]{:S(2)}) collective-permute-start(bf16[128,2048]{1,0:T(8,128)(2,1)S(1)} %get-tuple-element.109), channel_id=1, source_target_pairs={{2,0},{4,2},{6,4},{7,6},{5,7},{3,5},{1,3},{0,1},{10,8},{12,10},{14... | collective-permute-start | bytes 1572872 | tf_op jit(solution)/shard_map/ppermute | solution.py:50
  (123 other events, 1800.4 us)
Sparse Core Ops, SparseCore 0:
  9.8 35.9 all-gather.2
  47.4 23.2 all-gather.4
  523.4 65.5 reduce-scatter.1

commit v2 on v1

--- a/solution.py
+++ b/solution.py
@@ -49,33 +49,45 @@
     def send(self, x, way):
         return lax.ppermute(x, "expert", way)
 
-    def gather(self, own):
+    def gather(self, own, arrived=None, first=None, lag=2):
         n = self.count
         half = own.shape[0] // 2
         slots = [None] * n
         slots[0] = own
         ahead = behind = own
-        for s in range(1, n // 2):
+        given = {}
+        for s in range(1, n // 2 + 1):
+            for done in [given.get(s - lag), first if s == 2 else None]:
+                if done is not None:
+                    ahead, behind = tie(ahead, done), tie(behind, done)
+            if s == n // 2:
+                break
             ahead = self.send(ahead, self.down)
             behind = self.send(behind, self.up)
             slots[s] = ahead
             slots[n - s] = behind
+            if arrived is not None and s <= n // 2 - 2:
+                given[s] = arrived(s, slots)
         slots[n // 2] = jnp.concatenate(
             [self.send(ahead[:half], self.down), self.send(behind[half:], self.up)], axis=0
         )
         return slots
 
-    def reduce(self, parts):
+    def reduce(self, parts, sent=None, last=()):
         n = self.count
         far = parts[n // 2]
         half = far.shape[0] // 2
         fwd, back = far[:half].astype(bf16), far[half:].astype(bf16)
+        wait = None
         for s in range(n // 2 - 1, -1, -1):
             fwd = self.send(fwd, self.up)
             back = self.send(back, self.down)
             if s == 0:
                 break
             a, b = parts[s].astype(f32), parts[n - s].astype(f32)
+            if wait is not None:
+                a = tie(a, wait)
+            wait = None
             if s == n // 2 - 1:
                 fwd = jnp.concatenate([a[:half] + fwd.astype(f32), a[half:]], axis=0)
                 back = jnp.concatenate([b[:half], b[half:] + back.astype(f32)], axis=0)
@@ -83,12 +95,24 @@
                 fwd = a + fwd.astype(f32)
                 back = b + back.astype(f32)
             fwd, back = fwd.astype(bf16), back.astype(bf16)
-        return parts[0].astype(f32) + fwd.astype(f32) + back.astype(f32)
+            wait = sent(s, back) if sent is not None else None
+        total = parts[0].astype(f32)
+        for ahead_of in (wait, *last):
+            if ahead_of is not None:
+                total = tie(total, ahead_of)
+        return total + fwd.astype(f32) + back.astype(f32)
 
 
 class Chips:
     def __init__(self, count):
         self.steps = count // 2
+        me = lax.axis_index("dp")
+        self.places = jnp.stack(
+            [
+                ((me // 2 + b // 2) % self.steps) * 2 + (me % 2 + b % 2) % 2
+                for b in range(count)
+            ]
+        ).astype(jnp.int32)
         self.swap = [(i, i ^ 1) for i in range(count)]
 
     def other_core(self, x):
@@ -106,40 +130,59 @@
             x, "dp", [(i, ((i // 2 + step) % n) * 2 + i % 2) for i in range(2 * n)]
         )
 
-    def gather(self, own):
-        blocks = []
-        for step in range(self.steps):
-            block = own if step == 0 else self.from_ahead(own, step)
-            blocks += [block, self.other_core(block)]
-        return blocks
-
-    def reduce(self, term):
-        total = None
-        for step in range(self.steps - 1, -1, -1):
-            theirs = self.other_core(term(2 * step + 1).astype(bf16)).astype(f32)
-            mine = term(2 * step) + theirs
-            if step:
-                mine = self.to_ahead(mine.astype(bf16), step).astype(f32)
-            total = mine if total is None else total + mine
-        return total
+    def first_half(self, own):
+        ahead = [self.from_ahead(own, step) for step in range(1, self.steps)]
+        return [own, self.other_core(own), *ahead]
+
+    def second_half(self, blocks, wait):
+        out = blocks[:2]
+        for block in blocks[2:]:
+            block = tie(block, wait)
+            out += [block, self.other_core(block)]
+        return out
+
+
+def block_at(step, steps, experts_dev):
+    block = step // experts_dev
+    half = steps // experts_dev // 2
+    return 2 * (block % half) + block // half
 
 
 def expert_kernel(
     steps,
     num_experts,
+    places,
     f_ref,
     h_ref,
     mask_ref,
     sel_ref,
     wr_ref,
-    w_ref,
     *refs,
 ):
-    gc_ref, gp_ref, ga_ref, gl_ref, acc, router, gate_sums = refs[-7:]
+    w_refs = refs[: steps // sel_ref.shape[0]]
+    gc_ref, gp_ref, ga_ref, gl_ref, acc, router, gate_sums, held, sems = refs[-9:]
     step = pl.program_id(0)
     experts_dev = sel_ref.shape[0]
-    ff_tile = w_ref.shape[3]
+    ff_tile = h_ref.shape[1]
     rows_in = f_ref[...]
+    now = lax.rem(step, 2)
+
+    def fetch(target):
+        for j in range(steps):
+
+            @pl.when(target == j)
+            def _():
+                pltpu.make_async_copy(
+                    w_refs[block_at(j, steps, experts_dev)].at[j % experts_dev],
+                    held.at[j % 2],
+                    sems.at[j % 2],
+                ).start()
+
+    @pl.when(step == 0)
+    def _():
+        fetch(step)
+
+    fetch(step + 1)
 
     @pl.when(step == 0)
     def _():
@@ -153,7 +196,8 @@
 
     lanes = sel_ref[pl.ds(step % experts_dev, 1), :] * mask_ref[...].astype(f32)
     gate = jnp.sum(router[...] * lanes, axis=-1, keepdims=True)
-    weight_gate, weight_up = w_ref[0, 0, 0], w_ref[0, 0, 1]
+    pltpu.make_async_copy(w_refs[0].at[0], held.at[now], sems.at[now]).wait()
+    weight_gate, weight_up = held[now, 0], held[now, 1]
     gate_pre = dot(rows_in, weight_gate, ((1,), (1,)))
     up_pre = dot(rows_in, weight_up, ((1,), (1,)))
     back_hidden = h_ref[...]
@@ -182,57 +226,150 @@
         gc_ref[...] = total.astype(bf16)
 
 
-def expert_chunk(index, chunks, num_experts, f, hidden, mask, select, router, weights, kept):
-    blocks, experts_dev, _, ff_tile, width = weights.shape
-    steps = blocks * experts_dev
+def expert_chunk(
+    index, chunks, num_experts, places, f, hidden, mask, select, router, weights, kept
+):
+    experts_dev, _, ff_tile, width = weights[0].shape
+    steps = len(weights) * experts_dev
     rows = f.shape[0]
     whole = pl.BlockSpec(memory_space=pltpu.VMEM)
+    apart = pl.BlockSpec(memory_space=pl.ANY)
+
+    def placed(j, places):
+        return (index, places[block_at(j, steps, experts_dev)] * experts_dev + j % experts_dev)
+
     in_specs = [
         whole,
-        pl.BlockSpec((rows, ff_tile), lambda j: (index, j)),
-        pl.BlockSpec((rows, 128), lambda j: (index, 0)),
+        pl.BlockSpec((rows, ff_tile), placed),
+        pl.BlockSpec((rows, 128), lambda j, places: (index, 0)),
         whole,
         whole,
-        pl.BlockSpec(
-            (1, 1, 2, ff_tile, width), lambda j: (j // experts_dev, j % experts_dev, 0, 0, 0)
-        ),
-    ]
-    args = [f, hidden, mask, select, router, weights]
+    ] + [apart] * len(weights)
+    args = [places, f, hidden, mask, select, router, *weights]
     aliases = {}
     if kept is not None:
-        in_specs += [pl.BlockSpec(memory_space=pl.ANY)] * 2
-        aliases = {len(args): 1, len(args) + 1: 2}
+        in_specs += [apart] * 2
+        aliases = {len(args) + i: 1 + i for i in range(2)}
         args += list(kept)
     total = rows * chunks
     return pl.pallas_call(
         functools.partial(expert_kernel, steps, num_experts),
-        grid=(steps,),
-        in_specs=in_specs,
-        out_specs=[
-            pl.BlockSpec((rows, width), lambda j: (0, 0)),
-            pl.BlockSpec((rows, 2 * ff_tile), lambda j: (index, j)),
-            pl.BlockSpec((rows, ff_tile), lambda j: (index, j)),
-            pl.BlockSpec((rows, 128), lambda j: (0, 0)),
-        ],
+        grid_spec=pltpu.PrefetchScalarGridSpec(
+            num_scalar_prefetch=1,
+            grid=(steps,),
+            in_specs=in_specs,
+            out_specs=[
+                pl.BlockSpec((rows, width), lambda j, places: (0, 0)),
+                pl.BlockSpec((rows, 2 * ff_tile), lambda j, places: (index, j)),
+                pl.BlockSpec((rows, ff_tile), placed),
+                pl.BlockSpec((rows, 128), lambda j, places: (0, 0)),
+            ],
+            scratch_shapes=[
+                pltpu.VMEM((rows, width), f32),
+                pltpu.VMEM((rows, 128), f32),
+                pltpu.VMEM((rows, 128), f32),
+                pltpu.VMEM((2, 2, ff_tile, width), bf16),
+                pltpu.SemaphoreType.DMA((2,)),
+            ],
+        ),
         out_shape=[
             jax.ShapeDtypeStruct((rows, width), bf16),
             jax.ShapeDtypeStruct((total, 2 * ff_tile * steps), bf16),
             jax.ShapeDtypeStruct((total, ff_tile * steps), bf16),
             jax.ShapeDtypeStruct((rows, 128), bf16),
         ],
-        scratch_shapes=[
-            pltpu.VMEM((rows, width), f32),
-            pltpu.VMEM((rows, 128), f32),
-            pltpu.VMEM((rows, 128), f32),
-        ],
         input_output_aliases=aliases,
-        compiler_params=pltpu.CompilerParams(vmem_limit_bytes=48 << 20),
+        compiler_params=pltpu.CompilerParams(vmem_limit_bytes=40 << 20),
         cost_estimate=pl.CostEstimate(
             flops=8 * rows * ff_tile * steps * width,
             bytes_accessed=4 * ff_tile * steps * width,
             transcendentals=0,
         ),
     )(*args)
+
+
+def product_kernel(a_ref, b_ref, _, o_ref):
+    o_ref[...] = jnp.dot(a_ref[...], b_ref[...], preferred_element_type=f32).astype(bf16)
+
+
+def product(a, b, wait):
+    rows, depth = a.shape
+    width = b.shape[1]
+    tile = min(512, rows)
+    return pl.pallas_call(
+        product_kernel,
+        grid=(rows // tile,),
+        in_specs=[
+            pl.BlockSpec((tile, depth), lambda i: (i, 0)),
+            pl.BlockSpec(memory_space=pltpu.VMEM),
+            pl.BlockSpec(memory_space=pl.ANY),
+        ],
+        out_specs=pl.BlockSpec((tile, width), lambda i: (i, 0)),
+        out_shape=jax.ShapeDtypeStruct((rows, width), bf16),
+        compiler_params=pltpu.CompilerParams(vmem_limit_bytes=40 << 20),
+        cost_estimate=pl.CostEstimate(
+            flops=2 * rows * depth * width, bytes_accessed=4 * rows * depth, transcendentals=0
+        ),
+    )(a, b, wait)
+
+
+def pair_kernel(first, block, a_ref, ap_ref, b_ref, bp_ref, x_ref, xp_ref, y_ref, yp_ref, _, o_ref):
+    def product(own, peer, rows, rows_peer):
+        total = dot(own[...], rows[...], ((0,), (0,))) + dot(peer[...], rows_peer[...], ((0,), (0,)))
+        o_ref[...] = total.astype(o_ref.dtype)
+
+    @pl.when(pl.program_id(0) < first)
+    def _():
+        product(a_ref, ap_ref, x_ref, xp_ref)
+
+    @pl.when(pl.program_id(0) >= first)
+    def _():
+        product(b_ref, bp_ref, y_ref, yp_ref)
+
+
+def pair_grad(
+    step, block, a, peer, a_cols, x, x_peer, b, b_first, b_cols, y, y_peer, wait, dtype
+):
+    rows, width = x.shape
+    tile = min(256, b_cols)
+    first, second = a_cols // tile, b_cols // tile
+    whole = pl.BlockSpec(memory_space=pltpu.VMEM)
+
+    def a_at(j, block):
+        return (0, step * first + jnp.minimum(j, first - 1))
+
+    def b_at(j, block):
+        return (0, block[0] * second + jnp.maximum(j - first, 0))
+
+    def bp_at(j, block):
+        return (0, (b_first + step) * second + jnp.maximum(j - first, 0))
+
+    return pl.pallas_call(
+        functools.partial(pair_kernel, first),
+        grid_spec=pltpu.PrefetchScalarGridSpec(
+            num_scalar_prefetch=1,
+            grid=(first + second,),
+            in_specs=[
+                pl.BlockSpec((rows, tile), a_at),
+                pl.BlockSpec((rows, tile), a_at),
+                pl.BlockSpec((rows, tile), b_at),
+                pl.BlockSpec((rows, tile), bp_at),
+                whole,
+                whole,
+                whole,
+                whole,
+                pl.BlockSpec(memory_space=pl.ANY),
+            ],
+            out_specs=pl.BlockSpec((tile, width), lambda j, block: (j, 0)),
+        ),
+        out_shape=jax.ShapeDtypeStruct((a_cols + b_cols, width), dtype),
+        compiler_params=pltpu.CompilerParams(vmem_limit_bytes=44 << 20),
+        cost_estimate=pl.CostEstimate(
+            flops=4 * rows * (a_cols + b_cols) * width,
+            bytes_accessed=16 * rows * width,
+            transcendentals=0,
+        ),
+    )(block, a, peer, b, peer, x, x_peer, y, y_peer, wait)
 
 
 def all_sum(x):
@@ -253,8 +390,9 @@
     return jnp.concatenate([slots[k] for k in slot_order(len(slots))], axis=0)
 
 
-def after(x, *others):
-    return lax.optimization_barrier((x, *others))[0]
+def tie(x, other):
+    probe = other[(0,) * other.ndim]
+    return x + jnp.where(probe == probe, 0.0, 1.0).astype(x.dtype)
 
 
 def rms_scale(values):
@@ -363,18 +501,19 @@
     attn_normed = states_all * attn_scale
     features = (attn_normed * attn_gain).astype(bf16)
 
-    gu_blocks = chips.gather(after(expert_gate_up, states_slots[1]).transpose(1, 2, 0, 3))
-    gu_all = jnp.stack(gu_blocks)
-    down_blocks = chips.gather(after(expert_down, gu_blocks[2]).transpose(1, 0, 2))
-    down_all = jnp.stack(down_blocks).reshape(experts_dev * ff, width)
+    down_all = lax.all_gather(expert_down.transpose(1, 0, 2), "dp", axis=0)
+    down_all = down_all.reshape(n_dp * experts_dev * ff_dev, width)
+    gu_blocks = chips.first_half(expert_gate_up.transpose(1, 2, 0, 3))
 
     expert_ids = jnp.arange(num_experts, dtype=jnp.int32)
     chosen = jnp.any(expert_routes[:, :, None] == expert_ids[None, None, :], axis=1)
     chosen = jnp.pad(chosen.astype(bf16), ((0, 0), (0, 128 - num_experts)))
     sent_grad = jnp.concatenate([out_grad, chosen], axis=1)
-    grad_slots = ring.gather(after(sent_grad, states_slots[n_exp // 2]))
+    sent_grad = tie(sent_grad, states_slots[n_exp // 2])
+    grad_slots = ring.gather(sent_grad)
     grad_top_all = in_order([g[:, :width] for g in grad_slots])
     chosen_all = in_order([g[:, width:] for g in grad_slots])
+    back_hidden = dot(grad_top_all, down_all, ((1,), (1,)))
 
     place = (ring.members[:, None] * tok_rows + jnp.arange(tok_rows, dtype=jnp.int32)).reshape(-1)
     segment, position = seq_layout(seq_lengths[0], seq_order[0], place)
@@ -384,11 +523,13 @@
     head_proj = projected.reshape(3, rows, heads, head_dim).transpose(0, 2, 1, 3)
     query_scale, key_scale = rms_scale(head_proj[0]), rms_scale(head_proj[1])
     query_normed, key_normed = head_proj[0] * query_scale, head_proj[1] * key_scale
-    query = rotate(query_normed * query_gain, cos_rows, sin_rows).astype(bf16)
+    query = rotate(query_normed * query_gain, cos_rows, sin_rows)
+    query = tie(query, grad_slots[1]).astype(bf16)
     key = rotate(key_normed * key_gain, cos_rows, sin_rows).astype(bf16)
     value = head_proj[2].astype(bf16)
     attended, log_sums = attend(query, key, value, segment, scaling)
-    attended = attended.transpose(1, 0, 2).reshape(rows, local_width).astype(bf16)
+    attended = attended.transpose(1, 0, 2).reshape(rows, local_width)
+    attended = tie(attended, grad_slots[2]).astype(bf16)
     branch_part = dot(attended, out_full, ((1,), (1,)))
 
     def slots_of(x):
@@ -401,47 +542,109 @@
     ffn_scale = rms_scale(mixed)
     ffn_normed = mixed * ffn_scale
     ffn_in = (ffn_normed * ffn_gain).astype(bf16)
-    ffn_slots = ring.gather(ffn_in)
-    ffn_all = in_order(ffn_slots)
-
-    back_hidden = dot(grad_top_all, down_all, ((1,), (1,)))
+    gu_blocks = chips.second_half(gu_blocks, ffn_in)
+
     router_wide = jnp.pad(router_weight, ((0, 0), (0, 128 - num_experts)))
     lanes = jnp.arange(128, dtype=jnp.int32)
     own_ids = ring.me * experts_dev + jnp.arange(experts_dev, dtype=jnp.int32)
     select = (lanes[None, :] == own_ids[:, None]).astype(f32)
-    kept = None
+    chunks = n_exp // 2
     grad_ffn_parts = [None] * n_exp
-    logit_chunks = []
-    chunks = n_exp // 2
-    for i in range(chunks):
+    logit_chunks = [None] * chunks
+    kept = [None]
+
+    def run_chunk(i, slots):
         a, b = (n_exp - i) % n_exp, i + 1
-        chunk = jnp.concatenate([ffn_slots[a], ffn_slots[b]], axis=0)
-        grad_chunk, grad_pre, gated_act, logit_low = expert_chunk(
-            i, chunks, num_experts, chunk, back_hidden, chosen_all, select, router_wide, gu_all, kept
+        chunk = jnp.concatenate([slots[a], slots[b]], axis=0)
+        grad_chunk, *kept_now, logit_chunks[i] = expert_chunk(
+            i,
+            chunks,
+            num_experts,
+            chips.places,
+            chunk,
+            back_hidden,
+            chosen_all,
+            select,
+            router_wide,
+            gu_blocks,
+            kept[0],
         )
-        kept = (grad_pre, gated_act)
+        kept[0] = tuple(kept_now)
         grad_ffn_parts[a], grad_ffn_parts[b] = grad_chunk[:tok_rows], grad_chunk[tok_rows:]
-        logit_chunks.append(logit_low)
+        return logit_chunks[i]
+
+    ffn_slots = ring.gather(ffn_in, lambda s, slots: run_chunk(s - 1, slots), back_hidden, 3)
+    run_chunk(chunks - 1, ffn_slots)
+    run_chunk(chunks - 2, ffn_slots)
+    ffn_all = in_order(ffn_slots)
+    grad_pre, gated_act = kept[0]
     logit_low = jnp.concatenate(logit_chunks, axis=0)
     router_part = dot(ffn_all, logit_low, ((0,), (0,)))[:, :num_experts]
-    grad_ffn = ring.reduce(grad_ffn_parts)
-    moe_part = dot(gated_act, down_all, ((1,), (0,)))
-
+
+    steps = n_dp // 2
     gu_cols, down_cols = experts_dev * 2 * ff_dev, experts_dev * ff_dev
-    down_grad = chips.reduce(
-        lambda b: dot(gated_act[:, b * down_cols : (b + 1) * down_cols], grad_top_all, ((0,), (0,)))
-    ).reshape(experts_dev, ff_dev, width)
-    gate_up_grad = chips.reduce(
-        lambda b: dot(grad_pre[:, b * gu_cols : (b + 1) * gu_cols], ffn_all, ((0,), (0,)))
-    ).reshape(experts_dev, 2, ff_dev, width)
+    ffn_peer, grad_peer = chips.other_core(ffn_all), chips.other_core(grad_top_all)
+    pre_away = [
+        grad_pre[:, (steps + s) * gu_cols : (steps + s + 1) * gu_cols] for s in range(steps)
+    ]
+    act_away = [
+        lax.dynamic_slice_in_dim(gated_act, chips.places[2 * s + 1] * down_cols, down_cols, 1)
+        for s in range(steps)
+    ]
+    away_peer = chips.other_core(jnp.concatenate(pre_away + act_away, axis=1))
+    terms = [None] * steps
+    jobs = list(range(steps - 1, -1, -1))
+
+    def next_term(wait):
+        if not jobs:
+            return None
+        s = jobs.pop(0)
+        terms[s] = pair_grad(
+            s,
+            chips.places[2 * s : 2 * s + 1],
+            grad_pre,
+            away_peer,
+            gu_cols,
+            ffn_all,
+            ffn_peer,
+            gated_act,
+            steps * gu_cols // down_cols,
+            down_cols,
+            grad_top_all,
+            grad_peer,
+            wait,
+            bf16,
+        )
+        return terms[s]
+
+    grad_ffn = ring.reduce(
+        grad_ffn_parts, lambda s, x: next_term(x) if s == 2 else None
+    )
 
     grad_top = out_grad.astype(f32)
     ffn_gain_part = jnp.sum(ffn_normed * grad_ffn, axis=0)
     grad_mixed = grad_top + norm_back(grad_ffn, ffn_gain, ffn_normed, ffn_scale)
-    branch_slots = ring.gather(grad_mixed.astype(bf16))
+    moe_made = []
+
+    def in_gather(s, slots):
+        if s == 1:
+            moe_made.append(product(gated_act, down_all, slots[1]))
+            return moe_made[0]
+        return next_term(slots[s])
+
+    branch_slots = ring.gather(
+        grad_mixed.astype(bf16), in_gather
+    )
+    while jobs:
+        next_term(branch_slots[n_exp // 2])
+    weight_grads = terms[0].astype(f32)
+    for s in range(1, steps):
+        weight_grads = weight_grads + chips.to_ahead(terms[s], s).astype(f32)
     grad_rows = in_order(branch_slots)
-    moe_part = after(moe_part.astype(bf16), branch_slots[n_exp // 2])
-    moe = ring.reduce(slots_of(moe_part))
+    moe_parts = slots_of(moe_made[0])
+    moe_parts[n_exp // 2] = tie(moe_parts[n_exp // 2], branch_slots[n_exp // 2])
+    moe_steps = {}
+    moe = ring.reduce(moe_parts, moe_steps.__setitem__)
     output = mixed + moe
 
     grad_attended = dot(grad_rows, out_full, ((1,), (0,))).astype(bf16)
@@ -451,6 +654,7 @@
     )
     grad_query = rotate_back(grad_query, cos_rows, sin_rows)
     grad_key = rotate_back(grad_key, cos_rows, sin_rows)
+    grad_query = tie(grad_query, moe_steps[1])
     query_gain_part = jnp.sum(query_normed * grad_query, axis=(0, 1))
     key_gain_part = jnp.sum(key_normed * grad_key, axis=(0, 1))
     grad_query = norm_back(grad_query, query_gain, query_normed, query_scale)
@@ -462,7 +666,16 @@
         .reshape(3, rows, local_width)
     )
     features_part = jnp.einsum("ctf,cdf->td", grad_proj, qkv_full, preferred_element_type=f32)
-    grad_features = ring.reduce(slots_of(features_part))
+    attn_gain_part = jnp.sum(attn_normed * features_part, axis=0)
+    squares = jnp.stack([jnp.sum(output * output), jnp.sum(branch * branch), jnp.sum(moe * moe)])
+    wide = all_sum(jnp.concatenate([router_part.T, ffn_gain_part[None]], axis=0))
+    small = all_sum(
+        jnp.concatenate(
+            [attn_gain_part, query_gain_part, key_gain_part, jnp.pad(squares, (0, 125))]
+        ).reshape(-1, 128)
+    ).reshape(-1)
+    ends = {2: weight_grads, 1: wide}
+    grad_features = ring.reduce(slots_of(features_part), lambda s, x: ends.get(s), (small,))
     qkv_term = jnp.einsum("td,ctf->cdf", features, grad_proj, preferred_element_type=f32)
     out_term = dot(grad_rows, attended, ((0,), (0,)))
     attn_sums = lax.psum_scatter(
@@ -471,17 +684,9 @@
         scatter_dimension=1,
         tiled=True,
     ).astype(f32)
-    attn_gain_part = jnp.sum(attn_normed * features_part, axis=0)
     own_scale = rms_scale(states)
     input_grad = grad_mixed + norm_back(grad_features, attn_gain, states * own_scale, own_scale)
 
-    squares = jnp.stack([jnp.sum(output * output), jnp.sum(branch * branch), jnp.sum(moe * moe)])
-    wide = all_sum(jnp.concatenate([router_part.T, ffn_gain_part[None]], axis=0))
-    small = all_sum(
-        jnp.concatenate(
-            [attn_gain_part, query_gain_part, key_gain_part, jnp.pad(squares, (0, 125))]
-        ).reshape(-1, 128)
-    ).reshape(-1)
     stream_rms = jnp.sqrt(small[width + 2 * head_dim :][:3] / (rows * n_dp * width))
     return (
         output.astype(bf16),
@@ -493,8 +698,8 @@
         small[width + head_dim : width + 2 * head_dim],
         wide[num_experts],
         wide[:num_experts].T,
-        gate_up_grad.transpose(2, 0, 1, 3),
-        down_grad.transpose(1, 0, 2),
+        weight_grads[:gu_cols].reshape(experts_dev, 2, ff_dev, width).transpose(2, 0, 1, 3),
+        weight_grads[gu_cols:].reshape(experts_dev, ff_dev, width).transpose(1, 0, 2),
         stream_rms,
     )
 

time: 722 us -> 687 us (0.952)
  waiting for transfers between devices: 296 us -> 200 us
  matrix products: 122 us -> 61.5 us
  Pallas kernels: 68 us -> 126 us
  other arithmetic: 53.7 us -> 78 us
  local copies, waits for them, and re-layouts: 67.2 us -> 88 us
  between operations: 15.7 us -> 34.4 us
    ppermute x2 -> x1, waiting for transfers between devices: 86.2 us -> 0.01 us  [to_ahead(): lax.ppermute(x, 'dp', [(i, (i // 2 + step) % n * 2 + i % 2) for i in rang...]
    dot_general x14 -> x5, matrix products: 86.8 us -> 24.2 us  [dot(): return lax.dot_general(a, b, (dims, ((), ())), preferred_element_type=f32)]
    pallas_call x0 -> x3, Pallas kernels: none -> 53.9 us  [the longest x2 41.5 us: pair_grad(): pl.pallas_call(functools.partial(pair_kernel, first), grid_spec=pltpu.Pre...]
    add x0 -> x9, other arithmetic: none -> 17.8 us  [the longest x1 12.2 us: on_device(): weight_grads = weight_grads + chips.to_ahead(terms[s], s).astype(f32)]
    slice x0 -> x19, local copies, waits for them, and re-layouts: none -> 15.5 us  [the longest x14 9.36 us: tie(): probe = other[(0,) * other.ndim]]
    another operation x9 -> x8, other arithmetic: 18 us -> 3.43 us  [the longest x1 12.3 us: on_device(): gu_all = jnp.stack(gu_blocks)]
    ppermute x64, waiting for transfers between devices: 193 us -> 181 us  [send(): return lax.ppermute(x, 'expert', way)]
    unnamed x157 -> x179, local copies, waits for them, and re-layouts: 34.6 us -> 45.8 us
  transfers between devices with their start and end apart: 89 -> 85, of which waited for: 40 -> 29; matrix products, arithmetic and copies ran while one was open for 30% -> 29% of each run, Pallas kernels for 7% -> 13%
where the time goes in v2:
time: 687 us; the launch traced here: 679 us
  waiting for transfers between devices  200 us (29%)
  Pallas kernels  126 us (18%)
  starting transfers between devices  91.6 us (13%)
  local copies, waits for them, and re-layouts  88 us (13%)
  other arithmetic  78 us (11%)
  matrix products  61.5 us (9%)
  between operations  34.4 us (5%)
    ppermute x64, waiting for transfers between devices, send(): return lax.ppermute(x, 'expert', way)  181 us
    ppermute x64, starting transfers between devices, send(): return lax.ppermute(x, 'expert', way)  75.4 us
    pallas_call x4, Pallas kernels, expert_chunk(): pl.pallas_call(functools.partial(expert_kernel, steps, num_experts), grid...  71.8 us
    unnamed x179, local copies, waits for them, and re-layouts  45.8 us
    pallas_call x2, Pallas kernels, pair_grad(): pl.pallas_call(functools.partial(pair_kernel, first), grid_spec=pltpu.Pre...  41.5 us
    dot_general x5, matrix products, dot(): return lax.dot_general(a, b, (dims, ((), ())), preferred_element_type=f32)  24.2 us
    ppermute x10, waiting for transfers between devices, all_sum(): x = x + lax.ppermute(x, axis, [(i, i ^ bit) for i in range(n)])  17.5 us
  transfers between devices with their start and end apart: 85, of which 29 were waited for; matrix products, arithmetic and copies ran while one was open for 29% of the time, Pallas kernels for 13%

profile of v2, /device:TPU:0, one launch (start us, length us, event | category | flops | bytes accessed | tf_op | source)
XLA Modules:
  0.0 678.8 jit_solution(9765678156480461659)
XLA Ops:
  34.1 10.3 %collective-permute-done.2 = bf16[128,2048]{1,0:T(8,128)(2,1)S(1)} collective-permute-done((bf16[128,2048]{1,0:T(8,128)(2,1)S(1)}, bf16[128,2048]{1,0:T(8,128)(2,1)S(1)}, u32[]{:S(2)}, u32[]{:S(2)}) %collective-permute-start.2) | collective-permute-done | bytes 524320 | tf_op jit(solution)/shard_map/ppermute | solution.py:50
  47.6 10.1 %collective-permute-done.4 = bf16[128,2048]{1,0:T(8,128)(2,1)S(1)} collective-permute-done((bf16[128,2048]{1,0:T(8,128)(2,1)S(1)}, bf16[128,2048]{1,0:T(8,128)(2,1)S(1)}, u32[]{:S(2)}, u32[]{:S(2)}) %collective-permute-start.4) | collective-permute-done | bytes 524320 | tf_op jit(solution)/shard_map/ppermute | solution.py:50
  93.6 8.9 %fusion.15 = f32[1024,3,256]{0,2,1:T(8,128)} fusion(bf16[3,2048,256]{1,2,0:T(8,128)(2,1)} %all-gather.5.cloned.1.call-done, bf16[1024,2048]{1,0:T(8,128)(2,1)} %copy-done.11, f32[2048]{0:T(1024)S(1)} %copy-done.53, f32[1024]{0:T(1024)S(1)} %add_rsqrt_fusion.2), kind=kOutput, calls=%fused_computation.31 | convolution fusion | flops 3229614080 | bytes 10498048 | tf_op jit(solution)/shard_map/td,cdf->ctf/dot_general | solution.py:522
  136.8 10.9 %collective-permute-done.11 = bf16[128,2048]{1,0:T(8,128)(2,1)S(1)} collective-permute-done((bf16[128,2048]{1,0:T(8,128)(2,1)S(1)}, bf16[128,2048]{1,0:T(8,128)(2,1)S(1)}, u32[]{:S(2)}, u32[]{:S(2)}) %collective-permute-start.11) | collective-permute-done | bytes 524320 | tf_op jit(solution)/shard_map/ppermute | solution.py:50
  155.0 7.8 %collective-permute-done.15 = bf16[128,2048]{1,0:T(8,128)(2,1)S(1)} collective-permute-done((bf16[128,2048]{1,0:T(8,128)(2,1)S(1)}, bf16[128,2048]{1,0:T(8,128)(2,1)S(1)}, u32[]{:S(2)}, u32[]{:S(2)}) %collective-permute-start.15) | collective-permute-done | bytes 524320 | tf_op jit(solution)/shard_map/ppermute | solution.py:50
  183.0 7.0 %collective-permute-done.17 = bf16[128,2048]{1,0:T(8,128)(2,1)S(1)} collective-permute-done((bf16[128,2048]{1,0:T(8,128)(2,1)S(1)}, bf16[128,2048]{1,0:T(8,128)(2,1)S(1)}, u32[]{:S(2)}, u32[]{:S(2)}) %collective-permute-start.17) | collective-permute-done | bytes 524320 | tf_op jit(solution)/shard_map/ppermute | solution.py:50
  201.5 12.7 %fusion.87.h_ref = f32[1024,2048]{1,0:T(8,128)S(1)} fusion(bf16[1024,2048]{1,0:T(8,128)(2,1)} %slice_dynamic-update-slice_fusion.y_ref, bf16[2048,2048]{1,0:T(8,128)(2,1)} %bitcast.176), kind=kOutput, calls=%fused_computation.281 | convolution fusion | flops 8589934592 | bytes 20971520 | tf_op jit(solution)/shard_map/dot_general | solution.py:28
  223.3 9.3 %collective-permute-done.25 = bf16[128,2048]{1,0:T(8,128)(2,1)S(1)} collective-permute-done((bf16[128,2048]{1,0:T(8,128)(2,1)S(1)}, bf16[128,2048]{1,0:T(8,128)(2,1)S(1)}, u32[]{:S(2)}, u32[]{:S(2)}) %collective-permute-start.25) | collective-permute-done | bytes 524320 | tf_op jit(solution)/shard_map/ppermute | solution.py:50
  234.4 18.0 %shard_map.256 = (bf16[256,2048]{1,0:T(8,128)(2,1)S(1)}, bf16[1024,4096]{1,0:T(8,128)(2,1)}, bf16[1024,2048]{1,0:T(8,128)(2,1)S(1)}, bf16[256,128]{1,0:T(8,128)(2,1)S(1)}) custom-call(s32[4]{0:T(128)S(1)} %pad_add_fusion.places, bf16[256,2048]{1,0:T(8,128)(2,1)S(1)} %pad_maximum_fusion.3.f_ref, f32[1024,2048]{1,0:T(8,128)} %copy-done.4, ...), custom_call_target="tpu_custom_call" | custom-call | flops 8589934592 | bytes 16777216 | tf_op jit(solution)/shard_map/pallas_call | solution.py:255
  257.5 9.4 %collective-permute-done.28 = bf16[128,2048]{1,0:T(8,128)(2,1)S(1)} collective-permute-done((bf16[128,2048]{1,0:T(8,128)(2,1)S(1)}, bf16[128,2048]{1,0:T(8,128)(2,1)S(1)}, u32[]{:S(2)}, u32[]{:S(2)}) %collective-permute-start.28) | collective-permute-done | bytes 524320 | tf_op jit(solution)/shard_map/ppermute | solution.py:50
  267.8 17.9 %shard_map.257 = (bf16[256,2048]{1,0:T(8,128)(2,1)S(1)}, bf16[1024,4096]{1,0:T(8,128)(2,1)}, bf16[1024,2048]{1,0:T(8,128)(2,1)S(1)}, bf16[256,128]{1,0:T(8,128)(2,1)S(1)}) custom-call(s32[4]{0:T(128)S(1)} %pad_add_fusion.places, bf16[256,2048]{1,0:T(8,128)(2,1)S(1)} %pad_maximum_fusion.5.f_ref, ...), custom_call_target="tpu_custom_call", output_to_operand_aliasing={{1}: (10, {}), {2}: (11, {})} | custom-call | flops 8589934592 | bytes 16777216 | tf_op jit(solution)/shard_map/pallas_call | solution.py:255
  286.5 17.9 %shard_map.258 = (bf16[256,2048]{1,0:T(8,128)(2,1)S(1)}, bf16[1024,4096]{1,0:T(8,128)(2,1)}, bf16[1024,2048]{1,0:T(8,128)(2,1)S(1)}, bf16[256,128]{1,0:T(8,128)(2,1)S(1)}) custom-call(s32[4]{0:T(128)S(1)} %pad_add_fusion.places, bf16[256,2048]{1,0:T(8,128)(2,1)S(1)} %pad_maximum_fusion.4.f_ref, ...), custom_call_target="tpu_custom_call", output_to_operand_aliasing={{1}: (10, {}), {2}: (11, {})} | custom-call | flops 8589934592 | bytes 16777216 | tf_op jit(solution)/shard_map/pallas_call | solution.py:255
  304.5 18.0 %shard_map.259 = (bf16[256,2048]{1,0:T(8,128)(2,1)S(1)}, bf16[1024,4096]{1,0:T(8,128)(2,1)}, bf16[1024,2048]{1,0:T(8,128)(2,1)S(1)}, bf16[256,128]{1,0:T(8,128)(2,1)S(1)}) custom-call(s32[4]{0:T(128)S(1)} %pad_add_fusion.places, bf16[256,2048]{1,0:T(8,128)(2,1)S(1)} %pad_maximum_fusion.2.f_ref, ...), custom_call_target="tpu_custom_call", output_to_operand_aliasing={{1}: (10, {}), {2}: (11, {})} | custom-call | flops 8589934592 | bytes 16777216 | tf_op jit(solution)/shard_map/pallas_call | solution.py:255
  341.0 11.3 %collective-permute-done.39 = bf16[128,2048]{1,0:T(8,128)(2,1)S(1)} collective-permute-done((bf16[128,2048]{1,0:T(8,128)(2,1)S(1)}, bf16[128,2048]{1,0:T(8,128)(2,1)S(1)}, u32[]{:S(2)}, u32[]{:S(2)}) %collective-permute-start.39) | collective-permute-done | bytes 524320 | tf_op jit(solution)/shard_map/ppermute | solution.py:50
  352.9 12.4 %collective-permute-done.44 = bf16[128,2048]{1,0:T(8,128)(2,1)S(1)} collective-permute-done((bf16[128,2048]{1,0:T(8,128)(2,1)S(1)}, bf16[128,2048]{1,0:T(8,128)(2,1)S(1)}, u32[]{:S(2)}, u32[]{:S(2)}) %collective-permute-start.44) | collective-permute-done | bytes 524320 | tf_op jit(solution)/shard_map/ppermute | solution.py:50
  375.5 20.8 %shard_map.260 = bf16[1536,2048]{1,0:T(8,128)(2,1)} custom-call(s32[1]{0:T(128)} %bitcast.19.block, bf16[1024,4096]{1,0:T(8,128)(2,1)} %get-tuple-element.37.a_ref, bf16[1024,3072]{1,0:T(8,128)(2,1)} %copy-done.3, bf16[1024,2048]{1,0:T(8,128)(2,1)S(1)} %get-tuple-element.35.b_ref.a_ref, bf16[1024,3072]{1,0:T(8,128)(2,1)} %copy-done.3, ...), custom_call_target="tpu_custom_call" | custom-call | flops 12884901888 | bytes 33554432 | tf_op jit(solution)/shard_map/pallas_call | solution.py:347
  401.1 9.0 %collective-permute-done.43 = bf16[128,2048]{1,0:T(8,128)(2,1)S(1)} collective-permute-done((bf16[128,2048]{1,0:T(8,128)(2,1)S(1)}, bf16[128,2048]{1,0:T(8,128)(2,1)S(1)}, u32[]{:S(2)}, u32[]{:S(2)}) %collective-permute-start.43) | collective-permute-done | bytes 524320 | tf_op jit(solution)/shard_map/ppermute | solution.py:50
  422.6 12.4 %shard_map.261 = bf16[1024,2048]{1,0:T(8,128)(2,1)S(1)} custom-call(bf16[1024,2048]{1,0:T(8,128)(2,1)S(1)} %get-tuple-element.35.b_ref.a_ref, bf16[2048,2048]{1,0:T(8,128)(2,1)} %bitcast.177, bf16[128,2048]{1,0:T(8,128)(2,1)S(1)} %collective-permute-done.46._), custom_call_target="tpu_custom_call" | custom-call | flops 8589934592 | bytes 8388608 | tf_op jit(solution)/shard_map/pallas_call | solution.py:299
  450.2 20.7 %shard_map.262 = bf16[1536,2048]{1,0:T(8,128)(2,1)} custom-call(s32[1]{0:T(128)} %bitcast.17.block, bf16[1024,4096]{1,0:T(8,128)(2,1)} %get-tuple-element.37.a_ref, bf16[1024,3072]{1,0:T(8,128)(2,1)} %copy-done.3, bf16[1024,2048]{1,0:T(8,128)(2,1)S(1)} %get-tuple-element.35.b_ref.a_ref, bf16[1024,3072]{1,0:T(8,128)(2,1)} %copy-done.3, ...), custom_call_target="tpu_custom_call" | custom-call | flops 12884901888 | bytes 33554432 | tf_op jit(solution)/shard_map/pallas_call | solution.py:347
  510.3 8.1 %collective-permute-done.51 = bf16[128,2048]{1,0:T(8,128)(2,1)S(1)} collective-permute-done((bf16[128,2048]{1,0:T(8,128)(2,1)S(1)}, bf16[128,2048]{1,0:T(8,128)(2,1)S(1)}, u32[]{:S(2)}, u32[]{:S(2)}) %collective-permute-start.51) | collective-permute-done | bytes 524320 | tf_op jit(solution)/shard_map/ppermute | solution.py:50
  530.8 7.6 %collective-permute-done.56 = bf16[128,2048]{1,0:T(8,128)(2,1)S(1)} collective-permute-done((bf16[128,2048]{1,0:T(8,128)(2,1)S(1)}, bf16[128,2048]{1,0:T(8,128)(2,1)S(1)}, u32[]{:S(2)}, u32[]{:S(2)}) %collective-permute-start.56) | collective-permute-done | bytes 524320 | tf_op jit(solution)/shard_map/ppermute | solution.py:50
  556.2 7.2 %fusion.3 = (f32[2048]{0:T(1024)S(1)}, bf16[1024,2048]{1,0:T(8,128)(2,1)S(1)}, f32[1024,2048]{1,0:T(8,128)S(1)}) fusion(bf16[1024,2048]{1,0:T(8,128)(2,1)} %copy-done.11, f32[1024]{0:T(1024)S(1)} %copy-done.61, bf16[3,1024,256]{1,2,0:T(8,128)(2,1)S(1)} %bitcast.171, bf16[3,2048,256]{1,2,0:T(8,128)(2,1)} %all-gather.5.cloned.1.call-done), kind=kOutput, calls=%fused_computation.6 | convolution fusion | flops 3231709184 | bytes 21508096 | tf_op jit(solution)/shard_map/ctf,cdf->td/dot_general | solution.py:668
  606.9 12.2 %convert_add_fusion = f32[1536,2048]{1,0:T(8,128)} fusion(bf16[1536,2048]{1,0:T(8,128)(2,1)} %collective-permute-done.72, bf16[1536,2048]{1,0:T(8,128)(2,1)} %shard_map.262), kind=kLoop, calls=%fused_computation | loop fusion | flops 9437184 | bytes 25165824 | tf_op jit(solution)/shard_map/add | solution.py:642
  648.1 9.9 %copy.152 = f32[2,2,256,2048]{3,1,0,2:T(2,128)} copy(f32[2,2,256,2048]{3,2,1,0:T(8,128)S(1)} %bitcast.149) | data formatting | bytes 16777216 | tf_op jit(solution)/shard_map/reshape | solution.py:701
  (503 shorter events, 354.6 us)
Async XLA Ops:
  7.2 86.4 %all-gather.5.cloned.1.call-start = ((), (), s32[]{:S(2)}) async-start(), calls=%async_computation.1 | async-start | bytes 3932160 | tf_op jit(solution)/shard_map/all_gather | solution.py:493
  9.5 110.8 %all-gather.7.cloned.1.call-start = ((), (), s32[]{:S(2)}) async-start(), calls=%async_computation.2 | async-start | bytes 1310720 | tf_op jit(solution)/shard_map/all_gather | solution.py:494
  10.3 191.2 %all-gather.9.cloned.1.call-start = ((), (), s32[]{:S(2)}) async-start(), calls=%async_computation.4 | async-start | bytes 10485760 | tf_op jit(solution)/shard_map/all_gather | solution.py:504
  20.1 214.3 %collective-permute-start.29 = (bf16[2,2,256,2048]{3,2,1,0:T(8,128)(2,1)}, bf16[2,2,256,2048]{3,2,1,0:T(8,128)(2,1)}, u32[]{:S(2)}, u32[]{:S(2)}) collective-permute-start(bf16[2,2,256,2048]{3,2,1,0:T(8,128)(2,1)} %bitcast.145.refs_0_), channel_id=1, source_target_pairs={{0,8},{8,0},{16,24},{24,16},{1,9},{9,1},{17,25},{25,17},{2,10},{10... | collective-permute-start | bytes 12582920 | tf_op jit(solution)/shard_map/ppermute | solution.py:119
  20.2 173.9 %collective-permute-start.30 = (bf16[2,2,256,2048]{3,2,1,0:T(8,128)(2,1)}, bf16[2,2,256,2048]{3,2,1,0:T(8,128)(2,1)}, u32[]{:S(2)}, u32[]{:S(2)}) collective-permute-start(bf16[2,2,256,2048]{3,2,1,0:T(8,128)(2,1)} %bitcast.145.refs_0_), channel_id=1, source_target_pairs={{16,0},{24,8},{0,16},{8,24},{17,1},{25,9},{1,17},{9,25},{18,2},{26... | collective-permute-start | bytes 12582920 | tf_op jit(solution)/shard_map/ppermute | solution.py:123
  24.3 643.2 %reduce-scatter.2.cloned.1.call-start = ((), (), s32[]{:S(2)}) async-start(), calls=%async_computation.3 | async-start | bytes 5242880 | tf_op jit(solution)/shard_map/reduce_scatter | solution.py:681
  83.4 64.3 %collective-permute-start.20 = (bf16[128,2176]{1,0:T(8,128)(2,1)}, bf16[128,2176]{1,0:T(8,128)(2,1)}, u32[]{:S(2)}, u32[]{:S(2)}) collective-permute-start(bf16[128,2176]{1,0:T(8,128)(2,1)} %collective-permute-done.19), channel_id=1, source_target_pairs={{0,2},{2,4},{4,6},{6,7},{7,5},{5,3},{3,1},{1,0},{8,10},{10,12},{12... | collective-permute-start | bytes 1671176 | tf_op jit(solution)/shard_map/ppermute | solution.py:50
  129.6 23.3 %collective-permute-start.21 = (bf16[128,2176]{1,0:T(8,128)(2,1)S(1)}, bf16[128,2176]{1,0:T(8,128)(2,1)S(1)}, u32[]{:S(2)}, u32[]{:S(2)}) collective-permute-start(bf16[128,2176]{1,0:T(8,128)(2,1)S(1)} %copy-done.42), channel_id=1, source_target_pairs={{2,0},{4,2},{6,4},{7,6},{5,7},{3,5},{1,3},{0,1},{10,8},{12,10},{14... | collective-permute-start | bytes 1671176 | tf_op jit(solution)/shard_map/ppermute | solution.py:50
  198.5 35.9 %collective-permute-start.31 = (bf16[2,2,256,2048]{3,2,1,0:T(8,128)(2,1)}, bf16[2,2,256,2048]{3,2,1,0:T(8,128)(2,1)}, u32[]{:S(2)}, u32[]{:S(2)}) collective-permute-start(bf16[2,2,256,2048]{3,2,1,0:T(8,128)(2,1)} %broadcast_add_fusion.refs_2_), channel_id=1, source_target_pairs={{0,8},{8,0},{16,24},{24,16},{1,9},{9,1},{17,25},{25,17},{2,10},{10... | collective-permute-start | bytes 12582920 | tf_op jit(solution)/shard_map/ppermute | solution.py:119
  223.3 30.9 %collective-permute-start.27 = (bf16[128,2048]{1,0:T(8,128)(2,1)S(1)}, bf16[128,2048]{1,0:T(8,128)(2,1)S(1)}, u32[]{:S(2)}, u32[]{:S(2)}) collective-permute-start(bf16[128,2048]{1,0:T(8,128)(2,1)S(1)} %get-tuple-element.170), channel_id=1, source_target_pairs={{2,0},{4,2},{6,4},{7,6},{5,7},{3,5},{1,3},{0,1},{10,8},{12,10},{14... | collective-permute-start | bytes 1572872 | tf_op jit(solution)/shard_map/ppermute | solution.py:50
  232.6 23.1 %collective-permute-start.32 = (bf16[128,2048]{1,0:T(8,128)(2,1)S(1)}, bf16[128,2048]{1,0:T(8,128)(2,1)S(1)}, u32[]{:S(2)}, u32[]{:S(2)}) collective-permute-start(bf16[128,2048]{1,0:T(8,128)(2,1)S(1)} %collective-permute-done.25), channel_id=1, source_target_pairs={{0,2},{2,4},{4,6},{6,7},{7,5},{5,3},{3,1},{1,0},{8,10},{10,12},{12... | collective-permute-start | bytes 1572872 | tf_op jit(solution)/shard_map/ppermute | solution.py:50
  255.7 30.1 %collective-permute-start.34 = (bf16[64,2048]{1,0:T(8,128)(2,1)S(1)}, bf16[64,2048]{1,0:T(8,128)(2,1)S(1)}, u32[]{:S(2)}, u32[]{:S(2)}) collective-permute-start(bf16[64,2048]{1,0:T(8,128)(2,1)S(1)} %slice_add_fusion.17), channel_id=1, source_target_pairs={{0,2},{2,4},{4,6},{6,7},{7,5},{5,3},{3,1},{1,0},{8,10},{10,12},{12... | collective-permute-start | bytes 786440 | tf_op jit(solution)/shard_map/ppermute | solution.py:50
  328.8 44.0 %collective-permute-start.35 = (bf16[1024,3072]{1,0:T(8,128)(2,1)S(1)}, bf16[1024,3072]{1,0:T(8,128)(2,1)S(1)}, u32[]{:S(2)}, u32[]{:S(2)}) collective-permute-start(bf16[1024,3072]{1,0:T(8,128)(2,1)S(1)} %pad_maximum_fusion), channel_id=1, source_target_pairs={{0,8},{8,0},{16,24},{24,16},{1,9},{9,1},{17,25},{25,17},{2,10},{10... | collective-permute-start | bytes 18874376 | tf_op jit(solution)/shard_map/ppermute | solution.py:119
  328.8 39.9 %collective-permute-start.37 = (bf16[1024,2048]{1,0:T(8,128)(2,1)}, bf16[1024,2048]{1,0:T(8,128)(2,1)S(1)}, u32[]{:S(2)}, u32[]{:S(2)}) collective-permute-start(bf16[1024,2048]{1,0:T(8,128)(2,1)} %slice_dynamic-update-slice_fusion.y_ref), channel_id=1, source_target_pairs={{0,8},{8,0},{16,24},{24,16},{1,9},{9,1},{17,25},{25,17},{2,10},{10... | collective-permute-start | bytes 12582920 | tf_op jit(solution)/shard_map/ppermute | solution.py:119
  329.8 39.0 %collective-permute-start.36 = (bf16[1024,2048]{1,0:T(8,128)(2,1)S(1)}, bf16[1024,2048]{1,0:T(8,128)(2,1)S(1)}, u32[]{:S(2)}, u32[]{:S(2)}) collective-permute-start(bf16[1024,2048]{1,0:T(8,128)(2,1)S(1)} %constant_dynamic-update-slice_fusion.19.x_ref), channel_id=1, source_target_pairs={{0,8},{8,0},{16,24},{24,16},{1,9},{9,1},{17,25},{25,17},{2,10},{10... | collective-permute-start | bytes 12582920 | tf_op jit(solution)/shard_map/ppermute | solution.py:119
  366.4 34.7 %collective-permute-start.45 = (bf16[128,2048]{1,0:T(8,128)(2,1)}, bf16[128,2048]{1,0:T(8,128)(2,1)S(1)}, u32[]{:S(2)}, u32[]{:S(2)}) collective-permute-start(bf16[128,2048]{1,0:T(8,128)(2,1)} %get-tuple-element.154), channel_id=1, source_target_pairs={{2,0},{4,2},{6,4},{7,6},{5,7},{3,5},{1,3},{0,1},{10,8},{12,10},{14... | collective-permute-start | bytes 1572872 | tf_op jit(solution)/shard_map/ppermute | solution.py:50
  366.7 32.1 %collective-permute-start.42 = (bf16[128,2048]{1,0:T(8,128)(2,1)S(1)}, bf16[128,2048]{1,0:T(8,128)(2,1)S(1)}, u32[]{:S(2)}, u32[]{:S(2)}) collective-permute-start(bf16[128,2048]{1,0:T(8,128)(2,1)S(1)} %get-tuple-element.153), channel_id=1, source_target_pairs={{0,2},{2,4},{4,6},{6,7},{7,5},{5,3},{3,1},{1,0},{8,10},{10,12},{12... | collective-permute-start | bytes 1572872 | tf_op jit(solution)/shard_map/ppermute | solution.py:50
  412.8 194.1 %collective-permute-start.72 = (bf16[1536,2048]{1,0:T(8,128)(2,1)}, bf16[1536,2048]{1,0:T(8,128)(2,1)}, u32[]{:S(2)}, u32[]{:S(2)}) collective-permute-start(bf16[1536,2048]{1,0:T(8,128)(2,1)} %shard_map.260), channel_id=1, source_target_pairs={{0,16},{8,24},{16,0},{24,8},{1,17},{9,25},{17,1},{25,9},{2,18},{10... | collective-permute-start | bytes 18874376 | tf_op jit(solution)/shard_map/ppermute | solution.py:129
  416.1 149.4 %collective-permute-start.63 = (f32[17,2048]{1,0:T(8,128)}, f32[17,2048]{1,0:T(8,128)}, u32[]{:S(2)}, u32[]{:S(2)}) collective-permute-start(f32[17,2048]{1,0:T(8,128)} %fusion.79), channel_id=1, source_target_pairs={{0,16},{8,24},{16,0},{24,8},{1,17},{9,25},{17,1},{25,9},{2,18},{10... | collective-permute-start | bytes 417800 | tf_op jit(solution)/shard_map/ppermute | solution.py:380
  447.1 26.4 %collective-permute-start.48 = (bf16[128,2048]{1,0:T(8,128)(2,1)S(1)}, bf16[128,2048]{1,0:T(8,128)(2,1)S(1)}, u32[]{:S(2)}, u32[]{:S(2)}) collective-permute-start(bf16[128,2048]{1,0:T(8,128)(2,1)S(1)} %get-tuple-element.164), channel_id=1, source_target_pairs={{2,0},{4,2},{6,4},{7,6},{5,7},{3,5},{1,3},{0,1},{10,8},{12,10},{14... | collective-permute-start | bytes 1572872 | tf_op jit(solution)/shard_map/ppermute | solution.py:50
  448.3 25.6 %collective-permute-start.60 = (bf16[128,2048]{1,0:T(8,128)(2,1)S(1)}, bf16[128,2048]{1,0:T(8,128)(2,1)S(1)}, u32[]{:S(2)}, u32[]{:S(2)}) collective-permute-start(bf16[128,2048]{1,0:T(8,128)(2,1)S(1)} %get-tuple-element.161), channel_id=1, source_target_pairs={{0,2},{2,4},{4,6},{6,7},{7,5},{5,3},{3,1},{1,0},{8,10},{10,12},{12... | collective-permute-start | bytes 1572872 | tf_op jit(solution)/shard_map/ppermute | solution.py:50
  589.7 33.9 %collective-permute-start.66 = (f32[17,2048]{1,0:T(8,128)S(1)}, f32[17,2048]{1,0:T(8,128)S(1)}, u32[]{:S(2)}, u32[]{:S(2)}) collective-permute-start(f32[17,2048]{1,0:T(8,128)S(1)} %add.514), channel_id=1, source_target_pairs={{0,4},{1,5},{2,6},{3,7},{4,0},{5,1},{6,2},{7,3},{8,12},{9,13},{10,... | collective-permute-start | bytes 417800 | tf_op jit(solution)/shard_map/ppermute | solution.py:380
  594.6 27.1 %collective-permute-start.78 = (bf16[128,2048]{1,0:T(8,128)(2,1)S(1)}, bf16[128,2048]{1,0:T(8,128)(2,1)S(1)}, u32[]{:S(2)}, u32[]{:S(2)}) collective-permute-start(bf16[128,2048]{1,0:T(8,128)(2,1)S(1)} %pad_maximum_fusion.15), channel_id=1, source_target_pairs={{2,0},{4,2},{6,4},{7,6},{5,7},{3,5},{1,3},{0,1},{10,8},{12,10},{14... | collective-permute-start | bytes 1572872 | tf_op jit(solution)/shard_map/ppermute | solution.py:50
  637.9 25.4 %collective-permute-start.76 = (bf16[128,2048]{1,0:T(8,128)(2,1)S(1)}, bf16[128,2048]{1,0:T(8,128)(2,1)S(1)}, u32[]{:S(2)}, u32[]{:S(2)}) collective-permute-start(bf16[128,2048]{1,0:T(8,128)(2,1)S(1)} %get-tuple-element.114), channel_id=1, source_target_pairs={{0,2},{2,4},{4,6},{6,7},{7,5},{5,3},{3,1},{1,0},{8,10},{10,12},{12... | collective-permute-start | bytes 1572872 | tf_op jit(solution)/shard_map/ppermute | solution.py:50
  (133 other events, 1682.0 us)
Sparse Core Ops, SparseCore 0:
  10.1 47.9 all-gather.4
  59.7 21.6 all-gather.6
  83.0 99.0 all-gather.8
  555.0 44.1 reduce-scatter.1

commit v3 on v2

--- a/solution.py
+++ b/solution.py
@@ -288,6 +288,44 @@
     )(*args)
 
 
+def finish_kernel(experts_dev, own_ref, *refs):
+    gu_ref, down_ref = refs[-2:]
+    for e in range(experts_dev):
+        for k in range(3):
+            block = 2 * e + k if k < 2 else 2 * experts_dev + e
+            total = own_ref[block].astype(f32)
+            for ref in refs[:-3]:
+                total = total + ref[block].astype(f32)
+            if k < 2:
+                gu_ref[:, e, k, :] = total
+            else:
+                down_ref[:, e, :] = total
+
+
+def finish(terms, experts_dev, ff_dev, wait):
+    width = terms[0].shape[1]
+    tile = 32
+    blocks = 3 * experts_dev
+    return pl.pallas_call(
+        functools.partial(finish_kernel, experts_dev),
+        grid=(ff_dev // tile,),
+        in_specs=[pl.BlockSpec((blocks, tile, width), lambda i: (0, i, 0))] * len(terms)
+        + [pl.BlockSpec(memory_space=pl.ANY)],
+        out_specs=[
+            pl.BlockSpec((tile, experts_dev, 2, width), lambda i: (i, 0, 0, 0)),
+            pl.BlockSpec((tile, experts_dev, width), lambda i: (i, 0, 0)),
+        ],
+        out_shape=[
+            jax.ShapeDtypeStruct((ff_dev, experts_dev, 2, width), f32),
+            jax.ShapeDtypeStruct((ff_dev, experts_dev, width), f32),
+        ],
+        compiler_params=pltpu.CompilerParams(vmem_limit_bytes=40 << 20),
+        cost_estimate=pl.CostEstimate(
+            flops=0, bytes_accessed=8 * blocks * ff_dev * width, transcendentals=0
+        ),
+    )(*[t.reshape(blocks, ff_dev, width) for t in terms], wait)
+
+
 def product_kernel(a_ref, b_ref, _, o_ref):
     o_ref[...] = jnp.dot(a_ref[...], b_ref[...], preferred_element_type=f32).astype(bf16)
 
@@ -509,17 +547,18 @@
     chosen = jnp.any(expert_routes[:, :, None] == expert_ids[None, None, :], axis=1)
     chosen = jnp.pad(chosen.astype(bf16), ((0, 0), (0, 128 - num_experts)))
     sent_grad = jnp.concatenate([out_grad, chosen], axis=1)
+    place = (ring.members[:, None] * tok_rows + jnp.arange(tok_rows, dtype=jnp.int32)).reshape(-1)
+    segment, position = seq_layout(seq_lengths[0], seq_order[0], place)
+    cos_rows, sin_rows = rope_tables(position, head_dim)
+
+    projected = jnp.einsum("td,cdf->ctf", features, qkv_full, preferred_element_type=f32)
     sent_grad = tie(sent_grad, states_slots[n_exp // 2])
-    grad_slots = ring.gather(sent_grad)
+    stages = {1: projected}
+    grad_slots = ring.gather(sent_grad, lambda s, slots: stages.get(s), lag=1)
     grad_top_all = in_order([g[:, :width] for g in grad_slots])
     chosen_all = in_order([g[:, width:] for g in grad_slots])
     back_hidden = dot(grad_top_all, down_all, ((1,), (1,)))
 
-    place = (ring.members[:, None] * tok_rows + jnp.arange(tok_rows, dtype=jnp.int32)).reshape(-1)
-    segment, position = seq_layout(seq_lengths[0], seq_order[0], place)
-    cos_rows, sin_rows = rope_tables(position, head_dim)
-
-    projected = jnp.einsum("td,cdf->ctf", features, qkv_full, preferred_element_type=f32)
     head_proj = projected.reshape(3, rows, heads, head_dim).transpose(0, 2, 1, 3)
     query_scale, key_scale = rms_scale(head_proj[0]), rms_scale(head_proj[1])
     query_normed, key_normed = head_proj[0] * query_scale, head_proj[1] * key_scale
@@ -637,12 +676,10 @@
     )
     while jobs:
         next_term(branch_slots[n_exp // 2])
-    weight_grads = terms[0].astype(f32)
-    for s in range(1, steps):
-        weight_grads = weight_grads + chips.to_ahead(terms[s], s).astype(f32)
+    all_terms = [terms[0]] + [chips.to_ahead(terms[s], s) for s in range(1, steps)]
     grad_rows = in_order(branch_slots)
     moe_parts = slots_of(moe_made[0])
-    moe_parts[n_exp // 2] = tie(moe_parts[n_exp // 2], branch_slots[n_exp // 2])
+    moe_parts[n_exp // 2] = tie(moe_parts[n_exp // 2], branch_slots[2])
     moe_steps = {}
     moe = ring.reduce(moe_parts, moe_steps.__setitem__)
     output = mixed + moe
@@ -654,7 +691,7 @@
     )
     grad_query = rotate_back(grad_query, cos_rows, sin_rows)
     grad_key = rotate_back(grad_key, cos_rows, sin_rows)
-    grad_query = tie(grad_query, moe_steps[1])
+    grad_query = tie(grad_query, moe_steps[2])
     query_gain_part = jnp.sum(query_normed * grad_query, axis=(0, 1))
     key_gain_part = jnp.sum(key_normed * grad_key, axis=(0, 1))
     grad_query = norm_back(grad_query, query_gain, query_normed, query_scale)
@@ -674,8 +711,16 @@
             [attn_gain_part, query_gain_part, key_gain_part, jnp.pad(squares, (0, 125))]
         ).reshape(-1, 128)
     ).reshape(-1)
-    ends = {2: weight_grads, 1: wide}
-    grad_features = ring.reduce(slots_of(features_part), lambda s, x: ends.get(s), (small,))
+    weight_grads = []
+
+    def at_end(s, x):
+        if s == n_exp // 2 - 1:
+            weight_grads.extend(finish(all_terms, experts_dev, ff_dev, x))
+            return weight_grads[1]
+        return wide if s == 1 else None
+
+    grad_features = ring.reduce(slots_of(features_part), at_end, (small,))
+    grad_proj = tie(grad_proj, features_part)
     qkv_term = jnp.einsum("td,ctf->cdf", features, grad_proj, preferred_element_type=f32)
     out_term = dot(grad_rows, attended, ((0,), (0,)))
     attn_sums = lax.psum_scatter(
@@ -698,8 +743,7 @@
         small[width + head_dim : width + 2 * head_dim],
         wide[num_experts],
         wide[:num_experts].T,
-        weight_grads[:gu_cols].reshape(experts_dev, 2, ff_dev, width).transpose(2, 0, 1, 3),
-        weight_grads[gu_cols:].reshape(experts_dev, ff_dev, width).transpose(1, 0, 2),
+        *weight_grads,
         stream_rms,
     )
 

time: 687 us -> 678 us (0.987)
  waiting for transfers between devices: 200 us -> 228 us
  local copies, waits for them, and re-layouts: 88 us -> 64.9 us
  other arithmetic: 78 us -> 59.5 us
  Pallas kernels: 126 us -> 136 us
    reshape x3 -> x0, local copies, waits for them, and re-layouts: 18.7 us -> none  [the longest x1 9.88 us: on_device(): weight_grads[:gu_cols].reshape(experts_dev, 2, ff_dev, width)]
    ppermute x64, waiting for transfers between devices: 181 us -> 196 us  [send(): return lax.ppermute(x, 'expert', way)]
    ppermute x10, waiting for transfers between devices: 17.5 us -> 31.3 us  [all_sum(): x = x + lax.ppermute(x, axis, [(i, i ^ bit) for i in range(n)])]
    add x1 -> x0, other arithmetic: 12.2 us -> none  [on_device(): weight_grads = weight_grads + chips.to_ahead(terms[s], s).astype(f32)]
    pallas_call x0 -> x1, Pallas kernels: none -> 10.2 us  [finish(): pl.pallas_call(functools.partial(finish_kernel, experts_dev), grid=(ff_de...]
    ppermute x10, starting transfers between devices: 12 us -> 3.55 us  [all_sum(): x = x + lax.ppermute(x, axis, [(i, i ^ bit) for i in range(n)])]
    unnamed x179 -> x189, local copies, waits for them, and re-layouts: 45.8 us -> 39.7 us
  transfers between devices with their start and end apart: 85 -> 85, of which waited for: 29 -> 35; matrix products, arithmetic and copies ran while one was open for 29% -> 23% of each run, Pallas kernels for 13% -> 15%
where the time goes in v3:
time: 678 us; the launch traced here: 669 us
  waiting for transfers between devices  228 us (34%)
  Pallas kernels  136 us (20%)
  starting transfers between devices  85.1 us (13%)
  local copies, waits for them, and re-layouts  64.9 us (10%)
  other arithmetic  59.5 us (9%)
  matrix products  58.3 us (9%)
  between operations  37.2 us (5%)
    ppermute x64, waiting for transfers between devices, send(): return lax.ppermute(x, 'expert', way)  196 us
    ppermute x64, starting transfers between devices, send(): return lax.ppermute(x, 'expert', way)  78.2 us
    pallas_call x4, Pallas kernels, expert_chunk(): pl.pallas_call(functools.partial(expert_kernel, steps, num_experts), grid...  71.8 us
    pallas_call x2, Pallas kernels, pair_grad(): pl.pallas_call(functools.partial(pair_kernel, first), grid_spec=pltpu.Pre...  41.5 us
    unnamed x189, local copies, waits for them, and re-layouts  39.7 us
    ppermute x10, waiting for transfers between devices, all_sum(): x = x + lax.ppermute(x, axis, [(i, i ^ bit) for i in range(n)])  31.3 us
    dot_general x5, matrix products, dot(): return lax.dot_general(a, b, (dims, ((), ())), preferred_element_type=f32)  24.3 us
  transfers between devices with their start and end apart: 85, of which 35 were waited for; matrix products, arithmetic and copies ran while one was open for 23% of the time, Pallas kernels for 15%

profile of v3, /device:TPU:0, one launch (start us, length us, event | category | flops | bytes accessed | tf_op | source)
XLA Modules:
  0.0 668.6 jit_solution(3151012795051290930)
XLA Ops:
  35.3 9.5 %collective-permute-done.2 = bf16[128,2048]{1,0:T(8,128)(2,1)S(1)} collective-permute-done((bf16[128,2048]{1,0:T(8,128)(2,1)}, bf16[128,2048]{1,0:T(8,128)(2,1)S(1)}, u32[]{:S(2)}, u32[]{:S(2)}) %collective-permute-start.2) | collective-permute-done | bytes 524320 | tf_op jit(solution)/shard_map/ppermute | solution.py:50
  46.9 11.1 %collective-permute-done.4 = bf16[128,2048]{1,0:T(8,128)(2,1)S(1)} collective-permute-done((bf16[128,2048]{1,0:T(8,128)(2,1)S(1)}, bf16[128,2048]{1,0:T(8,128)(2,1)S(1)}, u32[]{:S(2)}, u32[]{:S(2)}) %collective-permute-start.4) | collective-permute-done | bytes 524320 | tf_op jit(solution)/shard_map/ppermute | solution.py:50
  123.3 14.9 %collective-permute-done.11 = bf16[128,2048]{1,0:T(8,128)(2,1)S(1)} collective-permute-done((bf16[128,2048]{1,0:T(8,128)(2,1)S(1)}, bf16[128,2048]{1,0:T(8,128)(2,1)S(1)}, u32[]{:S(2)}, u32[]{:S(2)}) %collective-permute-start.11) | collective-permute-done | bytes 524320 | tf_op jit(solution)/shard_map/ppermute | solution.py:50
  143.6 8.2 %collective-permute-done.15 = bf16[128,2048]{1,0:T(8,128)(2,1)S(1)} collective-permute-done((bf16[128,2048]{1,0:T(8,128)(2,1)S(1)}, bf16[128,2048]{1,0:T(8,128)(2,1)S(1)}, u32[]{:S(2)}, u32[]{:S(2)}) %collective-permute-start.15) | collective-permute-done | bytes 524320 | tf_op jit(solution)/shard_map/ppermute | solution.py:50
  191.6 12.7 %fusion.89.h_ref = f32[1024,2048]{1,0:T(8,128)S(1)} fusion(bf16[1024,2048]{1,0:T(8,128)(2,1)} %slice_dynamic-update-slice_fusion.y_ref, bf16[2048,2048]{1,0:T(8,128)(2,1)} %bitcast.170), kind=kOutput, calls=%fused_computation.283 | convolution fusion | flops 8589934592 | bytes 20971520 | tf_op jit(solution)/shard_map/dot_general | solution.py:28
  214.0 9.3 %collective-permute-done.25 = bf16[128,2048]{1,0:T(8,128)(2,1)S(1)} collective-permute-done((bf16[128,2048]{1,0:T(8,128)(2,1)S(1)}, bf16[128,2048]{1,0:T(8,128)(2,1)S(1)}, u32[]{:S(2)}, u32[]{:S(2)}) %collective-permute-start.25) | collective-permute-done | bytes 524320 | tf_op jit(solution)/shard_map/ppermute | solution.py:50
  225.2 18.0 %shard_map.256 = (bf16[256,2048]{1,0:T(8,128)(2,1)S(1)}, bf16[1024,4096]{1,0:T(8,128)(2,1)}, bf16[1024,2048]{1,0:T(8,128)(2,1)S(1)}, bf16[256,128]{1,0:T(8,128)(2,1)S(1)}) custom-call(s32[4]{0:T(128)S(1)} %pad_add_fusion.places, bf16[256,2048]{1,0:T(8,128)(2,1)S(1)} %pad_maximum_fusion.3.f_ref, f32[1024,2048]{1,0:T(8,128)} %copy-done.5, ...), custom_call_target="tpu_custom_call" | custom-call | flops 8589934592 | bytes 16777216 | tf_op jit(solution)/shard_map/pallas_call | solution.py:255
  247.3 10.6 %collective-permute-done.28 = bf16[128,2048]{1,0:T(8,128)(2,1)S(1)} collective-permute-done((bf16[128,2048]{1,0:T(8,128)(2,1)S(1)}, bf16[128,2048]{1,0:T(8,128)(2,1)S(1)}, u32[]{:S(2)}, u32[]{:S(2)}) %collective-permute-start.28) | collective-permute-done | bytes 524320 | tf_op jit(solution)/shard_map/ppermute | solution.py:50
  258.5 17.9 %shard_map.257 = (bf16[256,2048]{1,0:T(8,128)(2,1)S(1)}, bf16[1024,4096]{1,0:T(8,128)(2,1)}, bf16[1024,2048]{1,0:T(8,128)(2,1)S(1)}, bf16[256,128]{1,0:T(8,128)(2,1)S(1)}) custom-call(s32[4]{0:T(128)S(1)} %pad_add_fusion.places, bf16[256,2048]{1,0:T(8,128)(2,1)S(1)} %pad_maximum_fusion.5.f_ref, ...), custom_call_target="tpu_custom_call", output_to_operand_aliasing={{1}: (10, {}), {2}: (11, {})} | custom-call | flops 8589934592 | bytes 16777216 | tf_op jit(solution)/shard_map/pallas_call | solution.py:255
  276.7 17.9 %shard_map.258 = (bf16[256,2048]{1,0:T(8,128)(2,1)S(1)}, bf16[1024,4096]{1,0:T(8,128)(2,1)}, bf16[1024,2048]{1,0:T(8,128)(2,1)S(1)}, bf16[256,128]{1,0:T(8,128)(2,1)S(1)}) custom-call(s32[4]{0:T(128)S(1)} %pad_add_fusion.places, bf16[256,2048]{1,0:T(8,128)(2,1)S(1)} %pad_maximum_fusion.4.f_ref, ...), custom_call_target="tpu_custom_call", output_to_operand_aliasing={{1}: (10, {}), {2}: (11, {})} | custom-call | flops 8589934592 | bytes 16777216 | tf_op jit(solution)/shard_map/pallas_call | solution.py:255
  294.6 18.0 %shard_map.259 = (bf16[256,2048]{1,0:T(8,128)(2,1)S(1)}, bf16[1024,4096]{1,0:T(8,128)(2,1)}, bf16[1024,2048]{1,0:T(8,128)(2,1)S(1)}, bf16[256,128]{1,0:T(8,128)(2,1)S(1)}) custom-call(s32[4]{0:T(128)S(1)} %pad_add_fusion.places, bf16[256,2048]{1,0:T(8,128)(2,1)S(1)} %pad_maximum_fusion.2.f_ref, ...), custom_call_target="tpu_custom_call", output_to_operand_aliasing={{1}: (10, {}), {2}: (11, {})} | custom-call | flops 8589934592 | bytes 16777216 | tf_op jit(solution)/shard_map/pallas_call | solution.py:255
  331.1 11.3 %collective-permute-done.39 = bf16[128,2048]{1,0:T(8,128)(2,1)S(1)} collective-permute-done((bf16[128,2048]{1,0:T(8,128)(2,1)S(1)}, bf16[128,2048]{1,0:T(8,128)(2,1)S(1)}, u32[]{:S(2)}, u32[]{:S(2)}) %collective-permute-start.39) | collective-permute-done | bytes 524320 | tf_op jit(solution)/shard_map/ppermute | solution.py:50
  344.2 11.1 %collective-permute-done.44 = bf16[128,2048]{1,0:T(8,128)(2,1)S(1)} collective-permute-done((bf16[128,2048]{1,0:T(8,128)(2,1)S(1)}, bf16[128,2048]{1,0:T(8,128)(2,1)S(1)}, u32[]{:S(2)}, u32[]{:S(2)}) %collective-permute-start.44) | collective-permute-done | bytes 524320 | tf_op jit(solution)/shard_map/ppermute | solution.py:50
  364.6 20.7 %shard_map.260 = bf16[1536,2048]{1,0:T(8,128)(2,1)} custom-call(s32[1]{0:T(128)} %bitcast.19.block, bf16[1024,4096]{1,0:T(8,128)(2,1)} %get-tuple-element.39.a_ref, bf16[1024,3072]{1,0:T(8,128)(2,1)} %copy-done.4, bf16[1024,2048]{1,0:T(8,128)(2,1)S(1)} %get-tuple-element.37.b_ref.a_ref, bf16[1024,3072]{1,0:T(8,128)(2,1)} %copy-done.4, ...), custom_call_target="tpu_custom_call" | custom-call | flops 12884901888 | bytes 33554432 | tf_op jit(solution)/shard_map/pallas_call | solution.py:385
  389.9 9.5 %collective-permute-done.43 = bf16[128,2048]{1,0:T(8,128)(2,1)S(1)} collective-permute-done((bf16[128,2048]{1,0:T(8,128)(2,1)S(1)}, bf16[128,2048]{1,0:T(8,128)(2,1)S(1)}, u32[]{:S(2)}, u32[]{:S(2)}) %collective-permute-start.43) | collective-permute-done | bytes 524320 | tf_op jit(solution)/shard_map/ppermute | solution.py:50
  404.3 9.0 %collective-permute-done.46._ = bf16[128,2048]{1,0:T(8,128)(2,1)S(1)} collective-permute-done((bf16[128,2048]{1,0:T(8,128)(2,1)S(1)}, bf16[128,2048]{1,0:T(8,128)(2,1)S(1)}, u32[]{:S(2)}, u32[]{:S(2)}) %collective-permute-start.46) | collective-permute-done | bytes 524320 | tf_op jit(solution)/shard_map/ppermute | solution.py:50
  414.8 12.4 %shard_map.261 = bf16[1024,2048]{1,0:T(8,128)(2,1)S(1)} custom-call(bf16[1024,2048]{1,0:T(8,128)(2,1)S(1)} %get-tuple-element.37.b_ref.a_ref, bf16[2048,2048]{1,0:T(8,128)(2,1)} %bitcast.171, bf16[128,2048]{1,0:T(8,128)(2,1)S(1)} %collective-permute-done.46._), custom_call_target="tpu_custom_call" | custom-call | flops 8589934592 | bytes 8388608 | tf_op jit(solution)/shard_map/pallas_call | solution.py:337
  443.4 20.8 %shard_map.262 = bf16[1536,2048]{1,0:T(8,128)(2,1)} custom-call(s32[1]{0:T(128)} %bitcast.17.block, bf16[1024,4096]{1,0:T(8,128)(2,1)} %get-tuple-element.39.a_ref, bf16[1024,3072]{1,0:T(8,128)(2,1)} %copy-done.4, bf16[1024,2048]{1,0:T(8,128)(2,1)S(1)} %get-tuple-element.37.b_ref.a_ref, bf16[1024,3072]{1,0:T(8,128)(2,1)} %copy-done.4, ...), custom_call_target="tpu_custom_call" | custom-call | flops 12884901888 | bytes 33554432 | tf_op jit(solution)/shard_map/pallas_call | solution.py:385
  523.8 10.0 %fusion.3 = (f32[2048]{0:T(1024)S(1)}, bf16[1024,2048]{1,0:T(8,128)(2,1)}, f32[1024,2048]{1,0:T(8,128)S(1)}) fusion(bf16[1024,2048]{1,0:T(8,128)(2,1)} %copy-done.13, f32[1024]{0:T(1024)S(1)} %copy-done.62, bf16[3,1024,256]{1,2,0:T(8,128)(2,1)} %bitcast.164, bf16[3,2048,256]{1,2,0:T(8,128)(2,1)} %all-gather.5.cloned.1.call-done), kind=kOutput, calls=%fused_computation.5 | convolution fusion | flops 3231709184 | bytes 21508096 | tf_op jit(solution)/shard_map/ctf,cdf->td/dot_general | solution.py:705
  554.6 8.4 %collective-permute-done.54 = bf16[128,2048]{1,0:T(8,128)(2,1)S(1)} collective-permute-done((bf16[128,2048]{1,0:T(8,128)(2,1)}, bf16[128,2048]{1,0:T(8,128)(2,1)S(1)}, u32[]{:S(2)}, u32[]{:S(2)}) %collective-permute-start.54) | collective-permute-done | bytes 524320 | tf_op jit(solution)/shard_map/ppermute | solution.py:50
  575.2 9.5 %collective-permute-done.55 = bf16[128,2048]{1,0:T(8,128)(2,1)S(1)} collective-permute-done((bf16[128,2048]{1,0:T(8,128)(2,1)S(1)}, bf16[128,2048]{1,0:T(8,128)(2,1)S(1)}, u32[]{:S(2)}, u32[]{:S(2)}) %collective-permute-start.55) | collective-permute-done | bytes 524320 | tf_op jit(solution)/shard_map/ppermute | solution.py:50
  589.7 10.2 %shard_map.263 = (f32[256,2,2,2048]{3,2,1,0:T(2,128)}, f32[256,2,2048]{2,1,0:T(2,128)}) custom-call(bf16[6,256,2048]{2,1,0:T(8,128)(2,1)S(1)} %bitcast.148, bf16[6,256,2048]{2,1,0:T(8,128)(2,1)} %bitcast.53.refs_0_, bf16[128,2048]{1,0:T(8,128)(2,1)S(1)} %pad_maximum_fusion.14.refs_1_), custom_call_target="tpu_custom_call" | custom-call | bytes 25165824 | tf_op jit(solution)/shard_map/pallas_call | solution.py:309
  607.1 10.5 %collective-permute-done.64 = f32[17,2048]{1,0:T(8,128)S(1)} collective-permute-done((f32[17,2048]{1,0:T(8,128)S(1)}, f32[17,2048]{1,0:T(8,128)S(1)}, u32[]{:S(2)}, u32[]{:S(2)}) %collective-permute-start.64) | collective-permute-done | bytes 139296 | tf_op jit(solution)/shard_map/ppermute | solution.py:418
  617.7 8.8 %collective-permute-done.65 = f32[17,2048]{1,0:T(8,128)S(1)} collective-permute-done((f32[17,2048]{1,0:T(8,128)S(1)}, f32[17,2048]{1,0:T(8,128)S(1)}, u32[]{:S(2)}, u32[]{:S(2)}) %collective-permute-start.65) | collective-permute-done | bytes 139296 | tf_op jit(solution)/shard_map/ppermute | solution.py:418
  (513 shorter events, 331.0 us)
Async XLA Ops:
  7.2 75.7 %all-gather.5.cloned.1.call-start = ((), (), s32[]{:S(2)}) async-start(), calls=%async_computation.1 | async-start | bytes 3932160 | tf_op jit(solution)/shard_map/all_gather | solution.py:531
  9.6 97.5 %all-gather.7.cloned.1.call-start = ((), (), s32[]{:S(2)}) async-start(), calls=%async_computation.2 | async-start | bytes 1310720 | tf_op jit(solution)/shard_map/all_gather | solution.py:532
  10.3 181.2 %all-gather.9.cloned.1.call-start = ((), (), s32[]{:S(2)}) async-start(), calls=%async_computation.4 | async-start | bytes 10485760 | tf_op jit(solution)/shard_map/all_gather | solution.py:542
  20.1 205.1 %collective-permute-start.29 = (bf16[2,2,256,2048]{3,2,1,0:T(8,128)(2,1)}, bf16[2,2,256,2048]{3,2,1,0:T(8,128)(2,1)}, u32[]{:S(2)}, u32[]{:S(2)}) collective-permute-start(bf16[2,2,256,2048]{3,2,1,0:T(8,128)(2,1)} %bitcast.144.refs_0_), channel_id=1, source_target_pairs={{0,8},{8,0},{16,24},{24,16},{1,9},{9,1},{17,25},{25,17},{2,10},{10... | collective-permute-start | bytes 12582920 | tf_op jit(solution)/shard_map/ppermute | solution.py:119
  20.2 163.4 %collective-permute-start.30 = (bf16[2,2,256,2048]{3,2,1,0:T(8,128)(2,1)}, bf16[2,2,256,2048]{3,2,1,0:T(8,128)(2,1)}, u32[]{:S(2)}, u32[]{:S(2)}) collective-permute-start(bf16[2,2,256,2048]{3,2,1,0:T(8,128)(2,1)} %bitcast.144.refs_0_), channel_id=1, source_target_pairs={{16,0},{24,8},{0,16},{8,24},{17,1},{25,9},{1,17},{9,25},{18,2},{26... | collective-permute-start | bytes 12582920 | tf_op jit(solution)/shard_map/ppermute | solution.py:123
  24.4 633.2 %reduce-scatter.2.cloned.1.call-start = ((), (), s32[]{:S(2)}) async-start(), calls=%async_computation.3 | async-start | bytes 5242880 | tf_op jit(solution)/shard_map/reduce_scatter | solution.py:726
  188.0 37.2 %collective-permute-start.31 = (bf16[2,2,256,2048]{3,2,1,0:T(8,128)(2,1)}, bf16[2,2,256,2048]{3,2,1,0:T(8,128)(2,1)}, u32[]{:S(2)}, u32[]{:S(2)}) collective-permute-start(bf16[2,2,256,2048]{3,2,1,0:T(8,128)(2,1)} %broadcast_add_fusion.refs_2_), channel_id=1, source_target_pairs={{0,8},{8,0},{16,24},{24,16},{1,9},{9,1},{17,25},{25,17},{2,10},{10... | collective-permute-start | bytes 12582920 | tf_op jit(solution)/shard_map/ppermute | solution.py:119
  213.9 31.1 %collective-permute-start.27 = (bf16[128,2048]{1,0:T(8,128)(2,1)S(1)}, bf16[128,2048]{1,0:T(8,128)(2,1)S(1)}, u32[]{:S(2)}, u32[]{:S(2)}) collective-permute-start(bf16[128,2048]{1,0:T(8,128)(2,1)S(1)} %get-tuple-element.174), channel_id=1, source_target_pairs={{2,0},{4,2},{6,4},{7,6},{5,7},{3,5},{1,3},{0,1},{10,8},{12,10},{14... | collective-permute-start | bytes 1572872 | tf_op jit(solution)/shard_map/ppermute | solution.py:50
  245.3 31.2 %collective-permute-start.34 = (bf16[64,2048]{1,0:T(8,128)(2,1)S(1)}, bf16[64,2048]{1,0:T(8,128)(2,1)S(1)}, u32[]{:S(2)}, u32[]{:S(2)}) collective-permute-start(bf16[64,2048]{1,0:T(8,128)(2,1)S(1)} %slice_add_fusion.17), channel_id=1, source_target_pairs={{0,2},{2,4},{4,6},{6,7},{7,5},{5,3},{3,1},{1,0},{8,10},{10,12},{12... | collective-permute-start | bytes 786440 | tf_op jit(solution)/shard_map/ppermute | solution.py:50
  318.9 43.0 %collective-permute-start.35 = (bf16[1024,3072]{1,0:T(8,128)(2,1)S(1)}, bf16[1024,3072]{1,0:T(8,128)(2,1)S(1)}, u32[]{:S(2)}, u32[]{:S(2)}) collective-permute-start(bf16[1024,3072]{1,0:T(8,128)(2,1)S(1)} %pad_maximum_fusion), channel_id=1, source_target_pairs={{0,8},{8,0},{16,24},{24,16},{1,9},{9,1},{17,25},{25,17},{2,10},{10... | collective-permute-start | bytes 18874376 | tf_op jit(solution)/shard_map/ppermute | solution.py:119
  318.9 39.0 %collective-permute-start.37 = (bf16[1024,2048]{1,0:T(8,128)(2,1)}, bf16[1024,2048]{1,0:T(8,128)(2,1)S(1)}, u32[]{:S(2)}, u32[]{:S(2)}) collective-permute-start(bf16[1024,2048]{1,0:T(8,128)(2,1)} %slice_dynamic-update-slice_fusion.y_ref), channel_id=1, source_target_pairs={{0,8},{8,0},{16,24},{24,16},{1,9},{9,1},{17,25},{25,17},{2,10},{10... | collective-permute-start | bytes 12582920 | tf_op jit(solution)/shard_map/ppermute | solution.py:119
  319.9 38.1 %collective-permute-start.36 = (bf16[1024,2048]{1,0:T(8,128)(2,1)S(1)}, bf16[1024,2048]{1,0:T(8,128)(2,1)S(1)}, u32[]{:S(2)}, u32[]{:S(2)}) collective-permute-start(bf16[1024,2048]{1,0:T(8,128)(2,1)S(1)} %constant_dynamic-update-slice_fusion.19.x_ref), channel_id=1, source_target_pairs={{0,8},{8,0},{16,24},{24,16},{1,9},{9,1},{17,25},{25,17},{2,10},{10... | collective-permute-start | bytes 12582920 | tf_op jit(solution)/shard_map/ppermute | solution.py:119
  355.7 34.2 %collective-permute-start.45 = (bf16[128,2048]{1,0:T(8,128)(2,1)S(1)}, bf16[128,2048]{1,0:T(8,128)(2,1)S(1)}, u32[]{:S(2)}, u32[]{:S(2)}) collective-permute-start(bf16[128,2048]{1,0:T(8,128)(2,1)S(1)} %get-tuple-element.158), channel_id=1, source_target_pairs={{2,0},{4,2},{6,4},{7,6},{5,7},{3,5},{1,3},{0,1},{10,8},{12,10},{14... | collective-permute-start | bytes 1572872 | tf_op jit(solution)/shard_map/ppermute | solution.py:50
  357.3 30.6 %collective-permute-start.42 = (bf16[128,2048]{1,0:T(8,128)(2,1)S(1)}, bf16[128,2048]{1,0:T(8,128)(2,1)S(1)}, u32[]{:S(2)}, u32[]{:S(2)}) collective-permute-start(bf16[128,2048]{1,0:T(8,128)(2,1)S(1)} %get-tuple-element.157), channel_id=1, source_target_pairs={{0,2},{2,4},{4,6},{6,7},{7,5},{5,3},{3,1},{1,0},{8,10},{10,12},{12... | collective-permute-start | bytes 1572872 | tf_op jit(solution)/shard_map/ppermute | solution.py:50
  402.8 186.9 %collective-permute-start.72 = (bf16[1536,2048]{1,0:T(8,128)(2,1)}, bf16[1536,2048]{1,0:T(8,128)(2,1)}, u32[]{:S(2)}, u32[]{:S(2)}) collective-permute-start(bf16[1536,2048]{1,0:T(8,128)(2,1)} %shard_map.260), channel_id=1, source_target_pairs={{0,16},{8,24},{16,0},{24,8},{1,17},{9,25},{17,1},{25,9},{2,18},{10... | collective-permute-start | bytes 18874376 | tf_op jit(solution)/shard_map/ppermute | solution.py:129
  434.5 32.2 %collective-permute-start.48 = (bf16[64,2048]{1,0:T(8,128)(2,1)}, bf16[64,2048]{1,0:T(8,128)(2,1)S(1)}, u32[]{:S(2)}, u32[]{:S(2)}) collective-permute-start(bf16[64,2048]{1,0:T(8,128)(2,1)} %get-tuple-element.169), channel_id=1, source_target_pairs={{0,2},{2,4},{4,6},{6,7},{7,5},{5,3},{3,1},{1,0},{8,10},{10,12},{12... | collective-permute-start | bytes 786440 | tf_op jit(solution)/shard_map/ppermute | solution.py:50
  435.6 31.1 %collective-permute-start.52 = (bf16[64,2048]{1,0:T(8,128)(2,1)S(1)}, bf16[64,2048]{1,0:T(8,128)(2,1)S(1)}, u32[]{:S(2)}, u32[]{:S(2)}) collective-permute-start(bf16[64,2048]{1,0:T(8,128)(2,1)S(1)} %get-tuple-element.170), channel_id=1, source_target_pairs={{2,0},{4,2},{6,4},{7,6},{5,7},{3,5},{1,3},{0,1},{10,8},{12,10},{14... | collective-permute-start | bytes 786440 | tf_op jit(solution)/shard_map/ppermute | solution.py:50
  437.5 31.6 %collective-permute-start.58 = (bf16[128,2048]{1,0:T(8,128)(2,1)S(1)}, bf16[128,2048]{1,0:T(8,128)(2,1)S(1)}, u32[]{:S(2)}, u32[]{:S(2)}) collective-permute-start(bf16[128,2048]{1,0:T(8,128)(2,1)S(1)} %get-tuple-element.167), channel_id=1, source_target_pairs={{2,0},{4,2},{6,4},{7,6},{5,7},{3,5},{1,3},{0,1},{10,8},{12,10},{14... | collective-permute-start | bytes 1572872 | tf_op jit(solution)/shard_map/ppermute | solution.py:50
  443.0 28.1 %collective-permute-start.59 = (bf16[128,2048]{1,0:T(8,128)(2,1)S(1)}, bf16[128,2048]{1,0:T(8,128)(2,1)S(1)}, u32[]{:S(2)}, u32[]{:S(2)}) collective-permute-start(bf16[128,2048]{1,0:T(8,128)(2,1)S(1)} %get-tuple-element.165), channel_id=1, source_target_pairs={{0,2},{2,4},{4,6},{6,7},{7,5},{5,3},{3,1},{1,0},{8,10},{10,12},{12... | collective-permute-start | bytes 1572872 | tf_op jit(solution)/shard_map/ppermute | solution.py:50
  466.9 35.6 %collective-permute-start.49 = (bf16[128,2048]{1,0:T(8,128)(2,1)S(1)}, bf16[128,2048]{1,0:T(8,128)(2,1)S(1)}, u32[]{:S(2)}, u32[]{:S(2)}) collective-permute-start(bf16[128,2048]{1,0:T(8,128)(2,1)S(1)} %pad_maximum_fusion.12), channel_id=1, source_target_pairs={{0,2},{2,4},{4,6},{6,7},{7,5},{5,3},{3,1},{1,0},{8,10},{10,12},{12... | collective-permute-start | bytes 1572872 | tf_op jit(solution)/shard_map/ppermute | solution.py:50
  468.8 37.9 %collective-permute-start.53 = (bf16[128,2048]{1,0:T(8,128)(2,1)S(1)}, bf16[128,2048]{1,0:T(8,128)(2,1)S(1)}, u32[]{:S(2)}, u32[]{:S(2)}) collective-permute-start(bf16[128,2048]{1,0:T(8,128)(2,1)S(1)} %pad_maximum_fusion.13), channel_id=1, source_target_pairs={{2,0},{4,2},{6,4},{7,6},{5,7},{3,5},{1,3},{0,1},{10,8},{12,10},{14... | collective-permute-start | bytes 1572872 | tf_op jit(solution)/shard_map/ppermute | solution.py:50
  549.9 54.2 %collective-permute-start.63 = (f32[17,2048]{1,0:T(8,128)S(1)}, f32[17,2048]{1,0:T(8,128)S(1)}, u32[]{:S(2)}, u32[]{:S(2)}) collective-permute-start(f32[17,2048]{1,0:T(8,128)S(1)} %fusion.81), channel_id=1, source_target_pairs={{0,16},{8,24},{16,0},{24,8},{1,17},{9,25},{17,1},{25,9},{2,18},{10... | collective-permute-start | bytes 417800 | tf_op jit(solution)/shard_map/ppermute | solution.py:418
  573.0 29.4 %collective-permute-start.75 = (bf16[128,2048]{1,0:T(8,128)(2,1)}, bf16[128,2048]{1,0:T(8,128)(2,1)S(1)}, u32[]{:S(2)}, u32[]{:S(2)}) collective-permute-start(bf16[128,2048]{1,0:T(8,128)(2,1)} %pad_maximum_fusion.15), channel_id=1, source_target_pairs={{0,2},{2,4},{4,6},{6,7},{7,5},{5,3},{3,1},{1,0},{8,10},{10,12},{12... | collective-permute-start | bytes 1572872 | tf_op jit(solution)/shard_map/ppermute | solution.py:50
  574.6 52.7 %collective-permute-start.78 = (bf16[128,2048]{1,0:T(8,128)(2,1)S(1)}, bf16[128,2048]{1,0:T(8,128)(2,1)}, u32[]{:S(2)}, u32[]{:S(2)}) collective-permute-start(bf16[128,2048]{1,0:T(8,128)(2,1)S(1)} %pad_maximum_fusion.14.refs_1_), channel_id=1, source_target_pairs={{2,0},{4,2},{6,4},{7,6},{5,7},{3,5},{1,3},{0,1},{10,8},{12,10},{14... | collective-permute-start | bytes 1572872 | tf_op jit(solution)/shard_map/ppermute | solution.py:50
  (136 other events, 1844.2 us)
Sparse Core Ops, SparseCore 0:
  9.7 47.3 all-gather.4
  58.6 21.6 all-gather.6
  82.5 99.1 all-gather.8
  545.4 43.8 reduce-scatter.1

commit v4 on v3

--- a/solution.py
+++ b/solution.py
@@ -691,7 +691,7 @@
     )
     grad_query = rotate_back(grad_query, cos_rows, sin_rows)
     grad_key = rotate_back(grad_key, cos_rows, sin_rows)
-    grad_query = tie(grad_query, moe_steps[2])
+    grad_query = tie(grad_query, moe_steps[1])
     query_gain_part = jnp.sum(query_normed * grad_query, axis=(0, 1))
     key_gain_part = jnp.sum(key_normed * grad_key, axis=(0, 1))
     grad_query = norm_back(grad_query, query_gain, query_normed, query_scale)

time: 678 us -> 668 us (0.985)
    unnamed x189 -> x193, local copies, waits for them, and re-layouts: 39.7 us -> 37.5 us
  transfers between devices with their start and end apart: 85 -> 85, of which waited for: 35 -> 34; matrix products, arithmetic and copies ran while one was open for 23% -> 22% of each run, Pallas kernels for 15% -> 15%
where the time goes in v4:
time: 668 us; the launch traced here: 659 us
  waiting for transfers between devices  223 us (33%)
  Pallas kernels  136 us (20%)
  starting transfers between devices  88.4 us (13%)
  local copies, waits for them, and re-layouts  60.6 us (9%)
  other arithmetic  57.7 us (9%)
  matrix products  55.9 us (8%)
  between operations  37.3 us (6%)
    ppermute x64, waiting for transfers between devices, send(): return lax.ppermute(x, 'expert', way)  192 us
    ppermute x64, starting transfers between devices, send(): return lax.ppermute(x, 'expert', way)  79.8 us
    pallas_call x4, Pallas kernels, expert_chunk(): pl.pallas_call(functools.partial(expert_kernel, steps, num_experts), grid...  71.8 us
    pallas_call x2, Pallas kernels, pair_grad(): pl.pallas_call(functools.partial(pair_kernel, first), grid_spec=pltpu.Pre...  41.5 us
    unnamed x193, local copies, waits for them, and re-layouts  37.5 us
    ppermute x10, waiting for transfers between devices, all_sum(): x = x + lax.ppermute(x, axis, [(i, i ^ bit) for i in range(n)])  29.9 us
    dot_general x5, matrix products, dot(): return lax.dot_general(a, b, (dims, ((), ())), preferred_element_type=f32)  22 us
  transfers between devices with their start and end apart: 85, of which 34 were waited for; matrix products, arithmetic and copies ran while one was open for 22% of the time, Pallas kernels for 15%

profile of v4, /device:TPU:0, one launch (start us, length us, event | category | flops | bytes accessed | tf_op | source)
XLA Modules:
  0.0 659.1 jit_solution(4385520710634857454)
XLA Ops:
  35.3 9.5 %collective-permute-done.2 = bf16[128,2048]{1,0:T(8,128)(2,1)S(1)} collective-permute-done((bf16[128,2048]{1,0:T(8,128)(2,1)}, bf16[128,2048]{1,0:T(8,128)(2,1)S(1)}, u32[]{:S(2)}, u32[]{:S(2)}) %collective-permute-start.2) | collective-permute-done | bytes 524320 | tf_op jit(solution)/shard_map/ppermute | solution.py:50
  46.9 11.1 %collective-permute-done.4 = bf16[128,2048]{1,0:T(8,128)(2,1)S(1)} collective-permute-done((bf16[128,2048]{1,0:T(8,128)(2,1)S(1)}, bf16[128,2048]{1,0:T(8,128)(2,1)S(1)}, u32[]{:S(2)}, u32[]{:S(2)}) %collective-permute-start.4) | collective-permute-done | bytes 524320 | tf_op jit(solution)/shard_map/ppermute | solution.py:50
  71.2 8.1 %collective-permute-done.8 = bf16[128,2176]{1,0:T(8,128)(2,1)S(1)} collective-permute-done((bf16[128,2176]{1,0:T(8,128)(2,1)S(1)}, bf16[128,2176]{1,0:T(8,128)(2,1)S(1)}, u32[]{:S(2)}, u32[]{:S(2)}) %collective-permute-start.8) | collective-permute-done | bytes 557088 | tf_op jit(solution)/shard_map/ppermute | solution.py:50
  123.3 14.8 %collective-permute-done.11 = bf16[128,2048]{1,0:T(8,128)(2,1)S(1)} collective-permute-done((bf16[128,2048]{1,0:T(8,128)(2,1)S(1)}, bf16[128,2048]{1,0:T(8,128)(2,1)S(1)}, u32[]{:S(2)}, u32[]{:S(2)}) %collective-permute-start.11) | collective-permute-done | bytes 524320 | tf_op jit(solution)/shard_map/ppermute | solution.py:50
  143.7 8.3 %collective-permute-done.15 = bf16[128,2048]{1,0:T(8,128)(2,1)S(1)} collective-permute-done((bf16[128,2048]{1,0:T(8,128)(2,1)S(1)}, bf16[128,2048]{1,0:T(8,128)(2,1)S(1)}, u32[]{:S(2)}, u32[]{:S(2)}) %collective-permute-start.15) | collective-permute-done | bytes 524320 | tf_op jit(solution)/shard_map/ppermute | solution.py:50
  191.8 12.7 %fusion.89.h_ref = f32[1024,2048]{1,0:T(8,128)S(1)} fusion(bf16[1024,2048]{1,0:T(8,128)(2,1)} %slice_dynamic-update-slice_fusion.y_ref, bf16[2048,2048]{1,0:T(8,128)(2,1)} %bitcast.170), kind=kOutput, calls=%fused_computation.283 | convolution fusion | flops 8589934592 | bytes 20971520 | tf_op jit(solution)/shard_map/dot_general | solution.py:28
  214.2 9.3 %collective-permute-done.25 = bf16[128,2048]{1,0:T(8,128)(2,1)S(1)} collective-permute-done((bf16[128,2048]{1,0:T(8,128)(2,1)S(1)}, bf16[128,2048]{1,0:T(8,128)(2,1)S(1)}, u32[]{:S(2)}, u32[]{:S(2)}) %collective-permute-start.25) | collective-permute-done | bytes 524320 | tf_op jit(solution)/shard_map/ppermute | solution.py:50
  225.2 18.0 %shard_map.256 = (bf16[256,2048]{1,0:T(8,128)(2,1)S(1)}, bf16[1024,4096]{1,0:T(8,128)(2,1)}, bf16[1024,2048]{1,0:T(8,128)(2,1)S(1)}, bf16[256,128]{1,0:T(8,128)(2,1)S(1)}) custom-call(s32[4]{0:T(128)S(1)} %pad_add_fusion.places, bf16[256,2048]{1,0:T(8,128)(2,1)S(1)} %pad_maximum_fusion.3.f_ref, f32[1024,2048]{1,0:T(8,128)} %copy-done.5, ...), custom_call_target="tpu_custom_call" | custom-call | flops 8589934592 | bytes 16777216 | tf_op jit(solution)/shard_map/pallas_call | solution.py:255
  247.3 10.4 %collective-permute-done.28 = bf16[128,2048]{1,0:T(8,128)(2,1)S(1)} collective-permute-done((bf16[128,2048]{1,0:T(8,128)(2,1)S(1)}, bf16[128,2048]{1,0:T(8,128)(2,1)S(1)}, u32[]{:S(2)}, u32[]{:S(2)}) %collective-permute-start.28) | collective-permute-done | bytes 524320 | tf_op jit(solution)/shard_map/ppermute | solution.py:50
  258.6 17.9 %shard_map.257 = (bf16[256,2048]{1,0:T(8,128)(2,1)S(1)}, bf16[1024,4096]{1,0:T(8,128)(2,1)}, bf16[1024,2048]{1,0:T(8,128)(2,1)S(1)}, bf16[256,128]{1,0:T(8,128)(2,1)S(1)}) custom-call(s32[4]{0:T(128)S(1)} %pad_add_fusion.places, bf16[256,2048]{1,0:T(8,128)(2,1)S(1)} %pad_maximum_fusion.5.f_ref, ...), custom_call_target="tpu_custom_call", output_to_operand_aliasing={{1}: (10, {}), {2}: (11, {})} | custom-call | flops 8589934592 | bytes 16777216 | tf_op jit(solution)/shard_map/pallas_call | solution.py:255
  276.7 17.9 %shard_map.258 = (bf16[256,2048]{1,0:T(8,128)(2,1)S(1)}, bf16[1024,4096]{1,0:T(8,128)(2,1)}, bf16[1024,2048]{1,0:T(8,128)(2,1)S(1)}, bf16[256,128]{1,0:T(8,128)(2,1)S(1)}) custom-call(s32[4]{0:T(128)S(1)} %pad_add_fusion.places, bf16[256,2048]{1,0:T(8,128)(2,1)S(1)} %pad_maximum_fusion.4.f_ref, ...), custom_call_target="tpu_custom_call", output_to_operand_aliasing={{1}: (10, {}), {2}: (11, {})} | custom-call | flops 8589934592 | bytes 16777216 | tf_op jit(solution)/shard_map/pallas_call | solution.py:255
  294.7 18.0 %shard_map.259 = (bf16[256,2048]{1,0:T(8,128)(2,1)S(1)}, bf16[1024,4096]{1,0:T(8,128)(2,1)}, bf16[1024,2048]{1,0:T(8,128)(2,1)S(1)}, bf16[256,128]{1,0:T(8,128)(2,1)S(1)}) custom-call(s32[4]{0:T(128)S(1)} %pad_add_fusion.places, bf16[256,2048]{1,0:T(8,128)(2,1)S(1)} %pad_maximum_fusion.2.f_ref, ...), custom_call_target="tpu_custom_call", output_to_operand_aliasing={{1}: (10, {}), {2}: (11, {})} | custom-call | flops 8589934592 | bytes 16777216 | tf_op jit(solution)/shard_map/pallas_call | solution.py:255
  322.2 6.6 %collective-permute-done.38 = bf16[64,2048]{1,0:T(8,128)(2,1)S(1)} collective-permute-done((bf16[64,2048]{1,0:T(8,128)(2,1)S(1)}, bf16[64,2048]{1,0:T(8,128)(2,1)S(1)}, u32[]{:S(2)}, u32[]{:S(2)}) %collective-permute-start.38) | collective-permute-done | bytes 262176 | tf_op jit(solution)/shard_map/ppermute | solution.py:50
  331.2 11.3 %collective-permute-done.39 = bf16[128,2048]{1,0:T(8,128)(2,1)S(1)} collective-permute-done((bf16[128,2048]{1,0:T(8,128)(2,1)S(1)}, bf16[128,2048]{1,0:T(8,128)(2,1)S(1)}, u32[]{:S(2)}, u32[]{:S(2)}) %collective-permute-start.39) | collective-permute-done | bytes 524320 | tf_op jit(solution)/shard_map/ppermute | solution.py:50
  344.2 11.2 %collective-permute-done.44 = bf16[128,2048]{1,0:T(8,128)(2,1)S(1)} collective-permute-done((bf16[128,2048]{1,0:T(8,128)(2,1)S(1)}, bf16[128,2048]{1,0:T(8,128)(2,1)S(1)}, u32[]{:S(2)}, u32[]{:S(2)}) %collective-permute-start.44) | collective-permute-done | bytes 524320 | tf_op jit(solution)/shard_map/ppermute | solution.py:50
  364.6 20.8 %shard_map.260 = bf16[1536,2048]{1,0:T(8,128)(2,1)} custom-call(s32[1]{0:T(128)} %bitcast.19.block, bf16[1024,4096]{1,0:T(8,128)(2,1)} %get-tuple-element.39.a_ref, bf16[1024,3072]{1,0:T(8,128)(2,1)} %copy-done.4, bf16[1024,2048]{1,0:T(8,128)(2,1)S(1)} %get-tuple-element.37.b_ref.a_ref, bf16[1024,3072]{1,0:T(8,128)(2,1)} %copy-done.4, ...), custom_call_target="tpu_custom_call" | custom-call | flops 12884901888 | bytes 33554432 | tf_op jit(solution)/shard_map/pallas_call | solution.py:385
  389.6 9.7 %collective-permute-done.43 = bf16[128,2048]{1,0:T(8,128)(2,1)S(1)} collective-permute-done((bf16[128,2048]{1,0:T(8,128)(2,1)S(1)}, bf16[128,2048]{1,0:T(8,128)(2,1)S(1)}, u32[]{:S(2)}, u32[]{:S(2)}) %collective-permute-start.43) | collective-permute-done | bytes 524320 | tf_op jit(solution)/shard_map/ppermute | solution.py:50
  404.4 7.1 %collective-permute-done.46._ = bf16[128,2048]{1,0:T(8,128)(2,1)S(1)} collective-permute-done((bf16[128,2048]{1,0:T(8,128)(2,1)S(1)}, bf16[128,2048]{1,0:T(8,128)(2,1)S(1)}, u32[]{:S(2)}, u32[]{:S(2)}) %collective-permute-start.46) | collective-permute-done | bytes 524320 | tf_op jit(solution)/shard_map/ppermute | solution.py:50
  411.5 12.4 %shard_map.261 = bf16[1024,2048]{1,0:T(8,128)(2,1)S(1)} custom-call(bf16[1024,2048]{1,0:T(8,128)(2,1)S(1)} %get-tuple-element.37.b_ref.a_ref, bf16[2048,2048]{1,0:T(8,128)(2,1)} %bitcast.171, bf16[128,2048]{1,0:T(8,128)(2,1)S(1)} %collective-permute-done.46._), custom_call_target="tpu_custom_call" | custom-call | flops 8589934592 | bytes 8388608 | tf_op jit(solution)/shard_map/pallas_call | solution.py:337
  443.2 20.7 %shard_map.262 = bf16[1536,2048]{1,0:T(8,128)(2,1)} custom-call(s32[1]{0:T(128)} %bitcast.17.block, bf16[1024,4096]{1,0:T(8,128)(2,1)} %get-tuple-element.39.a_ref, bf16[1024,3072]{1,0:T(8,128)(2,1)} %copy-done.4, bf16[1024,2048]{1,0:T(8,128)(2,1)S(1)} %get-tuple-element.37.b_ref.a_ref, bf16[1024,3072]{1,0:T(8,128)(2,1)} %copy-done.4, ...), custom_call_target="tpu_custom_call" | custom-call | flops 12884901888 | bytes 33554432 | tf_op jit(solution)/shard_map/pallas_call | solution.py:385
  471.1 10.5 %collective-permute-done.49 = bf16[128,2048]{1,0:T(8,128)(2,1)S(1)} collective-permute-done((bf16[128,2048]{1,0:T(8,128)(2,1)S(1)}, bf16[128,2048]{1,0:T(8,128)(2,1)S(1)}, u32[]{:S(2)}, u32[]{:S(2)}) %collective-permute-start.49) | collective-permute-done | bytes 524320 | tf_op jit(solution)/shard_map/ppermute | solution.py:50
  525.7 10.0 %fusion.3 = (f32[2048]{0:T(1024)S(1)}, bf16[1024,2048]{1,0:T(8,128)(2,1)}, f32[1024,2048]{1,0:T(8,128)S(1)}) fusion(bf16[1024,2048]{1,0:T(8,128)(2,1)} %copy-done.13, f32[1024]{0:T(1024)S(1)} %copy-done.64, bf16[3,1024,256]{1,2,0:T(8,128)(2,1)} %bitcast.164, bf16[3,2048,256]{1,2,0:T(8,128)(2,1)} %all-gather.5.cloned.1.call-done), kind=kOutput, calls=%fused_computation.5 | convolution fusion | flops 3231709184 | bytes 21508096 | tf_op jit(solution)/shard_map/ctf,cdf->td/dot_general | solution.py:705
  579.0 10.4 %shard_map.263 = (f32[256,2,2,2048]{3,2,1,0:T(2,128)}, f32[256,2,2048]{2,1,0:T(2,128)}) custom-call(bf16[6,256,2048]{2,1,0:T(8,128)(2,1)S(1)} %bitcast.148, bf16[6,256,2048]{2,1,0:T(8,128)(2,1)} %bitcast.53.refs_0_, bf16[128,2048]{1,0:T(8,128)(2,1)S(1)} %pad_maximum_fusion.14.refs_1_), custom_call_target="tpu_custom_call" | custom-call | bytes 25165824 | tf_op jit(solution)/shard_map/pallas_call | solution.py:309
  595.8 13.0 %collective-permute-done.64 = f32[17,2048]{1,0:T(8,128)S(1)} collective-permute-done((f32[17,2048]{1,0:T(8,128)S(1)}, f32[17,2048]{1,0:T(8,128)S(1)}, u32[]{:S(2)}, u32[]{:S(2)}) %collective-permute-start.64) | collective-permute-done | bytes 139296 | tf_op jit(solution)/shard_map/ppermute | solution.py:418
  (517 shorter events, 322.1 us)
Async XLA Ops:
  7.2 75.7 %all-gather.5.cloned.1.call-start = ((), (), s32[]{:S(2)}) async-start(), calls=%async_computation.1 | async-start | bytes 3932160 | tf_op jit(solution)/shard_map/all_gather | solution.py:531
  9.6 97.5 %all-gather.7.cloned.1.call-start = ((), (), s32[]{:S(2)}) async-start(), calls=%async_computation.2 | async-start | bytes 1310720 | tf_op jit(solution)/shard_map/all_gather | solution.py:532
  10.3 181.4 %all-gather.9.cloned.1.call-start = ((), (), s32[]{:S(2)}) async-start(), calls=%async_computation.4 | async-start | bytes 10485760 | tf_op jit(solution)/shard_map/all_gather | solution.py:542
  20.1 205.1 %collective-permute-start.29 = (bf16[2,2,256,2048]{3,2,1,0:T(8,128)(2,1)}, bf16[2,2,256,2048]{3,2,1,0:T(8,128)(2,1)}, u32[]{:S(2)}, u32[]{:S(2)}) collective-permute-start(bf16[2,2,256,2048]{3,2,1,0:T(8,128)(2,1)} %bitcast.144.refs_0_), channel_id=1, source_target_pairs={{0,8},{8,0},{16,24},{24,16},{1,9},{9,1},{17,25},{25,17},{2,10},{10... | collective-permute-start | bytes 12582920 | tf_op jit(solution)/shard_map/ppermute | solution.py:119
  20.2 163.6 %collective-permute-start.30 = (bf16[2,2,256,2048]{3,2,1,0:T(8,128)(2,1)}, bf16[2,2,256,2048]{3,2,1,0:T(8,128)(2,1)}, u32[]{:S(2)}, u32[]{:S(2)}) collective-permute-start(bf16[2,2,256,2048]{3,2,1,0:T(8,128)(2,1)} %bitcast.144.refs_0_), channel_id=1, source_target_pairs={{16,0},{24,8},{0,16},{8,24},{17,1},{25,9},{1,17},{9,25},{18,2},{26... | collective-permute-start | bytes 12582920 | tf_op jit(solution)/shard_map/ppermute | solution.py:123
  24.4 623.7 %reduce-scatter.2.cloned.1.call-start = ((), (), s32[]{:S(2)}) async-start(), calls=%async_computation.3 | async-start | bytes 5242880 | tf_op jit(solution)/shard_map/reduce_scatter | solution.py:726
  112.0 27.5 %collective-permute-start.20 = (bf16[128,2176]{1,0:T(8,128)(2,1)S(1)}, bf16[128,2176]{1,0:T(8,128)(2,1)S(1)}, u32[]{:S(2)}, u32[]{:S(2)}) collective-permute-start(bf16[128,2176]{1,0:T(8,128)(2,1)S(1)} %broadcast_add_fusion.1), channel_id=1, source_target_pairs={{0,2},{2,4},{4,6},{6,7},{7,5},{5,3},{3,1},{1,0},{8,10},{10,12},{12... | collective-permute-start | bytes 1671176 | tf_op jit(solution)/shard_map/ppermute | solution.py:50
  188.2 37.0 %collective-permute-start.31 = (bf16[2,2,256,2048]{3,2,1,0:T(8,128)(2,1)}, bf16[2,2,256,2048]{3,2,1,0:T(8,128)(2,1)}, u32[]{:S(2)}, u32[]{:S(2)}) collective-permute-start(bf16[2,2,256,2048]{3,2,1,0:T(8,128)(2,1)} %broadcast_add_fusion.refs_2_), channel_id=1, source_target_pairs={{0,8},{8,0},{16,24},{24,16},{1,9},{9,1},{17,25},{25,17},{2,10},{10... | collective-permute-start | bytes 12582920 | tf_op jit(solution)/shard_map/ppermute | solution.py:119
  214.1 30.9 %collective-permute-start.27 = (bf16[128,2048]{1,0:T(8,128)(2,1)S(1)}, bf16[128,2048]{1,0:T(8,128)(2,1)S(1)}, u32[]{:S(2)}, u32[]{:S(2)}) collective-permute-start(bf16[128,2048]{1,0:T(8,128)(2,1)S(1)} %get-tuple-element.174), channel_id=1, source_target_pairs={{2,0},{4,2},{6,4},{7,6},{5,7},{3,5},{1,3},{0,1},{10,8},{12,10},{14... | collective-permute-start | bytes 1572872 | tf_op jit(solution)/shard_map/ppermute | solution.py:50
  245.5 31.1 %collective-permute-start.34 = (bf16[64,2048]{1,0:T(8,128)(2,1)S(1)}, bf16[64,2048]{1,0:T(8,128)(2,1)S(1)}, u32[]{:S(2)}, u32[]{:S(2)}) collective-permute-start(bf16[64,2048]{1,0:T(8,128)(2,1)S(1)} %slice_add_fusion.17), channel_id=1, source_target_pairs={{0,2},{2,4},{4,6},{6,7},{7,5},{5,3},{3,1},{1,0},{8,10},{10,12},{12... | collective-permute-start | bytes 786440 | tf_op jit(solution)/shard_map/ppermute | solution.py:50
  318.9 43.0 %collective-permute-start.35 = (bf16[1024,3072]{1,0:T(8,128)(2,1)S(1)}, bf16[1024,3072]{1,0:T(8,128)(2,1)S(1)}, u32[]{:S(2)}, u32[]{:S(2)}) collective-permute-start(bf16[1024,3072]{1,0:T(8,128)(2,1)S(1)} %pad_maximum_fusion), channel_id=1, source_target_pairs={{0,8},{8,0},{16,24},{24,16},{1,9},{9,1},{17,25},{25,17},{2,10},{10... | collective-permute-start | bytes 18874376 | tf_op jit(solution)/shard_map/ppermute | solution.py:119
  319.0 39.0 %collective-permute-start.37 = (bf16[1024,2048]{1,0:T(8,128)(2,1)}, bf16[1024,2048]{1,0:T(8,128)(2,1)S(1)}, u32[]{:S(2)}, u32[]{:S(2)}) collective-permute-start(bf16[1024,2048]{1,0:T(8,128)(2,1)} %slice_dynamic-update-slice_fusion.y_ref), channel_id=1, source_target_pairs={{0,8},{8,0},{16,24},{24,16},{1,9},{9,1},{17,25},{25,17},{2,10},{10... | collective-permute-start | bytes 12582920 | tf_op jit(solution)/shard_map/ppermute | solution.py:119
  319.9 38.1 %collective-permute-start.36 = (bf16[1024,2048]{1,0:T(8,128)(2,1)S(1)}, bf16[1024,2048]{1,0:T(8,128)(2,1)S(1)}, u32[]{:S(2)}, u32[]{:S(2)}) collective-permute-start(bf16[1024,2048]{1,0:T(8,128)(2,1)S(1)} %constant_dynamic-update-slice_fusion.19.x_ref), channel_id=1, source_target_pairs={{0,8},{8,0},{16,24},{24,16},{1,9},{9,1},{17,25},{25,17},{2,10},{10... | collective-permute-start | bytes 12582920 | tf_op jit(solution)/shard_map/ppermute | solution.py:119
  355.7 33.9 %collective-permute-start.45 = (bf16[128,2048]{1,0:T(8,128)(2,1)S(1)}, bf16[128,2048]{1,0:T(8,128)(2,1)S(1)}, u32[]{:S(2)}, u32[]{:S(2)}) collective-permute-start(bf16[128,2048]{1,0:T(8,128)(2,1)S(1)} %get-tuple-element.158), channel_id=1, source_target_pairs={{2,0},{4,2},{6,4},{7,6},{5,7},{3,5},{1,3},{0,1},{10,8},{12,10},{14... | collective-permute-start | bytes 1572872 | tf_op jit(solution)/shard_map/ppermute | solution.py:50
  357.3 30.7 %collective-permute-start.42 = (bf16[128,2048]{1,0:T(8,128)(2,1)S(1)}, bf16[128,2048]{1,0:T(8,128)(2,1)S(1)}, u32[]{:S(2)}, u32[]{:S(2)}) collective-permute-start(bf16[128,2048]{1,0:T(8,128)(2,1)S(1)} %get-tuple-element.157), channel_id=1, source_target_pairs={{0,2},{2,4},{4,6},{6,7},{7,5},{5,3},{3,1},{1,0},{8,10},{10,12},{12... | collective-permute-start | bytes 1572872 | tf_op jit(solution)/shard_map/ppermute | solution.py:50
  402.8 176.2 %collective-permute-start.72 = (bf16[1536,2048]{1,0:T(8,128)(2,1)}, bf16[1536,2048]{1,0:T(8,128)(2,1)}, u32[]{:S(2)}, u32[]{:S(2)}) collective-permute-start(bf16[1536,2048]{1,0:T(8,128)(2,1)} %shard_map.260), channel_id=1, source_target_pairs={{0,16},{8,24},{16,0},{24,8},{1,17},{9,25},{17,1},{25,9},{2,18},{10... | collective-permute-start | bytes 18874376 | tf_op jit(solution)/shard_map/ppermute | solution.py:129
  437.2 29.2 %collective-permute-start.48 = (bf16[64,2048]{1,0:T(8,128)(2,1)S(1)}, bf16[64,2048]{1,0:T(8,128)(2,1)S(1)}, u32[]{:S(2)}, u32[]{:S(2)}) collective-permute-start(bf16[64,2048]{1,0:T(8,128)(2,1)S(1)} %get-tuple-element.169), channel_id=1, source_target_pairs={{0,2},{2,4},{4,6},{6,7},{7,5},{5,3},{3,1},{1,0},{8,10},{10,12},{12... | collective-permute-start | bytes 786440 | tf_op jit(solution)/shard_map/ppermute | solution.py:50
  438.9 27.6 %collective-permute-start.52 = (bf16[64,2048]{1,0:T(8,128)(2,1)S(1)}, bf16[64,2048]{1,0:T(8,128)(2,1)S(1)}, u32[]{:S(2)}, u32[]{:S(2)}) collective-permute-start(bf16[64,2048]{1,0:T(8,128)(2,1)S(1)} %get-tuple-element.170), channel_id=1, source_target_pairs={{2,0},{4,2},{6,4},{7,6},{5,7},{3,5},{1,3},{0,1},{10,8},{12,10},{14... | collective-permute-start | bytes 786440 | tf_op jit(solution)/shard_map/ppermute | solution.py:50
  440.2 28.6 %collective-permute-start.58 = (bf16[128,2048]{1,0:T(8,128)(2,1)S(1)}, bf16[128,2048]{1,0:T(8,128)(2,1)S(1)}, u32[]{:S(2)}, u32[]{:S(2)}) collective-permute-start(bf16[128,2048]{1,0:T(8,128)(2,1)S(1)} %get-tuple-element.167), channel_id=1, source_target_pairs={{2,0},{4,2},{6,4},{7,6},{5,7},{3,5},{1,3},{0,1},{10,8},{12,10},{14... | collective-permute-start | bytes 1572872 | tf_op jit(solution)/shard_map/ppermute | solution.py:50
  442.9 27.8 %collective-permute-start.59 = (bf16[128,2048]{1,0:T(8,128)(2,1)S(1)}, bf16[128,2048]{1,0:T(8,128)(2,1)S(1)}, u32[]{:S(2)}, u32[]{:S(2)}) collective-permute-start(bf16[128,2048]{1,0:T(8,128)(2,1)S(1)} %get-tuple-element.165), channel_id=1, source_target_pairs={{0,2},{2,4},{4,6},{6,7},{7,5},{5,3},{3,1},{1,0},{8,10},{10,12},{12... | collective-permute-start | bytes 1572872 | tf_op jit(solution)/shard_map/ppermute | solution.py:50
  468.4 36.8 %collective-permute-start.53 = (bf16[128,2048]{1,0:T(8,128)(2,1)S(1)}, bf16[128,2048]{1,0:T(8,128)(2,1)S(1)}, u32[]{:S(2)}, u32[]{:S(2)}) collective-permute-start(bf16[128,2048]{1,0:T(8,128)(2,1)S(1)} %pad_maximum_fusion.13), channel_id=1, source_target_pairs={{2,0},{4,2},{6,4},{7,6},{5,7},{3,5},{1,3},{0,1},{10,8},{12,10},{14... | collective-permute-start | bytes 1572872 | tf_op jit(solution)/shard_map/ppermute | solution.py:50
  553.8 40.1 %collective-permute-start.63 = (f32[17,2048]{1,0:T(8,128)S(1)}, f32[17,2048]{1,0:T(8,128)S(1)}, u32[]{:S(2)}, u32[]{:S(2)}) collective-permute-start(f32[17,2048]{1,0:T(8,128)S(1)} %fusion.81), channel_id=1, source_target_pairs={{0,16},{8,24},{16,0},{24,8},{1,17},{9,25},{17,1},{25,9},{2,18},{10... | collective-permute-start | bytes 417800 | tf_op jit(solution)/shard_map/ppermute | solution.py:418
  564.5 27.4 %collective-permute-start.75 = (bf16[128,2048]{1,0:T(8,128)(2,1)}, bf16[128,2048]{1,0:T(8,128)(2,1)S(1)}, u32[]{:S(2)}, u32[]{:S(2)}) collective-permute-start(bf16[128,2048]{1,0:T(8,128)(2,1)} %pad_maximum_fusion.15), channel_id=1, source_target_pairs={{0,2},{2,4},{4,6},{6,7},{7,5},{5,3},{3,1},{1,0},{8,10},{10,12},{12... | collective-permute-start | bytes 1572872 | tf_op jit(solution)/shard_map/ppermute | solution.py:50
  572.0 45.6 %collective-permute-start.78 = (bf16[128,2048]{1,0:T(8,128)(2,1)S(1)}, bf16[128,2048]{1,0:T(8,128)(2,1)}, u32[]{:S(2)}, u32[]{:S(2)}) collective-permute-start(bf16[128,2048]{1,0:T(8,128)(2,1)S(1)} %pad_maximum_fusion.14.refs_1_), channel_id=1, source_target_pairs={{2,0},{4,2},{6,4},{7,6},{5,7},{3,5},{1,3},{0,1},{10,8},{12,10},{14... | collective-permute-start | bytes 1572872 | tf_op jit(solution)/shard_map/ppermute | solution.py:50
  (138 other events, 1830.0 us)
Sparse Core Ops, SparseCore 0:
  9.7 47.3 all-gather.4
  58.6 21.6 all-gather.6
  82.4 99.1 all-gather.8
  547.3 44.5 reduce-scatter.1
